TPU v7x, 32 devices: a whole 2x2x4 slice. The times are simulated.
32 devices in a mesh: seq: 16 (over z, y, x), ch: 2 (over core).
Axes of the slice: x: 2, y: 2, z: 4, core: 2. Of those that a mesh axis runs over, the one named last changes fastest.
Arguments:
- signal: bfloat16 [256, 8192], P('ch', 'seq'), may hold values from -6 to 6
- in_gate: bfloat16 [256, 8192], P('ch', 'seq'), may hold values from -6 to 6
- out_gate: bfloat16 [256, 8192], P('ch', 'seq'), may hold values from -6 to 6
- short_taps: float32 [256, 128], P('ch'), may hold values from -0.5 to 0.5
- skip_gain: float32 [256], P('ch'), may hold values from 0.5 to 1.5
- decay_rate: float32 [256], P('ch'), may hold values from 0.00037475585 to 0.0018737793
- embed_weight: float32 [33, 64], replicated, may hold values from -1 to 1
- embed_bias: float32 [64], replicated, may hold values from -3.140625 to 3.140625
- sine_freq: float32 [64], replicated, may hold values from 1 to 10
- mid_weight: float32 [64, 64], replicated, may hold values from -0.75 to 0.75
- mid_bias: float32 [64], replicated, may hold values from -3.140625 to 3.140625
- out_weight: float32 [64, 256], P(None, 'ch'), may hold values from -0.75 to 0.75
Outputs:
- mixed: bfloat16 [256, 8192], P('ch', 'seq')
All inputs are finite; a program needn't handle non-finite values.
Results may differ from a plain program's by a relative error of at most 0.001.
Values may be sent and summed in bfloat16 or wider, within the bound.
No kernel may reach another device: no remote copies, remote signals or barrier semaphores. Data moves between devices by JAX's collectives and lax.ppermute only.
A program may use at most 128 MiB of HBM per device.

v0:
```python
import math

import jax
import jax.numpy as jnp
from jax import lax
from jax.sharding import PartitionSpec as P

BANDS = 16


def from_behind(shard, axis, by):
    count = lax.axis_size(axis)
    pairs = [(i, i + by) for i in range(count) if 0 <= i + by < count]
    return lax.ppermute(shard, axis, pairs)


def embed_rows(positions, full_len):
    phase = positions % full_len
    columns = [positions.astype(jnp.float32) / full_len]
    for band in range(BANDS):
        angle = phase.astype(jnp.float32) * (2.0 * math.pi / full_len)
        columns.append(jnp.cos(angle))
        columns.append(jnp.sin(angle))
        phase = 2 * phase % full_len
    return jnp.stack(columns, axis=1)


def filter_hidden(positions, full_len, embed_weight, embed_bias, sine_freq, mid_weight, mid_bias):
    embedding = embed_rows(positions, full_len)
    first = jnp.sin(
        sine_freq
        * (
            jnp.dot(
                embedding,
                embed_weight,
                precision=lax.Precision.HIGHEST,
                preferred_element_type=jnp.float32,
            )
            + embed_bias
        )
    )
    return jnp.sin(
        sine_freq
        * (
            jnp.dot(
                first,
                mid_weight,
                precision=lax.Precision.HIGHEST,
                preferred_element_type=jnp.float32,
            )
            + mid_bias
        )
    )


def shape_filter(second, positions, out_weight, decay_rate):
    raw_vals = jnp.einsum("nf,fc->cn", second, out_weight, precision=lax.Precision.HIGHEST)
    return raw_vals * (
        jnp.sqrt(2.0 * decay_rate)[:, None]
        * jnp.exp(-decay_rate[:, None] * positions.astype(jnp.float32)[None, :])
    )


def angle_table(rows, cols, period):
    product = (
        lax.broadcasted_iota(jnp.int32, (rows, cols), 0)
        * lax.broadcasted_iota(jnp.int32, (rows, cols), 1)
        % period
    )
    angle = product.astype(jnp.float32) * (2.0 * math.pi / period)
    return (jnp.cos(angle), jnp.sin(angle))


def rotate(real_part, imag_part, cos_vals, sin_vals):
    return (
        real_part * cos_vals - imag_part * sin_vals,
        imag_part * cos_vals + real_part * sin_vals,
    )


def twiddle_angle(freq_ids, offsets, fft_len):
    return (freq_ids[:, None] * offsets[None, :]).astype(jnp.float32) * (2.0 * math.pi / fft_len)


def across_blocks(columns, block_cos, block_sin, seq_index, slice_len, fft_len):
    real_part = jnp.einsum("ca,kab->kcb", block_cos, columns, precision=lax.Precision.HIGHEST)
    imag_part = -jnp.einsum("ca,kab->kcb", block_sin, columns, precision=lax.Precision.HIGHEST)
    freq_ids = jnp.arange(block_cos.shape[0], dtype=jnp.int32)
    offsets = seq_index * slice_len + jnp.arange(slice_len, dtype=jnp.int32)
    angle = twiddle_angle(freq_ids, offsets, fft_len)
    return rotate(real_part, imag_part, jnp.cos(angle)[None], -jnp.sin(angle)[None])


def transform_rows(real_part, imag_part, offset_cos, offset_sin, sign):
    shape = real_part.shape
    flat_real = real_part.reshape(-1, shape[-1])
    flat_imag = imag_part.reshape(-1, shape[-1])
    cos_real = jnp.dot(
        flat_real, offset_cos, precision=lax.Precision.HIGHEST, preferred_element_type=jnp.float32
    )
    cos_imag = jnp.dot(
        flat_imag, offset_cos, precision=lax.Precision.HIGHEST, preferred_element_type=jnp.float32
    )
    sin_real = jnp.dot(
        flat_real, offset_sin, precision=lax.Precision.HIGHEST, preferred_element_type=jnp.float32
    )
    sin_imag = jnp.dot(
        flat_imag, offset_sin, precision=lax.Precision.HIGHEST, preferred_element_type=jnp.float32
    )
    return (
        (cos_real - sign * sin_imag).reshape(shape),
        (cos_imag + sign * sin_real).reshape(shape),
    )


def causal_matrix(short_taps):
    channels, tap_count = short_taps.shape
    period = 3 * tap_count
    padding = jnp.zeros((channels, 2 * tap_count - 1), jnp.float32)
    pattern = jnp.concatenate(
        [jnp.zeros((channels, 1), jnp.float32), short_taps[:, ::-1], padding], axis=1
    )
    tiled = jnp.tile(pattern, (1, tap_count))[:, : tap_count * (period - 1)]
    return tiled.reshape(channels, tap_count, period - 1)[:, :, : 2 * tap_count]


def on_device(
    signal,
    in_gate,
    out_gate,
    short_taps,
    skip_gain,
    decay_rate,
    embed_weight,
    embed_bias,
    sine_freq,
    mid_weight,
    mid_bias,
    out_weight,
):
    channels, local_len = signal.shape
    tap_count = short_taps.shape[1]
    seq_devs = lax.axis_size("seq")
    seq_index = lax.axis_index("seq")
    full_len = seq_devs * local_len
    fft_len = 2 * full_len
    slice_len = local_len // seq_devs
    prior_rim = from_behind(signal[:, local_len - tap_count :], "seq", 1)
    blocks = local_len // tap_count
    current = signal.reshape(channels, blocks, tap_count)
    earlier = jnp.concatenate([prior_rim[:, None, :], current[:, :-1, :]], axis=1)
    window = jnp.concatenate([earlier, current], axis=2).astype(jnp.float32)
    toeplitz = causal_matrix(short_taps)
    short_out = jnp.einsum(
        "cij,cbj->cbi", toeplitz, window, precision=lax.Precision.HIGHEST
    ).reshape(channels, local_len)
    gated_in = in_gate.astype(jnp.float32) * short_out
    block_cos, block_sin = angle_table(2 * seq_devs, seq_devs, 2 * seq_devs)
    offset_cos, offset_sin = angle_table(local_len, local_len, local_len)
    own_positions = seq_index * local_len + jnp.arange(local_len, dtype=jnp.int32)
    feat_rows = local_len // lax.axis_size("ch")
    start = seq_index * local_len + lax.axis_index("ch") * feat_rows
    part_rows = filter_hidden(
        start + jnp.arange(feat_rows, dtype=jnp.int32),
        full_len,
        embed_weight,
        embed_bias,
        sine_freq,
        mid_weight,
        mid_bias,
    )
    second = lax.all_gather(part_rows, "ch", axis=0, tiled=True)
    filter_vals = shape_filter(second, own_positions, out_weight, decay_rate)
    signal_cols, filter_cols = (
        lax.all_to_all(
            gated_in.reshape(channels, 1, local_len), "seq", split_axis=2, concat_axis=1, tiled=True
        ),
        lax.all_to_all(
            filter_vals.reshape(channels, 1, local_len),
            "seq",
            split_axis=2,
            concat_axis=1,
            tiled=True,
        ),
    )
    signal_real, signal_imag = across_blocks(
        signal_cols, block_cos, block_sin, seq_index, slice_len, fft_len
    )
    filt_real, filt_imag = across_blocks(
        filter_cols, block_cos, block_sin, seq_index, slice_len, fft_len
    )
    signal_real, signal_imag, filt_real, filt_imag = (
        lax.all_to_all(signal_real, "seq", split_axis=1, concat_axis=2, tiled=True),
        lax.all_to_all(signal_imag, "seq", split_axis=1, concat_axis=2, tiled=True),
        lax.all_to_all(filt_real, "seq", split_axis=1, concat_axis=2, tiled=True),
        lax.all_to_all(filt_imag, "seq", split_axis=1, concat_axis=2, tiled=True),
    )
    signal_real, signal_imag = transform_rows(
        signal_real, signal_imag, offset_cos, offset_sin, -1.0
    )
    filt_real, filt_imag = transform_rows(filt_real, filt_imag, offset_cos, offset_sin, -1.0)
    prod_real = signal_real * filt_real - signal_imag * filt_imag
    prod_imag = signal_real * filt_imag + signal_imag * filt_real
    back_real, back_imag = transform_rows(prod_real, prod_imag, offset_cos, offset_sin, 1.0)
    own_freqs = 2 * seq_index + jnp.arange(2, dtype=jnp.int32)
    angle = twiddle_angle(own_freqs, jnp.arange(local_len, dtype=jnp.int32), fft_len)
    back_real, back_imag = rotate(back_real, back_imag, jnp.cos(angle)[None], jnp.sin(angle)[None])
    back_real, back_imag = (
        lax.all_to_all(back_real, "seq", split_axis=2, concat_axis=1, tiled=True),
        lax.all_to_all(back_imag, "seq", split_axis=2, concat_axis=1, tiled=True),
    )
    result = (
        jnp.einsum("ca,kcb->kab", block_cos, back_real, precision=lax.Precision.HIGHEST)
        - jnp.einsum("ca,kcb->kab", block_sin, back_imag, precision=lax.Precision.HIGHEST)
    ) * (1.0 / fft_len)
    conv = lax.all_to_all(result, "seq", split_axis=1, concat_axis=2, tiled=True).reshape(
        channels, local_len
    )
    return (out_gate.astype(jnp.float32) * (conv + skip_gain[:, None] * gated_in)).astype(
        jnp.bfloat16
    )


def solution(mesh):
    in_specs = (
        P("ch", "seq"),
        P("ch", "seq"),
        P("ch", "seq"),
        P("ch", None),
        P("ch"),
        P("ch"),
        P(),
        P(),
        P(),
        P(),
        P(),
        P(None, "ch"),
    )
    out_specs = P("ch", "seq")
    return jax.shard_map(
        on_device, mesh=mesh, in_specs=in_specs, out_specs=out_specs, check_vma=False
    )
```

profile of v0, /device:TPU:0, one launch (start us, length us, event | category | flops | bytes accessed | tf_op | source)
XLA Modules:
  0.0 323.2 jit_solution(2174920377164158145)
XLA Ops:
  2.6 1.2 fusion.10
  3.8 1.2 fusion.8
  5.1 2.0 all_gather.3
  7.7 1.3 fusion.6
  9.0 8.2 %all-to-all-start.3 = ((f32[128,1,512]{0,1,2:T(1,128)}), f32[128,1,512]{0,1,2:T(1,128)S(1)}, u32[]{:S(2)}, u32[]{:S(2)}) async-start(f32[128,1,512]{0,1,2:T(1,128)} %bitcast.15), calls=%async_computation.3 | async-start | bytes 524288 | tf_op jit(solution)/shard_map/all_to_all | solution.py:178
  18.0 4.0 %collective-permute-start = (bf16[128,128]{1,0:T(8,128)(2,1)S(1)}, bf16[128,128]{1,0:T(8,128)(2,1)S(1)}, u32[]{:S(2)}, u32[]{:S(2)}) collective-permute-start(bf16[128,128]{1,0:T(8,128)(2,1)S(1)} %slice.12), channel_id=1, source_target_pairs={{0,2},{2,4},{4,6},{6,8},{8,10},{10,12},{12,14},{14,16},{16,18},{18... | collective-permute-start | bytes 98312 | tf_op jit(solution)/shard_map/ppermute | solution.py:14
  24.1 9.9 %tile.4 = f32[128,128,384]{2,1,0:T(8,128)} broadcast(f32[128,384]{1,0:T(8,128)S(1)} %maximum_maximum_fusion), dimensions={0,2} | broadcast | bytes 25362432 | tf_op jit(solution)/shard_map/tile | solution.py:123
  34.0 23.4 %copy.148 = f32[16,8,128,384]{3,1,2,0:T(8,128)S(1)} copy(f32[16,8,128,384]{3,2,1,0:T(8,128)} %bitcast.95) | data formatting | bytes 50331648
  57.4 8.6 %slice.17 = f32[128,49024]{1,0:T(8,128)} slice(f32[128,49152]{1,0:T(8,128)S(1)} %bitcast.96), slice={[0:128], [0:49024]} | slice | bytes 50200576 | tf_op jit(solution)/shard_map/slice | solution.py:123
  65.9 32.0 %reshape.975 = f32[128,128,383]{2,1,0:T(8,128)} reshape(f32[128,49024]{1,0:T(8,128)} %slice.17) | data formatting | bytes 50200576 | tf_op jit(solution)/shard_map/reshape | solution.py:124
  98.2 11.2 %fusion = f32[128,4,128]{2,1,0:T(4,128)S(1)} fusion(f32[128,128,383]{2,1,0:T(8,128)} %reshape.975, bf16[128,4,128]{2,1,0:T(4,128)(2,1)S(1)} %reshape.974, bf16[128,3,128]{2,1,0:T(4,128)(2,1)S(1)} %bitcast.113, bf16[128,1,128]{2,1,0:T(2,128)(2,1)S(1)} %copy.119), kind=kOutput, calls=%fused_computation | convolution fusion | flops 202113024 | bytes 17301504 | tf_op jit(solution)/shard_map/cij,cbj->cbi/dot_general | solution.py:154
  110.3 5.8 %all-to-all-start = ((f32[128,1,512]{0,1,2:T(1,128)}), f32[128,1,512]{0,1,2:T(1,128)S(1)}, u32[]{:S(2)}, u32[]{:S(2)}) async-start(f32[128,1,512]{0,1,2:T(1,128)} %bitcast.3), calls=%async_computation | async-start | bytes 524288 | tf_op jit(solution)/shard_map/all_to_all | solution.py:175
  116.9 8.4 %all-to-all-done = f32[128,1,512]{0,1,2:T(1,128)S(1)} async-done(((f32[128,1,512]{0,1,2:T(1,128)}), f32[128,1,512]{0,1,2:T(1,128)S(1)}, u32[]{:S(2)}, u32[]{:S(2)}) %all-to-all-start) | async-done | bytes 262176 | tf_op jit(solution)/shard_map/all_to_all | solution.py:175
  127.8 1.1 copy.131
  128.9 3.6 %all-to-all-start.4 = ((f32[128,32,32]{0,2,1:T(8,128)}), f32[128,32,32]{0,2,1:T(8,128)S(1)}, u32[]{:S(2)}, u32[]{:S(2)}) async-start(f32[128,32,32]{0,2,1:T(8,128)} %copy.131), calls=%async_computation.4 | async-start | bytes 1048576 | tf_op jit(solution)/shard_map/all_to_all | solution.py:195
  133.6 13.3 %all-to-all-done.4 = f32[128,32,32]{0,2,1:T(8,128)S(1)} async-done(((f32[128,32,32]{0,2,1:T(8,128)}), f32[128,32,32]{0,2,1:T(8,128)S(1)}, u32[]{:S(2)}, u32[]{:S(2)}) %all-to-all-start.4) | async-done | bytes 524320 | tf_op jit(solution)/shard_map/all_to_all | solution.py:195
  146.9 3.9 %all-to-all-start.5 = ((f32[128,32,32]{0,2,1:T(8,128)}), f32[128,32,32]{0,2,1:T(8,128)S(1)}, u32[]{:S(2)}, u32[]{:S(2)}) async-start(f32[128,32,32]{0,2,1:T(8,128)} %copy.133), calls=%async_computation.5 | async-start | bytes 1048576 | tf_op jit(solution)/shard_map/all_to_all | solution.py:196
  150.8 1.1 copy.126
  151.9 13.3 %all-to-all-done.5 = f32[128,32,32]{0,2,1:T(8,128)S(1)} async-done(((f32[128,32,32]{0,2,1:T(8,128)}), f32[128,32,32]{0,2,1:T(8,128)S(1)}, u32[]{:S(2)}, u32[]{:S(2)}) %all-to-all-start.5) | async-done | bytes 524320 | tf_op jit(solution)/shard_map/all_to_all | solution.py:196
  165.2 3.8 %all-to-all-start.2 = ((f32[128,32,32]{0,2,1:T(8,128)}), f32[128,32,32]{0,2,1:T(8,128)S(1)}, u32[]{:S(2)}, u32[]{:S(2)}) async-start(f32[128,32,32]{0,2,1:T(8,128)} %copy.126), calls=%async_computation.2 | async-start | bytes 1048576 | tf_op jit(solution)/shard_map/all_to_all | solution.py:194
  169.2 1.1 copy.124
  170.4 1.8 copy.132
  172.2 1.6 reshape.981
  173.8 2.9 copy.134
  176.7 1.6 reshape.982
  178.3 5.1 %all-to-all-done.2 = f32[128,32,32]{0,2,1:T(8,128)S(1)} async-done(((f32[128,32,32]{0,2,1:T(8,128)}), f32[128,32,32]{0,2,1:T(8,128)S(1)}, u32[]{:S(2)}, u32[]{:S(2)}) %all-to-all-start.2) | async-done | bytes 524320 | tf_op jit(solution)/shard_map/all_to_all | solution.py:194
  183.4 4.3 %all-to-all-start.1 = ((f32[128,32,32]{0,2,1:T(8,128)}), f32[128,32,32]{0,2,1:T(8,128)S(1)}, u32[]{:S(2)}, u32[]{:S(2)}) async-start(f32[128,32,32]{0,2,1:T(8,128)} %copy.124), calls=%async_computation.1 | async-start | bytes 1048576 | tf_op jit(solution)/shard_map/all_to_all | solution.py:193
  187.6 1.8 copy.127
  189.5 1.6 reshape.979
  191.1 6.3 %convolution_multiply_fusion = f32[256,512]{1,0:T(8,128)S(1)} fusion(f32[256,512]{1,0:T(8,128)} %reshape.981), kind=kOutput, calls=%fused_computation.7 | convolution fusion | flops 809107456 | bytes 1048576 | tf_op jit(solution)/shard_map/dot_general | solution.py:104
  197.4 6.9 %convolution_multiply_fusion.3 = f32[256,512]{1,0:T(8,128)} fusion(f32[256,512]{1,0:T(8,128)} %reshape.979), kind=kOutput, calls=%fused_computation.13 | convolution fusion | flops 809107456 | bytes 1048576 | tf_op jit(solution)/shard_map/dot_general | solution.py:107
  204.3 6.8 %convolution_multiply_fusion.2 = f32[256,512]{1,0:T(8,128)} fusion(f32[256,512]{1,0:T(8,128)} %reshape.982), kind=kOutput, calls=%fused_computation.11 | convolution fusion | flops 809107456 | bytes 1048576 | tf_op jit(solution)/shard_map/dot_general | solution.py:107
  211.1 7.0 %convolution_add_fusion.1 = f32[256,512]{1,0:T(8,128)} fusion(f32[256,512]{1,0:T(8,128)S(1)} %convolution_multiply_fusion, f32[256,512]{1,0:T(8,128)} %reshape.982), kind=kOutput, calls=%fused_computation.8 | convolution fusion | flops 809107456 | bytes 1572864 | tf_op jit(solution)/shard_map/dot_general | solution.py:101
  218.1 1.8 copy.125
  220.8 5.3 %convolution_multiply_fusion.1 = f32[256,512]{1,0:T(8,128)S(1)} fusion(f32[256,512]{1,0:T(8,128)S(1)} %reshape.978), kind=kOutput, calls=%fused_computation.9 | convolution fusion | flops 809107456 | bytes 1048576 | tf_op jit(solution)/shard_map/dot_general | solution.py:104
  226.1 6.3 %convolution_subtract_fusion.2 = f32[256,512]{1,0:T(8,128)S(1)} fusion(f32[256,512]{1,0:T(8,128)} %convolution_multiply_fusion.3, f32[256,512]{1,0:T(8,128)S(1)} %reshape.978), kind=kOutput, calls=%fused_computation.14 | convolution fusion | flops 809107456 | bytes 1572864 | tf_op jit(solution)/shard_map/dot_general | solution.py:98
  232.4 6.4 %convolution_subtract_fusion.1 = f32[256,512]{1,0:T(8,128)S(1)} fusion(f32[256,512]{1,0:T(8,128)} %convolution_multiply_fusion.2, f32[256,512]{1,0:T(8,128)S(1)} %copy-done.3), kind=kOutput, calls=%fused_computation.12 | convolution fusion | flops 809107456 | bytes 1572864 | tf_op jit(solution)/shard_map/dot_general | solution.py:98
  238.9 6.6 %multiply_subtract_fusion.1 = (f32[256,512]{1,0:T(8,128)S(1)}, f32[256,512]{1,0:T(8,128)S(1)}) fusion(f32[256,512]{1,0:T(8,128)} %convolution_add_fusion.1, f32[256,512]{1,0:T(8,128)S(1)} %convolution_subtract_fusion.2, f32[256,512]{1,0:T(8,128)S(1)} %convolution_subtract_fusion.1, f32[256,512]{1,0:T(8,128)S(1)} %convolution_multiply_fusion.1, ...), kind=kOutput, calls=%fused_computation.41 | convolution fusion | flops 809893888 | bytes 3670016 | tf_op jit(solution)/shard_map/dot_general | solution.py:101
  245.4 5.3 %fusion.19 = f32[256,512]{1,0:T(8,128)S(1)} fusion(f32[256,512]{1,0:T(8,128)S(1)} %get-tuple-element.6), kind=kOutput, calls=%fused_computation.47 | convolution fusion | flops 808976384 | bytes 1048576 | tf_op jit(solution)/shard_map/dot_general | solution.py:101
  250.7 5.3 %fusion.21 = f32[256,512]{1,0:T(8,128)S(1)} fusion(f32[256,512]{1,0:T(8,128)S(1)} %get-tuple-element.5), kind=kOutput, calls=%fused_computation.48 | convolution fusion | flops 808976384 | bytes 1048576 | tf_op jit(solution)/shard_map/dot_general | solution.py:98
  256.1 5.6 %convolution_add_fusion = f32[256,512]{1,0:T(8,128)S(1)} fusion(f32[256,512]{1,0:T(8,128)S(1)} %fusion.19, f32[256,512]{1,0:T(8,128)S(1)} %get-tuple-element.5), kind=kOutput, calls=%fused_computation.5 | convolution fusion | flops 809107456 | bytes 1572864 | tf_op jit(solution)/shard_map/dot_general | solution.py:104
  262.0 5.3 %convolution_subtract_fusion = f32[256,512]{1,0:T(8,128)S(1)} fusion(f32[256,512]{1,0:T(8,128)S(1)} %fusion.21, f32[256,512]{1,0:T(8,128)S(1)} %get-tuple-element.6), kind=kOutput, calls=%fused_computation.6 | convolution fusion | flops 809107456 | bytes 1572864 | tf_op jit(solution)/shard_map/dot_general | solution.py:107
  268.8 7.0 %all-to-all-start.6 = ((f32[128,2,512]{0,1,2:T(2,128)}), f32[128,2,512]{0,1,2:T(2,128)S(1)}, u32[]{:S(2)}, u32[]{:S(2)}) async-start(f32[128,2,512]{0,1,2:T(2,128)} %copy.137), calls=%async_computation.6 | async-start | bytes 1048576 | tf_op jit(solution)/shard_map/all_to_all | solution.py:209
  276.9 12.6 %all-to-all-done.6 = f32[128,2,512]{0,1,2:T(2,128)S(1)} async-done(((f32[128,2,512]{0,1,2:T(2,128)}), f32[128,2,512]{0,1,2:T(2,128)S(1)}, u32[]{:S(2)}, u32[]{:S(2)}) %all-to-all-start.6) | async-done | bytes 524320 | tf_op jit(solution)/shard_map/all_to_all | solution.py:209
  289.5 3.8 %all-to-all-start.7 = ((f32[128,2,512]{0,1,2:T(2,128)}), f32[128,2,512]{0,1,2:T(2,128)S(1)}, u32[]{:S(2)}, u32[]{:S(2)}) async-start(f32[128,2,512]{0,1,2:T(2,128)} %copy.142), calls=%async_computation.7 | async-start | bytes 1048576 | tf_op jit(solution)/shard_map/all_to_all | solution.py:210
  294.3 12.8 %all-to-all-done.7 = f32[128,2,512]{0,1,2:T(2,128)S(1)} async-done(((f32[128,2,512]{0,1,2:T(2,128)}), f32[128,2,512]{0,1,2:T(2,128)S(1)}, u32[]{:S(2)}, u32[]{:S(2)}) %all-to-all-start.7) | async-done | bytes 524320 | tf_op jit(solution)/shard_map/all_to_all | solution.py:210
  308.8 3.8 %all-to-all-start.8 = ((f32[128,16,32]{0,2,1:T(8,128)}), f32[128,16,32]{0,2,1:T(8,128)S(1)}, u32[]{:S(2)}, u32[]{:S(2)}) async-start(f32[128,16,32]{0,2,1:T(8,128)} %copy.145), calls=%async_computation.8 | async-start | bytes 524288 | tf_op jit(solution)/shard_map/all_to_all | solution.py:216
  312.8 8.4 %all-to-all-done.8 = f32[128,16,32]{0,2,1:T(8,128)S(1)} async-done(((f32[128,16,32]{0,2,1:T(8,128)}), f32[128,16,32]{0,2,1:T(8,128)S(1)}, u32[]{:S(2)}, u32[]{:S(2)}) %all-to-all-start.8) | async-done | bytes 262176 | tf_op jit(solution)/shard_map/all_to_all | solution.py:216
  (73 shorter events, 19.6 us)
Async XLA Ops:
  0.0 7.7 %copy-start = (f32[64,128]{1,0:T(8,128)S(1)}, f32[64,128]{1,0:T(8,128)}, u32[]{:S(2)}) copy-start(f32[64,128]{1,0:T(8,128)} %param.23) | copy-start | bytes 98308
  9.0 101.2 %all-to-all-start.3 = ((f32[128,1,512]{0,1,2:T(1,128)}), f32[128,1,512]{0,1,2:T(1,128)S(1)}, u32[]{:S(2)}, u32[]{:S(2)}) async-start(f32[128,1,512]{0,1,2:T(1,128)} %bitcast.15), calls=%async_computation.3 | async-start | bytes 524288 | tf_op jit(solution)/shard_map/all_to_all | solution.py:178
  18.0 80.1 %collective-permute-start = (bf16[128,128]{1,0:T(8,128)(2,1)S(1)}, bf16[128,128]{1,0:T(8,128)(2,1)S(1)}, u32[]{:S(2)}, u32[]{:S(2)}) collective-permute-start(bf16[128,128]{1,0:T(8,128)(2,1)S(1)} %slice.12), channel_id=1, source_target_pairs={{0,2},{2,4},{4,6},{6,8},{8,10},{10,12},{12,14},{14,16},{16,18},{18... | collective-permute-start | bytes 98312 | tf_op jit(solution)/shard_map/ppermute | solution.py:14
  65.9 32.0 %copy-start.4 = (bf16[128,512]{1,0:T(8,128)(2,1)S(1)}, bf16[128,512]{1,0:T(8,128)(2,1)}, u32[]{:S(2)}) copy-start(bf16[128,512]{1,0:T(8,128)(2,1)} %param.13) | copy-start | bytes 393220
  110.3 15.1 %all-to-all-start = ((f32[128,1,512]{0,1,2:T(1,128)}), f32[128,1,512]{0,1,2:T(1,128)S(1)}, u32[]{:S(2)}, u32[]{:S(2)}) async-start(f32[128,1,512]{0,1,2:T(1,128)} %bitcast.3), calls=%async_computation | async-start | bytes 524288 | tf_op jit(solution)/shard_map/all_to_all | solution.py:175
  128.9 18.0 %all-to-all-start.4 = ((f32[128,32,32]{0,2,1:T(8,128)}), f32[128,32,32]{0,2,1:T(8,128)S(1)}, u32[]{:S(2)}, u32[]{:S(2)}) async-start(f32[128,32,32]{0,2,1:T(8,128)} %copy.131), calls=%async_computation.4 | async-start | bytes 1048576 | tf_op jit(solution)/shard_map/all_to_all | solution.py:195
  146.9 18.3 %all-to-all-start.5 = ((f32[128,32,32]{0,2,1:T(8,128)}), f32[128,32,32]{0,2,1:T(8,128)S(1)}, u32[]{:S(2)}, u32[]{:S(2)}) async-start(f32[128,32,32]{0,2,1:T(8,128)} %copy.133), calls=%async_computation.5 | async-start | bytes 1048576 | tf_op jit(solution)/shard_map/all_to_all | solution.py:196
  165.2 5.2 %copy-start.2 = (f32[128,32,32]{0,2,1:T(8,128)}, f32[128,32,32]{0,2,1:T(8,128)S(1)}, u32[]{:S(2)}) copy-start(f32[128,32,32]{0,2,1:T(8,128)S(1)} %all-to-all-done.5) | copy-start | bytes 1572868
  165.2 18.2 %all-to-all-start.2 = ((f32[128,32,32]{0,2,1:T(8,128)}), f32[128,32,32]{0,2,1:T(8,128)S(1)}, u32[]{:S(2)}, u32[]{:S(2)}) async-start(f32[128,32,32]{0,2,1:T(8,128)} %copy.126), calls=%async_computation.2 | async-start | bytes 1048576 | tf_op jit(solution)/shard_map/all_to_all | solution.py:194
  183.4 34.7 %all-to-all-start.1 = ((f32[128,32,32]{0,2,1:T(8,128)}), f32[128,32,32]{0,2,1:T(8,128)S(1)}, u32[]{:S(2)}, u32[]{:S(2)}) async-start(f32[128,32,32]{0,2,1:T(8,128)} %copy.124), calls=%async_computation.1 | async-start | bytes 1048576 | tf_op jit(solution)/shard_map/all_to_all | solution.py:193
  189.5 42.9 %copy-start.3 = (f32[256,512]{1,0:T(8,128)S(1)}, f32[256,512]{1,0:T(8,128)}, u32[]{:S(2)}) copy-start(f32[256,512]{1,0:T(8,128)} %reshape.981) | copy-start | bytes 1572868
  220.8 102.2 %copy-start.1 = (f32[64,128]{1,0:T(8,128)S(1)}, f32[64,128]{1,0:T(8,128)}, u32[]{:S(2)}) copy-start(f32[64,128]{1,0:T(8,128)} %param.23) | copy-start | bytes 98308
  226.1 86.6 %copy-start.5 = (bf16[128,512]{1,0:T(8,128)(2,1)S(1)}, bf16[128,512]{1,0:T(8,128)(2,1)}, u32[]{:S(2)}) copy-start(bf16[128,512]{1,0:T(8,128)(2,1)} %param.14) | copy-start | bytes 393220
  226.1 95.1 %copy-start.6 = (f32[128]{0:T(128)S(1)}, f32[128]{0:T(128)}, u32[]{:S(2)}) copy-start(f32[128]{0:T(128)} %param.16) | copy-start | bytes 1540
  268.8 20.7 %all-to-all-start.6 = ((f32[128,2,512]{0,1,2:T(2,128)}), f32[128,2,512]{0,1,2:T(2,128)S(1)}, u32[]{:S(2)}, u32[]{:S(2)}) async-start(f32[128,2,512]{0,1,2:T(2,128)} %copy.137), calls=%async_computation.6 | async-start | bytes 1048576 | tf_op jit(solution)/shard_map/all_to_all | solution.py:209
  289.5 17.6 %all-to-all-start.7 = ((f32[128,2,512]{0,1,2:T(2,128)}), f32[128,2,512]{0,1,2:T(2,128)S(1)}, u32[]{:S(2)}, u32[]{:S(2)}) async-start(f32[128,2,512]{0,1,2:T(2,128)} %copy.142), calls=%async_computation.7 | async-start | bytes 1048576 | tf_op jit(solution)/shard_map/all_to_all | solution.py:210
  308.8 12.4 %all-to-all-start.8 = ((f32[128,16,32]{0,2,1:T(8,128)}), f32[128,16,32]{0,2,1:T(8,128)S(1)}, u32[]{:S(2)}, u32[]{:S(2)}) async-start(f32[128,16,32]{0,2,1:T(8,128)} %copy.145), calls=%async_computation.8 | async-start | bytes 524288 | tf_op jit(solution)/shard_map/all_to_all | solution.py:216
where the time goes:
time: 329 us; the launch traced here: 323 us
  local copies, waits for them, and re-layouts  101 us (31%)
  matrix products  92.1 us (28%)
  waiting for transfers between devices  74 us (22%)
  starting transfers between devices  48.2 us (15%)
  other arithmetic  5.37 us (2%)
    reshape x1, local copies, waits for them, and re-layouts, causal_matrix(): return tiled.reshape(channels, tap_count, period - 1)[:, :, :2 * tap_count]  32 us
    unnamed x17, local copies, waits for them, and re-layouts  23.6 us
    dot_general x3, matrix products, transform_rows(): jnp.dot(flat_imag, offset_sin, precision=lax.Precision.HIGHEST, preferred...  19 us
    dot_general x3, matrix products, transform_rows(): jnp.dot(flat_imag, offset_cos, precision=lax.Precision.HIGHEST, preferred...  18.8 us
    dot_general x3, matrix products, transform_rows(): jnp.dot(flat_real, offset_cos, precision=lax.Precision.HIGHEST, preferred...  18.1 us
    dot_general x3, matrix products, transform_rows(): jnp.dot(flat_real, offset_sin, precision=lax.Precision.HIGHEST, preferred...  17.2 us
    all_to_all x1, waiting for transfers between devices, on_device(): lax.all_to_all(filt_real, 'seq', split_axis=1, concat_axis=2, tiled=True)  13.3 us
    all_to_all x1, waiting for transfers between devices, on_device(): lax.all_to_all(filt_imag, 'seq', split_axis=1, concat_axis=2, tiled=True)  13.3 us
  transfers between devices with their start and end apart: 10, of which 7 were waited for; matrix products, arithmetic and copies ran while one was open for 41% of the time, Pallas kernels for 0%

commit v1 on v0

v1 whole, which is shorter than its diff:
```python
import functools
import math

import jax
import jax.numpy as jnp
import numpy as np
from jax import lax
from jax.experimental import pallas as pl
from jax.experimental.pallas import tpu as pltpu
from jax.sharding import PartitionSpec as P

BANDS = 16
LANES = 128
TILE = 1024
F32 = jnp.float32
BF16 = jnp.bfloat16


def round_up(count, step):
    return (count + step - 1) // step * step


def halves(table):
    high = table.astype(BF16)
    low = (table - high.astype(np.float64)).astype(BF16)
    return high, low


@functools.lru_cache(maxsize=None)
def embed_table(full_len):
    positions = np.arange(full_len, dtype=np.int64)
    rows = [positions / full_len]
    phase = positions
    for _ in range(BANDS):
        angle = phase * (2.0 * math.pi / full_len)
        rows += [np.cos(angle), np.sin(angle)]
        phase = 2 * phase % full_len
    table = np.zeros((round_up(len(rows), 8), full_len), np.float32)
    table[: len(rows)] = np.stack(rows)
    return table


@functools.lru_cache(maxsize=None)
def transform_tables(full_len):
    blocks = full_len // LANES
    a = np.arange(blocks)
    k1 = np.arange(blocks)
    b = np.arange(LANES)
    theta = 2.0 * math.pi / blocks * ((4 * k1 + 1)[:, None] * a[None, :] % (4 * blocks)) / 4.0
    phi = 2.0 * math.pi / full_len * ((4 * k1 + 1)[:, None] * b[None, :]) / 4.0
    psi = 2.0 * math.pi / LANES * (b[:, None] * b[None, :] % LANES)
    outer_high, outer_low = halves(np.concatenate([np.cos(theta), -np.sin(theta)], axis=0))
    outer = np.concatenate([outer_high, outer_high, outer_low], axis=1)
    back = np.concatenate([np.cos(theta).T, -np.sin(theta).T], axis=1) / full_len
    back_high, back_low = halves(back)
    outer_back = np.concatenate([back_high, back_high, back_low], axis=1)
    twiddle = np.stack([np.cos(phi), np.sin(phi)]).astype(np.float32)
    cos_in, sin_in = np.cos(psi), np.sin(psi)
    inner = np.stack(halves(np.block([[cos_in, -sin_in], [sin_in, cos_in]])))
    inner_back = np.stack(halves(np.block([[cos_in, sin_in], [-sin_in, cos_in]])))
    return outer, twiddle, inner, inner_back, outer_back


def sine_constants():
    nodes = np.cos((np.arange(400) + 0.5) * math.pi / 400) * (math.pi / 2)
    squares = nodes * nodes
    basis = np.stack([squares**p for p in range(6)], axis=1)
    fit = np.linalg.lstsq(basis, np.sin(nodes) / nodes, rcond=None)[0]
    first = np.floor(math.pi * 2.0**13) / 2.0**13
    second = np.floor((math.pi - first) * 2.0**28) / 2.0**28
    return [float(v) for v in fit], (float(first), float(second), math.pi - first - second)


SINE_FIT, PI_PARTS = sine_constants()


def sine(angle):
    turns = jnp.round(angle * (1.0 / math.pi))
    rest = angle
    for part in PI_PARTS:
        rest = rest - turns * part
    half = turns * 0.5
    odd = half - jnp.floor(half)
    square = rest * rest
    value = SINE_FIT[5]
    for term in SINE_FIT[4::-1]:
        value = value * square + term
    return value * (rest - rest * (4.0 * odd))


def split_two(vals):
    high = vals.astype(BF16)
    return high, (vals - high.astype(F32)).astype(BF16)


def split_three(vals):
    first = vals.astype(BF16).astype(F32)
    rest = vals - first
    second = rest.astype(BF16).astype(F32)
    return first, second, rest - second


def matmul(lhs, rhs):
    return jnp.dot(lhs, rhs, preferred_element_type=F32)


def six_left(vals):
    one, two, three = split_three(vals)
    return jnp.concatenate([one, one, two, one, three, two], axis=0)


def six_right(vals):
    one, two, three = split_three(vals)
    return jnp.concatenate([one, two, one, three, one, two], axis=0).astype(BF16)


def stack_three(vals):
    high, low = split_two(vals)
    return jnp.concatenate([high, low, high], axis=0)


def inner_product(vals, table_ref):
    high, low = split_two(vals)
    return (
        matmul(high, table_ref[0]) + matmul(low, table_ref[0]) + matmul(high, table_ref[1])
    )


def forward(columns, outer_ref, twiddle_ref, inner_ref):
    blocks = columns[0].shape[0]
    mixed = matmul(outer_ref[...], stack_three(jnp.concatenate(columns, axis=1)))
    cos_vals, sin_vals = twiddle_ref[0], twiddle_ref[1]
    rows = []
    for c in range(len(columns)):
        real = mixed[:blocks, c * LANES : (c + 1) * LANES]
        imag = mixed[blocks:, c * LANES : (c + 1) * LANES]
        rows.append(
            jnp.concatenate(
                [real * cos_vals + imag * sin_vals, imag * cos_vals - real * sin_vals], axis=1
            )
        )
    return inner_product(jnp.concatenate(rows, axis=0), inner_ref)


def backward(spectrum, channels, inner_back_ref, twiddle_ref, outer_back_ref):
    vals = inner_product(spectrum, inner_back_ref)
    blocks = vals.shape[0] // channels
    cos_vals, sin_vals = twiddle_ref[0], twiddle_ref[1]
    columns = []
    for c in range(channels):
        real = vals[c * blocks : (c + 1) * blocks, :LANES]
        imag = vals[c * blocks : (c + 1) * blocks, LANES:]
        columns.append(
            jnp.concatenate(
                [real * cos_vals - imag * sin_vals, imag * cos_vals + real * sin_vals], axis=0
            )
        )
    return matmul(outer_back_ref[...], stack_three(jnp.concatenate(columns, axis=1)))


def filter_kernel(
    own,
    embed_ref,
    embed_weight_ref,
    embed_bias_ref,
    sine_freq_ref,
    mid_weight_ref,
    mid_bias_ref,
    out_weight_ref,
    decay_ref,
    taps_ref,
    outer_ref,
    twiddle_ref,
    inner_ref,
    spectrum_ref,
    toeplitz_ref,
    pad_ref,
    vec_ref,
    out_rows_ref,
    filter_ref,
):
    full_len = embed_ref.shape[1]
    tap_count = taps_ref.shape[1]
    first_channel = pl.multiple_of(lax.axis_index("seq") * own, own)
    pad_ref[...] = jnp.zeros_like(pad_ref)
    pad_ref[: embed_weight_ref.shape[0], :] = embed_weight_ref[...]
    weight_one = six_left(pad_ref[...]).T.astype(BF16)
    weight_two = six_left(mid_weight_ref[...]).T.astype(BF16)
    high, low = split_two(out_weight_ref[...])
    high, low = high.astype(F32), low.astype(F32)
    out_rows_ref[...] = jnp.concatenate([high, high, low], axis=0).T
    weight_three = out_rows_ref[pl.ds(first_channel, own), :].astype(BF16)
    vec_ref[...] = jnp.zeros_like(vec_ref)
    vec_ref[0:1, : embed_bias_ref.shape[1]] = embed_bias_ref[...]
    vec_ref[1:2, : embed_bias_ref.shape[1]] = mid_bias_ref[...]
    vec_ref[2:3, : embed_bias_ref.shape[1]] = sine_freq_ref[...]
    vectors = vec_ref[...].T[: embed_bias_ref.shape[1]]
    bias_one, bias_two, freq = vectors[:, 0:1], vectors[:, 1:2], vectors[:, 2:3]
    decay = decay_ref[pl.ds(first_channel, own), :]
    scale = jnp.sqrt(2.0 * decay)

    def tile(index, carry):
        start = pl.multiple_of(index * TILE, TILE)
        first = sine(
            freq * (matmul(weight_one, six_right(embed_ref[:, pl.ds(start, TILE)])) + bias_one)
        )
        second = sine(freq * (matmul(weight_two, six_right(first)) + bias_two))
        raw = matmul(weight_three, stack_three(second))
        positions = (start + lax.broadcasted_iota(jnp.int32, (own, TILE), 1)).astype(F32)
        vals = raw * (scale * jnp.exp(-decay * positions))
        for j in range(TILE // LANES):
            row = pl.multiple_of(index * (TILE // LANES * own) + j * own, own)
            filter_ref[pl.ds(row, own), :] = vals[:, j * LANES : (j + 1) * LANES]
        return carry

    lax.fori_loop(0, full_len // TILE, tile, 0)
    blocks = full_len // LANES
    columns = [filter_ref[pl.ds(c, blocks, stride=own), :] for c in range(own)]
    spectrum_ref[...] = forward(columns, outer_ref, twiddle_ref, inner_ref)
    taps = taps_ref[pl.ds(first_channel, own), :]
    for c in range(own):
        line = jnp.concatenate(
            [taps[c : c + 1], jnp.zeros((1, tap_count), F32)], axis=1
        )
        table = pltpu.roll(
            jnp.broadcast_to(line, (2 * tap_count, 2 * tap_count)),
            tap_count,
            1,
            stride=1,
            stride_axis=0,
        )[:, :tap_count]
        high, low = split_two(table)
        toeplitz_ref[c] = jnp.concatenate([high, low], axis=1)


def mix_kernel(
    own,
    skip_ref,
    parts_ref,
    spectrum_ref,
    toeplitz_ref,
    outer_ref,
    twiddle_ref,
    inner_ref,
    inner_back_ref,
    outer_back_ref,
    out_ref,
    signal_ref,
    in_gate_ref,
    out_gate_ref,
    mixed_ref,
):
    seq_devs, _, part_rows, _ = parts_ref.shape
    blocks = seq_devs * part_rows // own
    first_channel = lax.axis_index("seq") * own
    signal_ref[:own, :] = jnp.zeros((own, LANES), F32)
    for p in range(seq_devs):
        at = p * part_rows
        signal_ref[own + at : own + at + part_rows, :] = parts_ref[p, 0].astype(F32)
        in_gate_ref[at : at + part_rows, :] = parts_ref[p, 1].astype(F32)
        out_gate_ref[at : at + part_rows, :] = parts_ref[p, 2].astype(F32)
    gated = []
    for c in range(own):
        window = jnp.concatenate(
            [
                signal_ref[pl.ds(c, blocks, stride=own), :],
                signal_ref[pl.ds(own + c, blocks, stride=own), :],
            ],
            axis=1,
        ).astype(BF16)
        both = matmul(window, toeplitz_ref[c])
        gated.append(
            in_gate_ref[pl.ds(c, blocks, stride=own), :] * (both[:, :LANES] + both[:, LANES:])
        )
    vals = forward(gated, outer_ref, twiddle_ref, inner_ref)
    real, imag = vals[:, :LANES], vals[:, LANES:]
    filt_real, filt_imag = spectrum_ref[:, :LANES], spectrum_ref[:, LANES:]
    product = jnp.concatenate(
        [real * filt_real - imag * filt_imag, real * filt_imag + imag * filt_real], axis=1
    )
    conv = backward(product, own, inner_back_ref, twiddle_ref, outer_back_ref)
    for c in range(own):
        mixed_ref[pl.ds(c, blocks, stride=own), :] = out_gate_ref[
            pl.ds(c, blocks, stride=own), :
        ] * (conv[:, c * LANES : (c + 1) * LANES] + skip_ref[first_channel + c] * gated[c])
    for q in range(part_rows // own):
        if own % 8 == 0:
            column = jnp.concatenate(
                [
                    mixed_ref[p * part_rows + q * own : p * part_rows + (q + 1) * own, :]
                    for p in range(seq_devs)
                ],
                axis=0,
            )
            out_ref[:, q * LANES : (q + 1) * LANES] = column.astype(BF16)
        else:
            for c in range(own):
                signal_ref[pl.ds(c, seq_devs, stride=own), :] = mixed_ref[
                    pl.ds(q * own + c, seq_devs, stride=part_rows), :
                ]
            out_ref[:, q * LANES : (q + 1) * LANES] = signal_ref[: seq_devs * own, :].astype(BF16)


def on_device(
    signal,
    in_gate,
    out_gate,
    short_taps,
    skip_gain,
    decay_rate,
    embed_weight,
    embed_bias,
    sine_freq,
    mid_weight,
    mid_bias,
    out_weight,
):
    channels, local_len = signal.shape
    tap_count = short_taps.shape[1]
    hidden = mid_weight.shape[0]
    seq_devs = lax.axis_size("seq")
    own = -(-channels // seq_devs)
    spare = own * seq_devs - channels
    full_len = seq_devs * local_len
    blocks = full_len // LANES
    local_blocks = local_len // LANES
    outer, twiddle, inner, inner_back, outer_back = transform_tables(full_len)
    embed = embed_table(full_len)

    parts = jnp.stack([signal, in_gate, out_gate])
    if spare:
        parts = jnp.pad(parts, ((0, 0), (0, spare), (0, 0)))
        short_taps = jnp.pad(short_taps, ((0, spare), (0, 0)))
        skip_gain = jnp.pad(skip_gain, (0, spare))
        decay_rate = jnp.pad(decay_rate, (0, spare), mode="edge")
        out_weight = jnp.pad(out_weight, ((0, 0), (0, spare)))
    parts = parts.reshape(3, seq_devs, own, local_blocks, LANES)
    parts = parts.transpose(1, 0, 3, 2, 4).reshape(seq_devs, 3, local_blocks * own, LANES)
    parts = lax.all_to_all(parts, "seq", split_axis=0, concat_axis=0, tiled=True)

    spectrum, toeplitz = pl.pallas_call(
        functools.partial(filter_kernel, own),
        out_shape=(
            jax.ShapeDtypeStruct((own * blocks, 2 * LANES), F32),
            jax.ShapeDtypeStruct((own, 2 * tap_count, 2 * tap_count), BF16),
        ),
        scratch_shapes=[
            pltpu.VMEM((embed.shape[0], hidden), F32),
            pltpu.VMEM((8, LANES), F32),
            pltpu.VMEM((channels + spare, 3 * hidden), F32),
            pltpu.VMEM((blocks * own, LANES), F32),
        ],
        compiler_params=pltpu.CompilerParams(vmem_limit_bytes=48 * 2**20),
    )(
        embed,
        embed_weight,
        embed_bias[None, :],
        sine_freq[None, :],
        mid_weight,
        mid_bias[None, :],
        out_weight,
        decay_rate[:, None],
        short_taps,
        outer,
        twiddle,
        inner,
    )
    vmem = pl.BlockSpec(memory_space=pltpu.VMEM)
    mixed = pl.pallas_call(
        functools.partial(mix_kernel, own),
        out_shape=jax.ShapeDtypeStruct((channels + spare, local_len), BF16),
        in_specs=[pl.BlockSpec(memory_space=pltpu.SMEM)] + [vmem] * 8,
        out_specs=vmem,
        scratch_shapes=[pltpu.VMEM(((blocks + 1) * own, LANES), F32)]
        + [pltpu.VMEM((blocks * own, LANES), F32)] * 3,
        compiler_params=pltpu.CompilerParams(vmem_limit_bytes=48 * 2**20),
    )(skip_gain, parts, spectrum, toeplitz, outer, twiddle, inner, inner_back, outer_back)
    return lax.all_to_all(mixed, "seq", split_axis=0, concat_axis=0, tiled=True)[:channels]


def solution(mesh):
    in_specs = (
        P("ch", "seq"),
        P("ch", "seq"),
        P("ch", "seq"),
        P("ch", None),
        P("ch"),
        P("ch"),
        P(),
        P(),
        P(),
        P(),
        P(),
        P(None, "ch"),
    )
    out_specs = P("ch", "seq")
    return jax.shard_map(
        on_device, mesh=mesh, in_specs=in_specs, out_specs=out_specs, check_vma=False
    )
```

time: 329 us -> 46.6 us (0.14); the launches traced: 323 us -> 45.8 us
  matrix products: 92.1 us -> 0 us
  local copies, waits for them, and re-layouts: 101 us -> 10.4 us
  waiting for transfers between devices: 74 us -> 0.01 us
  starting transfers between devices: 48.2 us -> 8.46 us
  blocking collectives: 2 us -> 14.5 us
  Pallas kernels: 0 us -> 10.4 us
  other arithmetic: 5.37 us -> 1.94 us
    dot_general x22 -> x0, matrix products: 92.1 us -> none  [the longest x3 19 us: transform_rows(): jnp.dot(flat_imag, offset_sin, precision=lax.Precision.HIGHEST, preferred...]
    all_to_all x9 -> x1, waiting for transfers between devices: 74 us -> 0.01 us  [on_device(): lax.all_to_all(parts, 'seq', split_axis=0, concat_axis=0, tiled=True)]
    reshape x9 -> x0, local copies, waits for them, and re-layouts: 39.4 us -> none  [the longest x1 32 us: causal_matrix(): return tiled.reshape(channels, tap_count, period - 1)[:, :, :2 * tap_count]]
    all_to_all x9 -> x1, starting transfers between devices: 44.2 us -> 8.46 us  [on_device(): lax.all_to_all(parts, 'seq', split_axis=0, concat_axis=0, tiled=True)]
    all_to_all x0 -> x1, blocking collectives: none -> 14.5 us  [on_device(): lax.all_to_all(mixed, 'seq', split_axis=0, concat_axis=0, tiled=True)]
    unnamed x17 -> x37, local copies, waits for them, and re-layouts: 23.6 us -> 9.7 us
    pallas_call x0 -> x2, Pallas kernels: none -> 10.4 us  [the longest x1 8.32 us: on_device(): pl.pallas_call(functools.partial(filter_kernel, own), out_shape=(jax.Shap...]
    another operation x2 -> x0, local copies, waits for them, and re-layouts: 10 us -> none  [the longest x1 9.92 us: causal_matrix(): tiled = jnp.tile(pattern, (1, tap_count))[:, :tap_count * (period - 1)]]
  transfers between devices with their start and end apart: 10 -> 1, of which waited for: 7 -> 0; matrix products, arithmetic and copies ran while one was open for 41% -> 2% of each run, Pallas kernels for 0% -> 18%
where the time goes in v1:
time: 46.6 us; the launch traced here: 45.8 us
  blocking collectives  14.5 us (31%)
  local copies, waits for them, and re-layouts  10.4 us (22%)
  Pallas kernels  10.4 us (22%)
  starting transfers between devices  8.46 us (18%)
  other arithmetic  1.94 us (4%)
    all_to_all x1, blocking collectives, on_device(): lax.all_to_all(mixed, 'seq', split_axis=0, concat_axis=0, tiled=True)  14.5 us
    unnamed x37, local copies, waits for them, and re-layouts  9.7 us
    all_to_all x1, starting transfers between devices, on_device(): lax.all_to_all(parts, 'seq', split_axis=0, concat_axis=0, tiled=True)  8.46 us
    pallas_call x1, Pallas kernels, on_device(): pl.pallas_call(functools.partial(filter_kernel, own), out_shape=(jax.Shap...  8.32 us
    pallas_call x1, Pallas kernels, on_device(): pl.pallas_call(functools.partial(mix_kernel, own), out_shape=jax.ShapeDty...  2.04 us
    reshape x1, other arithmetic, on_device(): parts.transpose(1, 0, 3, 2, 4)  1.94 us
  transfers between devices with their start and end apart: 1, of which 0 were waited for; matrix products, arithmetic and copies ran while one was open for 2% of the time, Pallas kernels for 18%

profile of v1, /device:TPU:0, one launch (start us, length us, event | category | flops | bytes accessed | tf_op | source)
XLA Modules:
  0.0 45.8 jit_solution(7549527283940860246)
XLA Ops:
  0.0 0.0 copy-start.1
  0.0 0.0 copy-start
  0.0 0.0 copy-start.17
  0.0 0.0 copy-start.16
  0.0 0.0 copy-start.15
  0.0 0.0 copy-start.14
  0.0 1.9 %maximum_bitcast_fusion = bf16[16,3,32,128]{3,2,1,0:T(8,128)(2,1)} fusion(bf16[1,16,8,4,128]{4,2,3,0,1:T(8,128)(2,1)} %bitcast.24, bf16[1,16,8,4,128]{4,2,3,0,1:T(8,128)(2,1)} %bitcast.25, bf16[1,16,8,4,128]{4,2,3,0,1:T(8,128)(2,1)} %bitcast.26), kind=kLoop, calls=%fused_computation | loop fusion | flops 393216 | bytes 786432 | tf_op jit(solution)/shard_map/reshape | solution.py:338
  2.0 0.0 copy-start.13
  2.0 8.5 %all-to-all-start = ((bf16[16,3,32,128]{3,2,1,0:T(8,128)(2,1)}), bf16[16,3,32,128]{3,2,1,0:T(8,128)(2,1)S(1)}, u32[]{:S(2)}, u32[]{:S(2)}) async-start(bf16[16,3,32,128]{3,2,1,0:T(8,128)(2,1)} %maximum_bitcast_fusion), calls=%async_computation | async-start | bytes 786432 | tf_op jit(solution)/shard_map/all_to_all | solution.py:339
  10.4 0.0 copy-done.17
  10.4 0.7 %copy.22.decay_ref = f32[128,1]{1,0:T(8,128)} copy(f32[128,1]{0,1:T(1,128)S(1)} %bitcast.27) | data formatting | bytes 1024 | tf_op jit(solution)/shard_map/broadcast_in_dim | solution.py:362
  11.2 0.0 copy-done.1
  11.2 0.0 copy-done
  11.2 0.0 copy-done.16
  11.2 0.0 copy-done.15
  11.2 0.0 copy-done.14
  11.2 0.0 copy-start.3
  11.2 0.8 %copy-done.3 = f32[2,64,128]{2,1,0:T(8,128)S(1)} copy-done((f32[2,64,128]{2,1,0:T(8,128)S(1)}, f32[2,64,128]{2,1,0:T(8,128)}, u32[]{:S(2)}) %copy-start.3) | copy-done | bytes 65560
  12.1 0.0 copy-start.5
  12.1 0.8 %copy-done.5 = bf16[128,192]{1,0:T(8,128)(2,1)S(1)} copy-done((bf16[128,192]{1,0:T(8,128)(2,1)S(1)}, bf16[128,192]{1,0:T(8,128)(2,1)}, u32[]{:S(2)}) %copy-start.5) | copy-done | bytes 49176
  12.9 0.0 copy-start.7
  12.9 0.8 %copy-done.7 = f32[128,1]{1,0:T(8,128)S(1)} copy-done((f32[128,1]{1,0:T(8,128)S(1)}, f32[128,1]{1,0:T(8,128)}, u32[]{:S(2)}) %copy-start.7) | copy-done | bytes 536
  13.7 0.0 copy-start.8
  13.7 0.8 %copy-done.8 = f32[128,128]{1,0:T(8,128)S(1)} copy-done((f32[128,128]{1,0:T(8,128)S(1)}, f32[128,128]{1,0:T(8,128)}, u32[]{:S(2)}) %copy-start.8) | copy-done | bytes 65560
  14.6 0.0 copy-start.10
  14.6 0.8 %copy-done.10 = f32[64,64]{1,0:T(8,128)S(1)} copy-done((f32[64,64]{1,0:T(8,128)S(1)}, f32[64,64]{1,0:T(8,128)}, u32[]{:S(2)}) %copy-start.10) | copy-done | bytes 16408
  15.3 0.0 copy-start.11
  15.3 0.8 %copy-done.11 = f32[64,128]{1,0:T(8,128)S(1)} copy-done((f32[64,128]{1,0:T(8,128)S(1)}, f32[64,128]{1,0:T(8,128)}, u32[]{:S(2)}) %copy-start.11) | copy-done | bytes 32792
  16.1 0.0 copy-start.12
  16.1 0.7 %copy-done.12 = f32[33,64]{1,0:T(8,128)S(1)} copy-done((f32[33,64]{1,0:T(8,128)S(1)}, f32[33,64]{1,0:T(8,128)}, u32[]{:S(2)}) %copy-start.12) | copy-done | bytes 8472
  16.8 8.3 %shard_map.172 = (f32[512,256]{1,0:T(8,128)S(1)}, bf16[8,256,256]{2,1,0:T(8,128)(2,1)S(1)}) custom-call(f32[40,8192]{1,0:T(8,128)S(1)} %copy-done, f32[33,64]{1,0:T(8,128)S(1)} %copy-done.12, f32[1,64]{1,0:T(1,128)S(1)} %bitcast.20, f32[1,64]{1,0:T(1,128)S(1)} %bitcast.21, f32[64,64]{1,0:T(8,128)S(1)} %copy-done.10, f32[1,64]{1,0:T(1,128)S(1)} %bitcast.22, ...), custom_call_target="tpu_custom_call" | custom-call | tf_op jit(solution)/shard_map/pallas_call | solution.py:341
  25.1 0.0 all-to-all-done.parts_ref
  25.2 0.0 copy-done.13
  25.2 0.0 copy-start.2
  25.2 0.9 %copy-done.2 = bf16[2,256,256]{2,1,0:T(8,128)(2,1)S(1)} copy-done((bf16[2,256,256]{2,1,0:T(8,128)(2,1)S(1)}, bf16[2,256,256]{2,1,0:T(8,128)(2,1)}, u32[]{:S(2)}) %copy-start.2) | copy-done | bytes 262168
  26.1 0.0 copy-start.4
  26.1 0.8 %copy-done.4 = f32[2,64,128]{2,1,0:T(8,128)S(1)} copy-done((f32[2,64,128]{2,1,0:T(8,128)S(1)}, f32[2,64,128]{2,1,0:T(8,128)}, u32[]{:S(2)}) %copy-start.4) | copy-done | bytes 65560
  27.0 0.0 copy-start.6
  27.0 0.8 %copy-done.6 = bf16[128,192]{1,0:T(8,128)(2,1)S(1)} copy-done((bf16[128,192]{1,0:T(8,128)(2,1)S(1)}, bf16[128,192]{1,0:T(8,128)(2,1)}, u32[]{:S(2)}) %copy-start.6) | copy-done | bytes 49176
  27.8 0.0 copy-start.9
  27.8 0.8 %copy-done.9 = bf16[64,384]{1,0:T(8,128)(2,1)S(1)} copy-done((bf16[64,384]{1,0:T(8,128)(2,1)S(1)}, bf16[64,384]{1,0:T(8,128)(2,1)}, u32[]{:S(2)}) %copy-start.9) | copy-done | bytes 49176
  28.6 2.0 %shard_map.173 = bf16[128,512]{1,0:T(8,128)(2,1)S(1)} custom-call(f32[128]{0:T(128)S(1)} %copy-done.13, bf16[16,3,32,128]{3,2,1,0:T(8,128)(2,1)S(1)} %all-to-all-done.parts_ref, f32[512,256]{1,0:T(8,128)S(1)} %get-tuple-element.7.spectrum_ref, bf16[8,256,256]{2,1,0:T(8,128)(2,1)S(1)} %get-tuple-element.8.toeplitz_ref, bf16[128,192]{1,0:T(8,128)(2,1)S(1)} %copy-done.6, ...), custom_call_target="tpu_custom_call" | custom-call | tf_op jit(solution)/shard_map/pallas_call | solution.py:369
  30.6 14.5 %all_to_all.17 = bf16[16,8,512]{2,1,0:T(8,128)(2,1)S(1)} all-to-all(bf16[16,8,512]{2,1,0:T(8,128)(2,1)S(1)} %bitcast.19), channel_id=1, replica_groups=mesh['seq'=16,'ch'=2] {'seq'}, dimensions={0} | all-to-all | bytes 262144 | tf_op jit(solution)/shard_map/all_to_all | solution.py:378
  45.2 0.7 %copy.24 = bf16[128,512]{1,0:T(8,128)(2,1)} copy(bf16[128,512]{1,0:T(8,128)(2,1)S(1)} %bitcast.23) | data formatting | bytes 262144
Async XLA Ops:
  0.0 11.2 %copy-start.1 = (bf16[2,256,256]{2,1,0:T(8,128)(2,1)S(1)}, bf16[2,256,256]{2,1,0:T(8,128)(2,1)}, u32[]{:S(2)}) copy-start(bf16[2,256,256]{2,1,0:T(8,128)(2,1)} %constant.15.clone.inner_ref) | copy-start | bytes 786436
  0.0 11.2 %copy-start = (f32[40,8192]{1,0:T(8,128)S(1)}, f32[40,8192]{1,0:T(8,128)}, u32[]{:S(2)}) copy-start(f32[40,8192]{1,0:T(8,128)} %constant.12.clone.embed_ref) | copy-start | bytes 3932164
  0.0 10.4 %copy-start.17 = (f32[128]{0:T(128)S(1)}, f32[128]{0:T(128)}, u32[]{:S(2)}) copy-start(f32[128]{0:T(128)} %param.23) | copy-start | bytes 1540
  0.0 11.2 %copy-start.16 = (f32[64]{0:T(128)S(1)}, f32[64]{0:T(128)}, u32[]{:S(2)}) copy-start(f32[64]{0:T(128)} %param.28) | copy-start | bytes 772
  0.0 11.2 %copy-start.15 = (f32[64]{0:T(128)S(1)}, f32[64]{0:T(128)}, u32[]{:S(2)}) copy-start(f32[64]{0:T(128)} %param.26) | copy-start | bytes 772
  0.0 11.2 %copy-start.14 = (f32[64]{0:T(128)S(1)}, f32[64]{0:T(128)}, u32[]{:S(2)}) copy-start(f32[64]{0:T(128)} %param.25) | copy-start | bytes 772
  2.0 23.2 %copy-start.13 = (f32[128]{0:T(128)S(1)}, f32[128]{0:T(128)}, u32[]{:S(2)}) copy-start(f32[128]{0:T(128)} %skip_ref.1) | copy-start | bytes 1540
  2.0 23.2 %all-to-all-start = ((bf16[16,3,32,128]{3,2,1,0:T(8,128)(2,1)}), bf16[16,3,32,128]{3,2,1,0:T(8,128)(2,1)S(1)}, u32[]{:S(2)}, u32[]{:S(2)}) async-start(bf16[16,3,32,128]{3,2,1,0:T(8,128)(2,1)} %maximum_bitcast_fusion), calls=%async_computation | async-start | bytes 786432 | tf_op jit(solution)/shard_map/all_to_all | solution.py:339
  11.2 0.8 %copy-start.3 = (f32[2,64,128]{2,1,0:T(8,128)S(1)}, f32[2,64,128]{2,1,0:T(8,128)}, u32[]{:S(2)}) copy-start(f32[2,64,128]{2,1,0:T(8,128)} %constant.14.clone.twiddle_ref) | copy-start | bytes 196612
  12.1 0.8 %copy-start.5 = (bf16[128,192]{1,0:T(8,128)(2,1)S(1)}, bf16[128,192]{1,0:T(8,128)(2,1)}, u32[]{:S(2)}) copy-start(bf16[128,192]{1,0:T(8,128)(2,1)} %constant.13.clone.outer_ref) | copy-start | bytes 147460
  12.9 0.8 %copy-start.7 = (f32[128,1]{1,0:T(8,128)S(1)}, f32[128,1]{1,0:T(8,128)}, u32[]{:S(2)}) copy-start(f32[128,1]{1,0:T(8,128)} %copy.22.decay_ref) | copy-start | bytes 1540
  13.7 0.8 %copy-start.8 = (f32[128,128]{1,0:T(8,128)S(1)}, f32[128,128]{1,0:T(8,128)}, u32[]{:S(2)}) copy-start(f32[128,128]{1,0:T(8,128)} %taps_ref.1) | copy-start | bytes 196612
  14.6 0.8 %copy-start.10 = (f32[64,64]{1,0:T(8,128)S(1)}, f32[64,64]{1,0:T(8,128)}, u32[]{:S(2)}) copy-start(f32[64,64]{1,0:T(8,128)} %mid_weight_ref.1) | copy-start | bytes 49156
  15.3 0.8 %copy-start.11 = (f32[64,128]{1,0:T(8,128)S(1)}, f32[64,128]{1,0:T(8,128)}, u32[]{:S(2)}) copy-start(f32[64,128]{1,0:T(8,128)} %out_weight_ref.1) | copy-start | bytes 98308
  16.1 0.7 %copy-start.12 = (f32[33,64]{1,0:T(8,128)S(1)}, f32[33,64]{1,0:T(8,128)}, u32[]{:S(2)}) copy-start(f32[33,64]{1,0:T(8,128)} %embed_weight_ref.1) | copy-start | bytes 25348
  25.2 1.0 %copy-start.2 = (bf16[2,256,256]{2,1,0:T(8,128)(2,1)S(1)}, bf16[2,256,256]{2,1,0:T(8,128)(2,1)}, u32[]{:S(2)}) copy-start(bf16[2,256,256]{2,1,0:T(8,128)(2,1)} %constant.16.clone.inner_back_ref) | copy-start | bytes 786436
  26.1 0.8 %copy-start.4 = (f32[2,64,128]{2,1,0:T(8,128)S(1)}, f32[2,64,128]{2,1,0:T(8,128)}, u32[]{:S(2)}) copy-start(f32[2,64,128]{2,1,0:T(8,128)} %constant.14.clone.twiddle_ref) | copy-start | bytes 196612
  27.0 0.8 %copy-start.6 = (bf16[128,192]{1,0:T(8,128)(2,1)S(1)}, bf16[128,192]{1,0:T(8,128)(2,1)}, u32[]{:S(2)}) copy-start(bf16[128,192]{1,0:T(8,128)(2,1)} %constant.13.clone.outer_ref) | copy-start | bytes 147460
  27.8 0.8 %copy-start.9 = (bf16[64,384]{1,0:T(8,128)(2,1)S(1)}, bf16[64,384]{1,0:T(8,128)(2,1)}, u32[]{:S(2)}) copy-start(bf16[64,384]{1,0:T(8,128)(2,1)} %constant.17.clone.outer_back_ref) | copy-start | bytes 147460

commit v2 on v1

--- a/solution.py
+++ b/solution.py
@@ -14,6 +14,7 @@
 TILE = 1024
 F32 = jnp.float32
 BF16 = jnp.bfloat16
+in_space = pltpu.with_memory_space_constraint
 
 
 def round_up(count, step):
@@ -158,31 +159,76 @@
     return matmul(outer_back_ref[...], stack_three(jnp.concatenate(columns, axis=1)))
 
 
+def pack_kernel(signal_ref, in_gate_ref, out_gate_ref, parts_ref, sems):
+    copies = [
+        pltpu.make_async_copy(ref, parts_ref.at[:, i], sems.at[i])
+        for i, ref in enumerate((signal_ref, in_gate_ref, out_gate_ref))
+    ]
+    for copy in copies:
+        copy.start()
+    for copy in copies:
+        copy.wait()
+
+
 def filter_kernel(
     own,
-    embed_ref,
-    embed_weight_ref,
-    embed_bias_ref,
-    sine_freq_ref,
-    mid_weight_ref,
-    mid_bias_ref,
-    out_weight_ref,
-    decay_ref,
-    taps_ref,
+    embed_hbm,
+    embed_weight_hbm,
+    vectors_hbm,
+    mid_weight_hbm,
+    out_weight_hbm,
+    channel_hbm,
+    taps_hbm,
+    outer_hbm,
+    twiddle_hbm,
+    inner_hbm,
+    inner_back_hbm,
+    outer_back_hbm,
+    spectrum_ref,
+    toeplitz_ref,
+    skip_ref,
     outer_ref,
     twiddle_ref,
     inner_ref,
-    spectrum_ref,
-    toeplitz_ref,
+    inner_back_ref,
+    outer_back_ref,
+    embed_ref,
+    embed_weight_ref,
+    vectors_ref,
+    mid_weight_ref,
+    out_weight_ref,
+    channel_ref,
+    taps_ref,
     pad_ref,
-    vec_ref,
     out_rows_ref,
+    columns_ref,
     filter_ref,
+    sems,
 ):
+    pairs = [
+        (embed_weight_hbm, embed_weight_ref),
+        (vectors_hbm, vectors_ref),
+        (mid_weight_hbm, mid_weight_ref),
+        (out_weight_hbm, out_weight_ref),
+        (channel_hbm, channel_ref),
+        (embed_hbm, embed_ref),
+        (taps_hbm, taps_ref),
+        (outer_hbm, outer_ref),
+        (twiddle_hbm, twiddle_ref),
+        (inner_hbm, inner_ref),
+        (inner_back_hbm, inner_back_ref),
+        (outer_back_hbm, outer_back_ref),
+    ]
+    copies = [pltpu.make_async_copy(*pair, sems.at[i]) for i, pair in enumerate(pairs)]
+    for copy in copies:
+        copy.start()
     full_len = embed_ref.shape[1]
+    hidden = mid_weight_ref.shape[0]
     tap_count = taps_ref.shape[1]
     first_channel = pl.multiple_of(lax.axis_index("seq") * own, own)
     pad_ref[...] = jnp.zeros_like(pad_ref)
+    for copy in copies:
+        copy.wait()
     pad_ref[: embed_weight_ref.shape[0], :] = embed_weight_ref[...]
     weight_one = six_left(pad_ref[...]).T.astype(BF16)
     weight_two = six_left(mid_weight_ref[...]).T.astype(BF16)
@@ -190,13 +236,11 @@
     high, low = high.astype(F32), low.astype(F32)
     out_rows_ref[...] = jnp.concatenate([high, high, low], axis=0).T
     weight_three = out_rows_ref[pl.ds(first_channel, own), :].astype(BF16)
-    vec_ref[...] = jnp.zeros_like(vec_ref)
-    vec_ref[0:1, : embed_bias_ref.shape[1]] = embed_bias_ref[...]
-    vec_ref[1:2, : embed_bias_ref.shape[1]] = mid_bias_ref[...]
-    vec_ref[2:3, : embed_bias_ref.shape[1]] = sine_freq_ref[...]
-    vectors = vec_ref[...].T[: embed_bias_ref.shape[1]]
+    vectors = vectors_ref[...].T
     bias_one, bias_two, freq = vectors[:, 0:1], vectors[:, 1:2], vectors[:, 2:3]
-    decay = decay_ref[pl.ds(first_channel, own), :]
+    columns_ref[...] = channel_ref[...].T
+    decay = columns_ref[pl.ds(first_channel, own), 0:1]
+    skip_ref[...] = jnp.broadcast_to(columns_ref[pl.ds(first_channel, own), 1:2], skip_ref.shape)
     scale = jnp.sqrt(2.0 * decay)
 
     def tile(index, carry):
@@ -235,10 +279,10 @@
 
 def mix_kernel(
     own,
-    skip_ref,
     parts_ref,
     spectrum_ref,
     toeplitz_ref,
+    skip_ref,
     outer_ref,
     twiddle_ref,
     inner_ref,
@@ -250,15 +294,18 @@
     out_gate_ref,
     mixed_ref,
 ):
-    seq_devs, _, part_rows, _ = parts_ref.shape
-    blocks = seq_devs * part_rows // own
-    first_channel = lax.axis_index("seq") * own
+    seq_devs, _, _, local_len = parts_ref.shape
+    local_blocks = local_len // LANES
+    part_rows = local_blocks * own
+    blocks = seq_devs * local_blocks
     signal_ref[:own, :] = jnp.zeros((own, LANES), F32)
     for p in range(seq_devs):
-        at = p * part_rows
-        signal_ref[own + at : own + at + part_rows, :] = parts_ref[p, 0].astype(F32)
-        in_gate_ref[at : at + part_rows, :] = parts_ref[p, 1].astype(F32)
-        out_gate_ref[at : at + part_rows, :] = parts_ref[p, 2].astype(F32)
+        for q in range(local_blocks):
+            at = p * part_rows + q * own
+            lanes = slice(q * LANES, (q + 1) * LANES)
+            signal_ref[own + at : 2 * own + at, :] = parts_ref[p, 0, :, lanes].astype(F32)
+            in_gate_ref[at : at + own, :] = parts_ref[p, 1, :, lanes].astype(F32)
+            out_gate_ref[at : at + own, :] = parts_ref[p, 2, :, lanes].astype(F32)
     gated = []
     for c in range(own):
         window = jnp.concatenate(
@@ -282,8 +329,8 @@
     for c in range(own):
         mixed_ref[pl.ds(c, blocks, stride=own), :] = out_gate_ref[
             pl.ds(c, blocks, stride=own), :
-        ] * (conv[:, c * LANES : (c + 1) * LANES] + skip_ref[first_channel + c] * gated[c])
-    for q in range(part_rows // own):
+        ] * (conv[:, c * LANES : (c + 1) * LANES] + skip_ref[c : c + 1, :] * gated[c])
+    for q in range(local_blocks):
         if own % 8 == 0:
             column = jnp.concatenate(
                 [
@@ -327,54 +374,63 @@
     outer, twiddle, inner, inner_back, outer_back = transform_tables(full_len)
     embed = embed_table(full_len)
 
-    parts = jnp.stack([signal, in_gate, out_gate])
+    parts = [signal, in_gate, out_gate]
     if spare:
-        parts = jnp.pad(parts, ((0, 0), (0, spare), (0, 0)))
+        parts = [jnp.pad(part, ((0, spare), (0, 0))) for part in parts]
         short_taps = jnp.pad(short_taps, ((0, spare), (0, 0)))
         skip_gain = jnp.pad(skip_gain, (0, spare))
         decay_rate = jnp.pad(decay_rate, (0, spare), mode="edge")
         out_weight = jnp.pad(out_weight, ((0, 0), (0, spare)))
-    parts = parts.reshape(3, seq_devs, own, local_blocks, LANES)
-    parts = parts.transpose(1, 0, 3, 2, 4).reshape(seq_devs, 3, local_blocks * own, LANES)
+    hbm = pl.BlockSpec(memory_space=pltpu.HBM)
+    vmem = pl.BlockSpec(memory_space=pltpu.VMEM)
+    parts = pl.pallas_call(
+        pack_kernel,
+        out_shape=pltpu.VMEM((seq_devs, 3, own, local_len), BF16),
+        in_specs=[hbm] * 3,
+        out_specs=vmem,
+        scratch_shapes=[pltpu.SemaphoreType.DMA((3,))],
+    )(*[in_space(part.reshape(seq_devs, own, local_len), pltpu.HBM) for part in parts])
     parts = lax.all_to_all(parts, "seq", split_axis=0, concat_axis=0, tiled=True)
 
-    spectrum, toeplitz = pl.pallas_call(
+    params = (
+        embed,
+        embed_weight,
+        jnp.stack([embed_bias, mid_bias, sine_freq]),
+        mid_weight,
+        out_weight,
+        jnp.stack([decay_rate, skip_gain]),
+        short_taps,
+    )
+    tables = (outer, twiddle, inner, inner_back, outer_back)
+    shared = pl.pallas_call(
         functools.partial(filter_kernel, own),
         out_shape=(
-            jax.ShapeDtypeStruct((own * blocks, 2 * LANES), F32),
-            jax.ShapeDtypeStruct((own, 2 * tap_count, 2 * tap_count), BF16),
-        ),
-        scratch_shapes=[
+            pltpu.VMEM((own * blocks, 2 * LANES), F32),
+            pltpu.VMEM((own, 2 * tap_count, 2 * tap_count), BF16),
+            pltpu.VMEM((own, LANES), F32),
+        )
+        + tuple(pltpu.VMEM(table.shape, table.dtype) for table in tables),
+        in_specs=[hbm] * (len(params) + len(tables)),
+        out_specs=(vmem,) * (3 + len(tables)),
+        scratch_shapes=[pltpu.VMEM(param.shape, F32) for param in params]
+        + [
             pltpu.VMEM((embed.shape[0], hidden), F32),
-            pltpu.VMEM((8, LANES), F32),
             pltpu.VMEM((channels + spare, 3 * hidden), F32),
+            pltpu.VMEM((channels + spare, 2), F32),
             pltpu.VMEM((blocks * own, LANES), F32),
+            pltpu.SemaphoreType.DMA((len(params) + len(tables),)),
         ],
         compiler_params=pltpu.CompilerParams(vmem_limit_bytes=48 * 2**20),
-    )(
-        embed,
-        embed_weight,
-        embed_bias[None, :],
-        sine_freq[None, :],
-        mid_weight,
-        mid_bias[None, :],
-        out_weight,
-        decay_rate[:, None],
-        short_taps,
-        outer,
-        twiddle,
-        inner,
-    )
-    vmem = pl.BlockSpec(memory_space=pltpu.VMEM)
+    )(*[in_space(jnp.asarray(vals), pltpu.HBM) for vals in params + tables])
     mixed = pl.pallas_call(
         functools.partial(mix_kernel, own),
         out_shape=jax.ShapeDtypeStruct((channels + spare, local_len), BF16),
-        in_specs=[pl.BlockSpec(memory_space=pltpu.SMEM)] + [vmem] * 8,
+        in_specs=[vmem] * (1 + len(shared)),
         out_specs=vmem,
         scratch_shapes=[pltpu.VMEM(((blocks + 1) * own, LANES), F32)]
         + [pltpu.VMEM((blocks * own, LANES), F32)] * 3,
         compiler_params=pltpu.CompilerParams(vmem_limit_bytes=48 * 2**20),
-    )(skip_gain, parts, spectrum, toeplitz, outer, twiddle, inner, inner_back, outer_back)
+    )(parts, *[in_space(vals, pltpu.VMEM) for vals in shared])
     return lax.all_to_all(mixed, "seq", split_axis=0, concat_axis=0, tiled=True)[:channels]
 
 

time: 46.6 us -> 38.4 us (0.82); the launches traced: 45.8 us -> 38.1 us
  local copies, waits for them, and re-layouts: 10.4 us -> 0.67 us
  Pallas kernels: 10.4 us -> 13.4 us
  blocking collectives: 14.5 us -> 13.1 us
  waiting for transfers between devices: 0.01 us -> 1.38 us
  other arithmetic: 1.94 us -> 1.19 us
    unnamed x37 -> x11, local copies, waits for them, and re-layouts: 9.7 us -> 0.67 us
    pallas_call x1 -> x2, Pallas kernels: 8.32 us -> 11.9 us  [the longest x1 10 us: on_device(): pl.pallas_call(functools.partial(filter_kernel, own), out_shape=(pltpu.VM...]
    reshape x1 -> x0, other arithmetic: 1.94 us -> none  [on_device(): parts.transpose(1, 0, 3, 2, 4)]
    all_to_all x1, blocking collectives: 14.5 us -> 13.1 us  [on_device(): lax.all_to_all(mixed, 'seq', split_axis=0, concat_axis=0, tiled=True)]
    all_to_all x1, waiting for transfers between devices: 0.01 us -> 1.38 us  [on_device(): lax.all_to_all(parts, 'seq', split_axis=0, concat_axis=0, tiled=True)]
    another operation x0 -> x2, other arithmetic: none -> 1.19 us  [the longest x1 0.6 us: on_device(): jnp.stack([decay_rate, skip_gain])]
    broadcast_in_dim x1 -> x0, local copies, waits for them, and re-layouts: 0.74 us -> none  [on_device(): decay_rate[:, None]]
    pallas_call x1, Pallas kernels: 2.04 us -> 1.51 us  [on_device(): pl.pallas_call(functools.partial(mix_kernel, own), out_shape=jax.ShapeDty...]
  transfers between devices with their start and end apart: 1 -> 1, of which waited for: 0 -> 1; matrix products, arithmetic and copies ran while one was open for 2% -> 3% of each run, Pallas kernels for 18% -> 26%
where the time goes in v2:
time: 38.4 us; the launch traced here: 38.1 us
  Pallas kernels  13.4 us (35%)
  blocking collectives  13.1 us (34%)
  starting transfers between devices  8.32 us (22%)
  waiting for transfers between devices  1.38 us (4%)
  other arithmetic  1.19 us (3%)
  local copies, waits for them, and re-layouts  0.67 us (2%)
    all_to_all x1, blocking collectives, on_device(): lax.all_to_all(mixed, 'seq', split_axis=0, concat_axis=0, tiled=True)  13.1 us
    pallas_call x1, Pallas kernels, on_device(): pl.pallas_call(functools.partial(filter_kernel, own), out_shape=(pltpu.VM...  10 us
    all_to_all x1, starting transfers between devices, on_device(): lax.all_to_all(parts, 'seq', split_axis=0, concat_axis=0, tiled=True)  8.32 us
    pallas_call x1, Pallas kernels, on_device(): pl.pallas_call(pack_kernel, out_shape=pltpu.VMEM((seq_devs, 3, own, local...  1.86 us
    pallas_call x1, Pallas kernels, on_device(): pl.pallas_call(functools.partial(mix_kernel, own), out_shape=jax.ShapeDty...  1.51 us
    all_to_all x1, waiting for transfers between devices, on_device(): lax.all_to_all(parts, 'seq', split_axis=0, concat_axis=0, tiled=True)  1.38 us
  transfers between devices with their start and end apart: 1, of which 1 were waited for; matrix products, arithmetic and copies ran while one was open for 3% of the time, Pallas kernels for 26%

profile of v2, /device:TPU:0, one launch (start us, length us, event | category | flops | bytes accessed | tf_op | source)
XLA Modules:
  0.0 38.1 jit_solution(1358558559473989650)
XLA Ops:
  0.0 0.0 copy-start.4
  0.0 0.0 copy-start.3
  0.0 0.0 copy-start.1
  0.0 0.0 copy-start
  0.0 0.0 copy-start.2
  0.0 1.9 %shard_map.172 = bf16[16,3,8,512]{3,2,1,0:T(8,128)(2,1)} custom-call(bf16[16,8,512]{2,1,0:T(8,128)(2,1)} %bitcast.12, bf16[16,8,512]{2,1,0:T(8,128)(2,1)} %bitcast.13, bf16[16,8,512]{2,1,0:T(8,128)(2,1)} %bitcast.14), custom_call_target="tpu_custom_call" | custom-call | tf_op jit(solution)/shard_map/pallas_call | solution.py:386
  1.9 8.3 %all-to-all-start = ((bf16[16,3,8,512]{3,2,1,0:T(8,128)(2,1)}), bf16[16,3,8,512]{3,2,1,0:T(8,128)(2,1)S(1)}, u32[]{:S(2)}, u32[]{:S(2)}) async-start(bf16[16,3,8,512]{3,2,1,0:T(8,128)(2,1)} %shard_map.172), calls=%async_computation | async-start | bytes 786432 | tf_op jit(solution)/shard_map/all_to_all | solution.py:393
  10.2 0.0 copy-done.4
  10.2 0.0 copy-done.3
  10.2 0.6 %pad_maximum_fusion.1.channel_hbm = f32[2,128]{1,0:T(2,128)} fusion(f32[1,128]{1,0:T(1,128)S(1)} %bitcast.18, f32[1,128]{1,0:T(1,128)S(1)} %bitcast.19), kind=kLoop, calls=%fused_computation.1 | loop fusion | flops 256 | bytes 2048 | tf_op jit(solution)/shard_map/stack | solution.py:401
  10.8 0.0 copy-done.1
  10.8 0.0 copy-done
  10.8 0.0 copy-done.2
  10.8 0.6 %pad_maximum_fusion.vectors_hbm = f32[3,64]{1,0:T(4,128)} fusion(f32[1,64]{1,0:T(1,128)S(1)} %bitcast.15, f32[1,64]{1,0:T(1,128)S(1)} %bitcast.16, f32[1,64]{1,0:T(1,128)S(1)} %bitcast.17), kind=kLoop, calls=%fused_computation | loop fusion | flops 384 | bytes 1536 | tf_op jit(solution)/shard_map/stack | solution.py:398
  11.4 10.0 %shard_map.173 = (f32[512,256]{1,0:T(8,128)S(1)}, bf16[8,256,256]{2,1,0:T(8,128)(2,1)S(1)}, f32[8,128]{1,0:T(8,128)S(1)}, bf16[128,192]{1,0:T(8,128)(2,1)S(1)}, ...) custom-call(f32[40,8192]{1,0:T(8,128)} %constant.12.clone.embed_hbm,, ...), custom_call_target="tpu_custom_call" | custom-call | tf_op jit(solution)/shard_map/pallas_call | solution.py:405
  21.5 1.4 %all-to-all-done.parts_ref = bf16[16,3,8,512]{3,2,1,0:T(8,128)(2,1)S(1)} async-done(((bf16[16,3,8,512]{3,2,1,0:T(8,128)(2,1)}), bf16[16,3,8,512]{3,2,1,0:T(8,128)(2,1)S(1)}, u32[]{:S(2)}, u32[]{:S(2)}) %all-to-all-start) | async-done | bytes 393248 | tf_op jit(solution)/shard_map/all_to_all | solution.py:393
  22.9 1.5 %shard_map.174 = bf16[128,512]{1,0:T(8,128)(2,1)S(1)} custom-call(bf16[16,3,8,512]{3,2,1,0:T(8,128)(2,1)S(1)} %all-to-all-done.parts_ref, f32[512,256]{1,0:T(8,128)S(1)} %get-tuple-element.13.spectrum_ref, bf16[8,256,256]{2,1,0:T(8,128)(2,1)S(1)} %get-tuple-element.14.toeplitz_ref, f32[8,128]{1,0:T(8,128)S(1)} %get-tuple-element.15.skip_ref, ...), custom_call_target="tpu_custom_call" | custom-call | tf_op jit(solution)/shard_map/pallas_call | solution.py:425
  24.4 13.1 %all_to_all.17 = bf16[16,8,512]{2,1,0:T(8,128)(2,1)S(1)} all-to-all(bf16[16,8,512]{2,1,0:T(8,128)(2,1)S(1)} %bitcast.10), channel_id=1, replica_groups=mesh['seq'=16,'ch'=2] {'seq'}, dimensions={0} | all-to-all | bytes 262144 | tf_op jit(solution)/shard_map/all_to_all | solution.py:434
  37.5 0.7 %copy.20 = bf16[128,512]{1,0:T(8,128)(2,1)} copy(bf16[128,512]{1,0:T(8,128)(2,1)S(1)} %bitcast.11) | data formatting | bytes 262144
Async XLA Ops:
  0.0 10.2 %copy-start.4 = (f32[128]{0:T(128)S(1)}, f32[128]{0:T(128)}, u32[]{:S(2)}) copy-start(f32[128]{0:T(128)} %param.23) | copy-start | bytes 1540
  0.0 10.2 %copy-start.3 = (f32[128]{0:T(128)S(1)}, f32[128]{0:T(128)}, u32[]{:S(2)}) copy-start(f32[128]{0:T(128)} %param.22) | copy-start | bytes 1540
  0.0 10.8 %copy-start.1 = (f32[64]{0:T(128)S(1)}, f32[64]{0:T(128)}, u32[]{:S(2)}) copy-start(f32[64]{0:T(128)} %param.28) | copy-start | bytes 772
  0.0 10.8 %copy-start = (f32[64]{0:T(128)S(1)}, f32[64]{0:T(128)}, u32[]{:S(2)}) copy-start(f32[64]{0:T(128)} %param.26) | copy-start | bytes 772
  0.0 10.8 %copy-start.2 = (f32[64]{0:T(128)S(1)}, f32[64]{0:T(128)}, u32[]{:S(2)}) copy-start(f32[64]{0:T(128)} %param.25) | copy-start | bytes 772
  1.9 21.0 %all-to-all-start = ((bf16[16,3,8,512]{3,2,1,0:T(8,128)(2,1)}), bf16[16,3,8,512]{3,2,1,0:T(8,128)(2,1)S(1)}, u32[]{:S(2)}, u32[]{:S(2)}) async-start(bf16[16,3,8,512]{3,2,1,0:T(8,128)(2,1)} %shard_map.172), calls=%async_computation | async-start | bytes 786432 | tf_op jit(solution)/shard_map/all_to_all | solution.py:393

commit v3 on v2

--- a/solution.py
+++ b/solution.py
@@ -11,7 +11,7 @@
 
 BANDS = 16
 LANES = 128
-TILE = 1024
+TILES = 4
 F32 = jnp.float32
 BF16 = jnp.bfloat16
 in_space = pltpu.with_memory_space_constraint
@@ -36,9 +36,13 @@
         angle = phase * (2.0 * math.pi / full_len)
         rows += [np.cos(angle), np.sin(angle)]
         phase = 2 * phase % full_len
-    table = np.zeros((round_up(len(rows), 8), full_len), np.float32)
+    rows.append(np.ones(full_len))
+    table = np.zeros((round_up(len(rows), 8), full_len))
     table[: len(rows)] = np.stack(rows)
-    return table
+    first, rest = halves(table)
+    second, third = halves(table - first.astype(np.float64))
+    stacked = np.concatenate([first, second, third], axis=0)
+    return np.pad(stacked, ((0, -len(stacked) % 16), (0, 0)))
 
 
 @functools.lru_cache(maxsize=None)
@@ -62,31 +66,23 @@
     return outer, twiddle, inner, inner_back, outer_back
 
 
-def sine_constants():
-    nodes = np.cos((np.arange(400) + 0.5) * math.pi / 400) * (math.pi / 2)
-    squares = nodes * nodes
-    basis = np.stack([squares**p for p in range(6)], axis=1)
-    fit = np.linalg.lstsq(basis, np.sin(nodes) / nodes, rcond=None)[0]
-    first = np.floor(math.pi * 2.0**13) / 2.0**13
-    second = np.floor((math.pi - first) * 2.0**28) / 2.0**28
-    return [float(v) for v in fit], (float(first), float(second), math.pi - first - second)
-
-
-SINE_FIT, PI_PARTS = sine_constants()
-
-
-def sine(angle):
-    turns = jnp.round(angle * (1.0 / math.pi))
-    rest = angle
-    for part in PI_PARTS:
-        rest = rest - turns * part
-    half = turns * 0.5
-    odd = half - jnp.floor(half)
-    square = rest * rest
-    value = SINE_FIT[5]
-    for term in SINE_FIT[4::-1]:
+def sine_fit(terms):
+    nodes = np.cos((np.arange(400) + 0.5) * math.pi / 400) * 0.5
+    basis = np.stack([nodes ** (2 * p + 1) for p in range(terms)], axis=1)
+    fit = np.linalg.lstsq(basis, np.sin(2.0 * math.pi * nodes), rcond=None)[0]
+    return [float(v) for v in fit]
+
+
+SINE_FIT = sine_fit(7)
+
+
+def sine_of_turns(turns):
+    part = turns - jnp.round(turns)
+    square = part * part
+    value = SINE_FIT[-1]
+    for term in SINE_FIT[-2::-1]:
         value = value * square + term
-    return value * (rest - rest * (4.0 * odd))
+    return value * part
 
 
 def split_two(vals):
@@ -103,16 +99,6 @@
 
 def matmul(lhs, rhs):
     return jnp.dot(lhs, rhs, preferred_element_type=F32)
-
-
-def six_left(vals):
-    one, two, three = split_three(vals)
-    return jnp.concatenate([one, one, two, one, three, two], axis=0)
-
-
-def six_right(vals):
-    one, two, three = split_three(vals)
-    return jnp.concatenate([one, two, one, three, one, two], axis=0).astype(BF16)
 
 
 def stack_three(vals):
@@ -174,10 +160,13 @@
     own,
     embed_hbm,
     embed_weight_hbm,
-    vectors_hbm,
+    embed_bias_hbm,
+    sine_freq_hbm,
     mid_weight_hbm,
+    mid_bias_hbm,
     out_weight_hbm,
-    channel_hbm,
+    decay_hbm,
+    skip_hbm,
     taps_hbm,
     outer_hbm,
     twiddle_hbm,
@@ -194,24 +183,35 @@
     outer_back_ref,
     embed_ref,
     embed_weight_ref,
-    vectors_ref,
+    embed_bias_ref,
+    sine_freq_ref,
     mid_weight_ref,
+    mid_bias_ref,
     out_weight_ref,
-    channel_ref,
+    decay_ref,
+    skip_row_ref,
     taps_ref,
     pad_ref,
+    vec_ref,
+    row_ref,
+    column_ref,
     out_rows_ref,
-    columns_ref,
     filter_ref,
     sems,
+    embed_sems,
 ):
+    full_len = embed_ref.shape[1]
+    tile_len = full_len // TILES
+    hidden = mid_weight_ref.shape[0]
     pairs = [
         (embed_weight_hbm, embed_weight_ref),
-        (vectors_hbm, vectors_ref),
+        (embed_bias_hbm, embed_bias_ref),
+        (sine_freq_hbm, sine_freq_ref),
         (mid_weight_hbm, mid_weight_ref),
+        (mid_bias_hbm, mid_bias_ref),
         (out_weight_hbm, out_weight_ref),
-        (channel_hbm, channel_ref),
-        (embed_hbm, embed_ref),
+        (decay_hbm, decay_ref),
+        (skip_hbm, skip_row_ref),
         (taps_hbm, taps_ref),
         (outer_hbm, outer_ref),
         (twiddle_hbm, twiddle_ref),
@@ -220,60 +220,92 @@
         (outer_back_hbm, outer_back_ref),
     ]
     copies = [pltpu.make_async_copy(*pair, sems.at[i]) for i, pair in enumerate(pairs)]
-    for copy in copies:
+    embed_copies = []
+    for i in range(TILES):
+        lanes = pl.ds(i * tile_len, tile_len)
+        embed_copies.append(
+            pltpu.make_async_copy(
+                embed_hbm.at[:, lanes], embed_ref.at[:, lanes], embed_sems.at[i]
+            )
+        )
+    for copy in copies[:8] + embed_copies + copies[8:]:
         copy.start()
-    full_len = embed_ref.shape[1]
-    hidden = mid_weight_ref.shape[0]
-    tap_count = taps_ref.shape[1]
     first_channel = pl.multiple_of(lax.axis_index("seq") * own, own)
     pad_ref[...] = jnp.zeros_like(pad_ref)
-    for copy in copies:
+    vec_ref[...] = jnp.zeros_like(vec_ref)
+    row_ref[...] = jnp.zeros_like(row_ref)
+    for copy in copies[:8]:
         copy.wait()
-    pad_ref[: embed_weight_ref.shape[0], :] = embed_weight_ref[...]
-    weight_one = six_left(pad_ref[...]).T.astype(BF16)
-    weight_two = six_left(mid_weight_ref[...]).T.astype(BF16)
-    high, low = split_two(out_weight_ref[...])
-    high, low = high.astype(F32), low.astype(F32)
-    out_rows_ref[...] = jnp.concatenate([high, high, low], axis=0).T
-    weight_three = out_rows_ref[pl.ds(first_channel, own), :].astype(BF16)
-    vectors = vectors_ref[...].T
-    bias_one, bias_two, freq = vectors[:, 0:1], vectors[:, 1:2], vectors[:, 2:3]
-    columns_ref[...] = channel_ref[...].T
-    decay = columns_ref[pl.ds(first_channel, own), 0:1]
-    skip_ref[...] = jnp.broadcast_to(columns_ref[pl.ds(first_channel, own), 1:2], skip_ref.shape)
+
+    freq = sine_freq_ref[...] * (0.5 / math.pi)
+    features = embed_weight_ref.shape[0]
+    pad_ref[:features, :] = embed_weight_ref[...] * freq
+    pad_ref[features : features + 1, :] = embed_bias_ref[...] * freq
+    one, two, three = split_three(pad_ref[...])
+    none = jnp.zeros_like(one)
+    rest = jnp.zeros((embed_ref.shape[0] - 3 * one.shape[0], hidden), F32)
+    weight_one = jnp.concatenate(
+        [
+            jnp.concatenate([one, one, one, rest], axis=0).T,
+            jnp.concatenate([two, two, none, rest], axis=0).T,
+            jnp.concatenate([three, none, none, rest], axis=0).T,
+        ],
+        axis=0,
+    ).astype(BF16)
+    one, two, _ = split_three(mid_weight_ref[...] * freq)
+    weight_two = jnp.concatenate(
+        [jnp.concatenate([one, one], axis=0).T, jnp.concatenate([two, two], axis=0).T], axis=0
+    ).astype(BF16)
+    vec_ref[0:1, :] = mid_bias_ref[...] * freq
+    bias_two = vec_ref[...].T[:, 0:1]
+    one, two, _ = split_three(out_weight_ref[...])
+    out_rows_ref[0] = jnp.concatenate([one, one], axis=0).T
+    out_rows_ref[1] = jnp.concatenate([two, two], axis=0).T
+    own_rows = pl.ds(first_channel, own)
+    weight_three = jnp.concatenate(
+        [out_rows_ref[0, own_rows, :], out_rows_ref[1, own_rows, :]], axis=0
+    ).astype(BF16)
+    row_ref[0:1, :] = decay_ref[...]
+    row_ref[1:2, :] = skip_row_ref[...]
+    column_ref[...] = row_ref[...].T
+    decay = column_ref[own_rows, 0:1]
+    skip_ref[...] = jnp.broadcast_to(column_ref[own_rows, 1:2], skip_ref.shape)
     scale = jnp.sqrt(2.0 * decay)
 
-    def tile(index, carry):
-        start = pl.multiple_of(index * TILE, TILE)
-        first = sine(
-            freq * (matmul(weight_one, six_right(embed_ref[:, pl.ds(start, TILE)])) + bias_one)
-        )
-        second = sine(freq * (matmul(weight_two, six_right(first)) + bias_two))
-        raw = matmul(weight_three, stack_three(second))
-        positions = (start + lax.broadcasted_iota(jnp.int32, (own, TILE), 1)).astype(F32)
-        vals = raw * (scale * jnp.exp(-decay * positions))
-        for j in range(TILE // LANES):
-            row = pl.multiple_of(index * (TILE // LANES * own) + j * own, own)
-            filter_ref[pl.ds(row, own), :] = vals[:, j * LANES : (j + 1) * LANES]
-        return carry
-
-    lax.fori_loop(0, full_len // TILE, tile, 0)
+    for i in range(TILES):
+        start = i * tile_len
+        embed_copies[i].wait()
+        turns = matmul(weight_one, embed_ref[:, start : start + tile_len])
+        first = sine_of_turns(
+            turns[:hidden] + turns[hidden : 2 * hidden] + turns[2 * hidden :]
+        )
+        turns = matmul(weight_two, jnp.concatenate(split_two(first), axis=0))
+        second = sine_of_turns(turns[:hidden] + turns[hidden:] + bias_two)
+        raw = matmul(weight_three, jnp.concatenate(split_two(second), axis=0))
+        positions = (start + lax.broadcasted_iota(jnp.int32, (own, tile_len), 1)).astype(F32)
+        vals = (raw[:own] + raw[own:]) * (scale * jnp.exp(-decay * positions))
+        for j in range(tile_len // LANES):
+            row = (start // LANES + j) * own
+            filter_ref[row : row + own, :] = vals[:, j * LANES : (j + 1) * LANES]
+
+    for copy in copies[8:]:
+        copy.wait()
     blocks = full_len // LANES
     columns = [filter_ref[pl.ds(c, blocks, stride=own), :] for c in range(own)]
     spectrum_ref[...] = forward(columns, outer_ref, twiddle_ref, inner_ref)
-    taps = taps_ref[pl.ds(first_channel, own), :]
+    taps = taps_ref[own_rows, :]
+    tap_count = taps.shape[1]
+    square = (tap_count, tap_count)
+    upper = lax.broadcasted_iota(jnp.int32, square, 1) >= lax.broadcasted_iota(
+        jnp.int32, square, 0
+    )
     for c in range(own):
-        line = jnp.concatenate(
-            [taps[c : c + 1], jnp.zeros((1, tap_count), F32)], axis=1
-        )
-        table = pltpu.roll(
-            jnp.broadcast_to(line, (2 * tap_count, 2 * tap_count)),
-            tap_count,
-            1,
-            stride=1,
-            stride_axis=0,
-        )[:, :tap_count]
-        high, low = split_two(table)
+        lags = pltpu.roll(
+            jnp.broadcast_to(taps[c : c + 1], square), 0, 1, stride=1, stride_axis=0
+        )
+        high, low = split_two(
+            jnp.concatenate([jnp.where(upper, 0.0, lags), jnp.where(upper, lags, 0.0)], axis=0)
+        )
         toeplitz_ref[c] = jnp.concatenate([high, low], axis=1)
 
 
@@ -348,6 +380,67 @@
             out_ref[:, q * LANES : (q + 1) * LANES] = signal_ref[: seq_devs * own, :].astype(BF16)
 
 
+def pack(parts, seq_devs, own):
+    local_len = parts[0].shape[1]
+    hbm = pl.BlockSpec(memory_space=pltpu.HBM)
+    return pl.pallas_call(
+        pack_kernel,
+        out_shape=pltpu.VMEM((seq_devs, 3, own, local_len), BF16),
+        in_specs=[hbm] * 3,
+        out_specs=pl.BlockSpec(memory_space=pltpu.VMEM),
+        scratch_shapes=[pltpu.SemaphoreType.DMA((3,))],
+    )(*[in_space(part.reshape(seq_devs, own, local_len), pltpu.HBM) for part in parts])
+
+
+def make_filter(params, own, full_len):
+    blocks = full_len // LANES
+    hidden, channels = params[5].shape
+    tap_count = params[8].shape[1]
+    embed = embed_table(full_len)
+    tables = transform_tables(full_len)
+    operands = (embed,) + params + tables
+    padded = round_up(params[0].shape[0] + 1, 8)
+    return pl.pallas_call(
+        functools.partial(filter_kernel, own),
+        out_shape=(
+            pltpu.VMEM((own * blocks, 2 * LANES), F32),
+            pltpu.VMEM((own, 2 * tap_count, 2 * tap_count), BF16),
+            pltpu.VMEM((own, LANES), F32),
+        )
+        + tuple(pltpu.VMEM(table.shape, table.dtype) for table in tables),
+        in_specs=[pl.BlockSpec(memory_space=pltpu.HBM)] * len(operands),
+        out_specs=(pl.BlockSpec(memory_space=pltpu.VMEM),) * (3 + len(tables)),
+        scratch_shapes=[pltpu.VMEM(embed.shape, BF16)]
+        + [pltpu.VMEM(vals.shape, F32) for vals in params]
+        + [
+            pltpu.VMEM((padded, hidden), F32),
+            pltpu.VMEM((8, hidden), F32),
+            pltpu.VMEM((8, channels), F32),
+            pltpu.VMEM((channels, 8), F32),
+            pltpu.VMEM((2, channels, 2 * hidden), F32),
+            pltpu.VMEM((blocks * own, LANES), F32),
+            pltpu.SemaphoreType.DMA((len(operands) - 1,)),
+            pltpu.SemaphoreType.DMA((TILES,)),
+        ],
+        compiler_params=pltpu.CompilerParams(vmem_limit_bytes=48 * 2**20),
+    )(*[in_space(jnp.asarray(vals), pltpu.HBM) for vals in operands])
+
+
+def mix(parts, shared):
+    seq_devs, _, own, local_len = parts.shape
+    rows = seq_devs * own * (local_len // LANES)
+    vmem = pl.BlockSpec(memory_space=pltpu.VMEM)
+    return pl.pallas_call(
+        functools.partial(mix_kernel, own),
+        out_shape=jax.ShapeDtypeStruct((seq_devs * own, local_len), BF16),
+        in_specs=[vmem] * (1 + len(shared)),
+        out_specs=vmem,
+        scratch_shapes=[pltpu.VMEM((rows + own, LANES), F32)]
+        + [pltpu.VMEM((rows, LANES), F32)] * 3,
+        compiler_params=pltpu.CompilerParams(vmem_limit_bytes=48 * 2**20),
+    )(parts, *[in_space(vals, pltpu.VMEM) for vals in shared])
+
+
 def on_device(
     signal,
     in_gate,
@@ -363,17 +456,9 @@
     out_weight,
 ):
     channels, local_len = signal.shape
-    tap_count = short_taps.shape[1]
-    hidden = mid_weight.shape[0]
     seq_devs = lax.axis_size("seq")
     own = -(-channels // seq_devs)
     spare = own * seq_devs - channels
-    full_len = seq_devs * local_len
-    blocks = full_len // LANES
-    local_blocks = local_len // LANES
-    outer, twiddle, inner, inner_back, outer_back = transform_tables(full_len)
-    embed = embed_table(full_len)
-
     parts = [signal, in_gate, out_gate]
     if spare:
         parts = [jnp.pad(part, ((0, spare), (0, 0))) for part in parts]
@@ -381,56 +466,21 @@
         skip_gain = jnp.pad(skip_gain, (0, spare))
         decay_rate = jnp.pad(decay_rate, (0, spare), mode="edge")
         out_weight = jnp.pad(out_weight, ((0, 0), (0, spare)))
-    hbm = pl.BlockSpec(memory_space=pltpu.HBM)
-    vmem = pl.BlockSpec(memory_space=pltpu.VMEM)
-    parts = pl.pallas_call(
-        pack_kernel,
-        out_shape=pltpu.VMEM((seq_devs, 3, own, local_len), BF16),
-        in_specs=[hbm] * 3,
-        out_specs=vmem,
-        scratch_shapes=[pltpu.SemaphoreType.DMA((3,))],
-    )(*[in_space(part.reshape(seq_devs, own, local_len), pltpu.HBM) for part in parts])
+    parts = pack(parts, seq_devs, own)
     parts = lax.all_to_all(parts, "seq", split_axis=0, concat_axis=0, tiled=True)
-
     params = (
-        embed,
         embed_weight,
-        jnp.stack([embed_bias, mid_bias, sine_freq]),
+        embed_bias[None, :],
+        sine_freq[None, :],
         mid_weight,
+        mid_bias[None, :],
         out_weight,
-        jnp.stack([decay_rate, skip_gain]),
+        decay_rate[None, :],
+        skip_gain[None, :],
         short_taps,
     )
-    tables = (outer, twiddle, inner, inner_back, outer_back)
-    shared = pl.pallas_call(
-        functools.partial(filter_kernel, own),
-        out_shape=(
-            pltpu.VMEM((own * blocks, 2 * LANES), F32),
-            pltpu.VMEM((own, 2 * tap_count, 2 * tap_count), BF16),
-            pltpu.VMEM((own, LANES), F32),
-        )
-        + tuple(pltpu.VMEM(table.shape, table.dtype) for table in tables),
-        in_specs=[hbm] * (len(params) + len(tables)),
-        out_specs=(vmem,) * (3 + len(tables)),
-        scratch_shapes=[pltpu.VMEM(param.shape, F32) for param in params]
-        + [
-            pltpu.VMEM((embed.shape[0], hidden), F32),
-            pltpu.VMEM((channels + spare, 3 * hidden), F32),
-            pltpu.VMEM((channels + spare, 2), F32),
-            pltpu.VMEM((blocks * own, LANES), F32),
-            pltpu.SemaphoreType.DMA((len(params) + len(tables),)),
-        ],
-        compiler_params=pltpu.CompilerParams(vmem_limit_bytes=48 * 2**20),
-    )(*[in_space(jnp.asarray(vals), pltpu.HBM) for vals in params + tables])
-    mixed = pl.pallas_call(
-        functools.partial(mix_kernel, own),
-        out_shape=jax.ShapeDtypeStruct((channels + spare, local_len), BF16),
-        in_specs=[vmem] * (1 + len(shared)),
-        out_specs=vmem,
-        scratch_shapes=[pltpu.VMEM(((blocks + 1) * own, LANES), F32)]
-        + [pltpu.VMEM((blocks * own, LANES), F32)] * 3,
-        compiler_params=pltpu.CompilerParams(vmem_limit_bytes=48 * 2**20),
-    )(parts, *[in_space(vals, pltpu.VMEM) for vals in shared])
+    shared = make_filter(params, own, seq_devs * local_len)
+    mixed = mix(parts, shared)
     return lax.all_to_all(mixed, "seq", split_axis=0, concat_axis=0, tiled=True)[:channels]
 
 

time: 38.4 us -> 36.4 us (0.948)
  waiting for transfers between devices: 1.38 us -> 6.47 us
  Pallas kernels: 13.4 us -> 9.48 us
  blocking collectives: 13.1 us -> 11.2 us
  other arithmetic: 1.19 us -> 0 us
    all_to_all x1, waiting for transfers between devices: 1.38 us -> 6.47 us  [on_device(): lax.all_to_all(parts, 'seq', split_axis=0, concat_axis=0, tiled=True)]
    pallas_call x3, Pallas kernels: 13.4 us -> 9.48 us  [the longest x1 6.16 us: make_filter(): pl.pallas_call(functools.partial(filter_kernel, own), out_shape=(pltpu.VM...]
    all_to_all x1, blocking collectives: 13.1 us -> 11.2 us  [on_device(): lax.all_to_all(mixed, 'seq', split_axis=0, concat_axis=0, tiled=True)]
    another operation x2 -> x0, other arithmetic: 1.19 us -> none  [the longest x1 0.6 us: on_device(): jnp.stack([decay_rate, skip_gain])]
  transfers between devices with their start and end apart: 1 -> 1, of which waited for: 1 -> 1; matrix products, arithmetic and copies ran while one was open for 3% -> 0% of each run, Pallas kernels for 26% -> 17%
where the time goes in v3:
time: 36.4 us; the launch traced here: 36.1 us
  blocking collectives  11.2 us (31%)
  Pallas kernels  9.48 us (26%)
  starting transfers between devices  8.32 us (23%)
  waiting for transfers between devices  6.47 us (18%)
  local copies, waits for them, and re-layouts  0.66 us (2%)
    all_to_all x1, blocking collectives, on_device(): lax.all_to_all(mixed, 'seq', split_axis=0, concat_axis=0, tiled=True)  11.2 us
    all_to_all x1, starting transfers between devices, on_device(): lax.all_to_all(parts, 'seq', split_axis=0, concat_axis=0, tiled=True)  8.32 us
    all_to_all x1, waiting for transfers between devices, on_device(): lax.all_to_all(parts, 'seq', split_axis=0, concat_axis=0, tiled=True)  6.47 us
    pallas_call x1, Pallas kernels, make_filter(): pl.pallas_call(functools.partial(filter_kernel, own), out_shape=(pltpu.VM...  6.16 us
    pallas_call x1, Pallas kernels, pack(): pl.pallas_call(pack_kernel, out_shape=pltpu.VMEM((seq_devs, 3, own, local...  1.81 us
    pallas_call x1, Pallas kernels, mix(): pl.pallas_call(functools.partial(mix_kernel, own), out_shape=jax.ShapeDty...  1.51 us
  transfers between devices with their start and end apart: 1, of which 1 were waited for; matrix products, arithmetic and copies ran while one was open for 0% of the time, Pallas kernels for 17%

profile of v3, /device:TPU:0, one launch (start us, length us, event | category | flops | bytes accessed | tf_op | source)
XLA Modules:
  0.0 36.1 jit_solution(370692728705956321)
XLA Ops:
  0.0 1.8 %shard_map.172 = bf16[16,3,8,512]{3,2,1,0:T(8,128)(2,1)} custom-call(bf16[16,8,512]{2,1,0:T(8,128)(2,1)} %bitcast.12, bf16[16,8,512]{2,1,0:T(8,128)(2,1)} %bitcast.13, bf16[16,8,512]{2,1,0:T(8,128)(2,1)} %bitcast.14), custom_call_target="tpu_custom_call" | custom-call | tf_op jit(solution)/shard_map/pallas_call | solution.py:386
  1.8 8.3 %all-to-all-start = ((bf16[16,3,8,512]{3,2,1,0:T(8,128)(2,1)}), bf16[16,3,8,512]{3,2,1,0:T(8,128)(2,1)S(1)}, u32[]{:S(2)}, u32[]{:S(2)}) async-start(bf16[16,3,8,512]{3,2,1,0:T(8,128)(2,1)} %shard_map.172), calls=%async_computation | async-start | bytes 786432 | tf_op jit(solution)/shard_map/all_to_all | solution.py:470
  10.2 6.2 %shard_map.173 = (f32[512,256]{1,0:T(8,128)S(1)}, bf16[8,256,256]{2,1,0:T(8,128)(2,1)S(1)}, f32[8,128]{1,0:T(8,128)S(1)}, bf16[128,192]{1,0:T(8,128)(2,1)S(1)}, ...) custom-call(bf16[128,8192]{1,0:T(8,128)(2,1)} %constant.12.clone.emb, ...), custom_call_target="tpu_custom_call" | custom-call | tf_op jit(solution)/shard_map/pallas_call | solution.py:403
  16.3 6.5 %all-to-all-done.parts_ref = bf16[16,3,8,512]{3,2,1,0:T(8,128)(2,1)S(1)} async-done(((bf16[16,3,8,512]{3,2,1,0:T(8,128)(2,1)}), bf16[16,3,8,512]{3,2,1,0:T(8,128)(2,1)S(1)}, u32[]{:S(2)}, u32[]{:S(2)}) %all-to-all-start) | async-done | bytes 393248 | tf_op jit(solution)/shard_map/all_to_all | solution.py:470
  22.8 1.5 %shard_map.174 = bf16[128,512]{1,0:T(8,128)(2,1)S(1)} custom-call(bf16[16,3,8,512]{3,2,1,0:T(8,128)(2,1)S(1)} %all-to-all-done.parts_ref, f32[512,256]{1,0:T(8,128)S(1)} %get-tuple-element.13.spectrum_ref, bf16[8,256,256]{2,1,0:T(8,128)(2,1)S(1)} %get-tuple-element.14.toeplitz_ref, f32[8,128]{1,0:T(8,128)S(1)} %get-tuple-element.15.skip_ref, ...), custom_call_target="tpu_custom_call" | custom-call | tf_op jit(solution)/shard_map/pallas_call | solution.py:433
  24.3 11.2 %all_to_all.17 = bf16[16,8,512]{2,1,0:T(8,128)(2,1)S(1)} all-to-all(bf16[16,8,512]{2,1,0:T(8,128)(2,1)S(1)} %bitcast.10), channel_id=1, replica_groups=mesh['seq'=16,'ch'=2] {'seq'}, dimensions={0} | all-to-all | bytes 262144 | tf_op jit(solution)/shard_map/all_to_all | solution.py:484
  35.5 0.7 %copy.20 = bf16[128,512]{1,0:T(8,128)(2,1)} copy(bf16[128,512]{1,0:T(8,128)(2,1)S(1)} %bitcast.11) | data formatting | bytes 262144
Async XLA Ops:
  1.8 21.0 %all-to-all-start = ((bf16[16,3,8,512]{3,2,1,0:T(8,128)(2,1)}), bf16[16,3,8,512]{3,2,1,0:T(8,128)(2,1)S(1)}, u32[]{:S(2)}, u32[]{:S(2)}) async-start(bf16[16,3,8,512]{3,2,1,0:T(8,128)(2,1)} %shard_map.172), calls=%async_computation | async-start | bytes 786432 | tf_op jit(solution)/shard_map/all_to_all | solution.py:470

commit v4 on v3

--- a/solution.py
+++ b/solution.py
@@ -145,10 +145,10 @@
     return matmul(outer_back_ref[...], stack_three(jnp.concatenate(columns, axis=1)))
 
 
-def pack_kernel(signal_ref, in_gate_ref, out_gate_ref, parts_ref, sems):
+def pack_kernel(signal_ref, in_gate_ref, parts_ref, sems):
     copies = [
         pltpu.make_async_copy(ref, parts_ref.at[:, i], sems.at[i])
-        for i, ref in enumerate((signal_ref, in_gate_ref, out_gate_ref))
+        for i, ref in enumerate((signal_ref, in_gate_ref))
     ]
     for copy in copies:
         copy.start()
@@ -323,7 +323,6 @@
     out_ref,
     signal_ref,
     in_gate_ref,
-    out_gate_ref,
     mixed_ref,
 ):
     seq_devs, _, _, local_len = parts_ref.shape
@@ -337,7 +336,6 @@
             lanes = slice(q * LANES, (q + 1) * LANES)
             signal_ref[own + at : 2 * own + at, :] = parts_ref[p, 0, :, lanes].astype(F32)
             in_gate_ref[at : at + own, :] = parts_ref[p, 1, :, lanes].astype(F32)
-            out_gate_ref[at : at + own, :] = parts_ref[p, 2, :, lanes].astype(F32)
     gated = []
     for c in range(own):
         window = jnp.concatenate(
@@ -359,9 +357,9 @@
     )
     conv = backward(product, own, inner_back_ref, twiddle_ref, outer_back_ref)
     for c in range(own):
-        mixed_ref[pl.ds(c, blocks, stride=own), :] = out_gate_ref[
-            pl.ds(c, blocks, stride=own), :
-        ] * (conv[:, c * LANES : (c + 1) * LANES] + skip_ref[c : c + 1, :] * gated[c])
+        mixed_ref[pl.ds(c, blocks, stride=own), :] = (
+            conv[:, c * LANES : (c + 1) * LANES] + skip_ref[c : c + 1, :] * gated[c]
+        )
     for q in range(local_blocks):
         if own % 8 == 0:
             column = jnp.concatenate(
@@ -371,13 +369,13 @@
                 ],
                 axis=0,
             )
-            out_ref[:, q * LANES : (q + 1) * LANES] = column.astype(BF16)
+            out_ref[:, q * LANES : (q + 1) * LANES] = column
         else:
             for c in range(own):
                 signal_ref[pl.ds(c, seq_devs, stride=own), :] = mixed_ref[
                     pl.ds(q * own + c, seq_devs, stride=part_rows), :
                 ]
-            out_ref[:, q * LANES : (q + 1) * LANES] = signal_ref[: seq_devs * own, :].astype(BF16)
+            out_ref[:, q * LANES : (q + 1) * LANES] = signal_ref[: seq_devs * own, :]
 
 
 def pack(parts, seq_devs, own):
@@ -385,10 +383,10 @@
     hbm = pl.BlockSpec(memory_space=pltpu.HBM)
     return pl.pallas_call(
         pack_kernel,
-        out_shape=pltpu.VMEM((seq_devs, 3, own, local_len), BF16),
-        in_specs=[hbm] * 3,
+        out_shape=pltpu.VMEM((seq_devs, 2, own, local_len), BF16),
+        in_specs=[hbm] * 2,
         out_specs=pl.BlockSpec(memory_space=pltpu.VMEM),
-        scratch_shapes=[pltpu.SemaphoreType.DMA((3,))],
+        scratch_shapes=[pltpu.SemaphoreType.DMA((2,))],
     )(*[in_space(part.reshape(seq_devs, own, local_len), pltpu.HBM) for part in parts])
 
 
@@ -432,11 +430,11 @@
     vmem = pl.BlockSpec(memory_space=pltpu.VMEM)
     return pl.pallas_call(
         functools.partial(mix_kernel, own),
-        out_shape=jax.ShapeDtypeStruct((seq_devs * own, local_len), BF16),
+        out_shape=jax.ShapeDtypeStruct((seq_devs * own, local_len), F32),
         in_specs=[vmem] * (1 + len(shared)),
         out_specs=vmem,
         scratch_shapes=[pltpu.VMEM((rows + own, LANES), F32)]
-        + [pltpu.VMEM((rows, LANES), F32)] * 3,
+        + [pltpu.VMEM((rows, LANES), F32)] * 2,
         compiler_params=pltpu.CompilerParams(vmem_limit_bytes=48 * 2**20),
     )(parts, *[in_space(vals, pltpu.VMEM) for vals in shared])
 
@@ -459,7 +457,7 @@
     seq_devs = lax.axis_size("seq")
     own = -(-channels // seq_devs)
     spare = own * seq_devs - channels
-    parts = [signal, in_gate, out_gate]
+    parts = [signal, in_gate]
     if spare:
         parts = [jnp.pad(part, ((0, spare), (0, 0))) for part in parts]
         short_taps = jnp.pad(short_taps, ((0, spare), (0, 0)))
@@ -481,7 +479,8 @@
     )
     shared = make_filter(params, own, seq_devs * local_len)
     mixed = mix(parts, shared)
-    return lax.all_to_all(mixed, "seq", split_axis=0, concat_axis=0, tiled=True)[:channels]
+    mixed = lax.all_to_all(mixed, "seq", split_axis=0, concat_axis=0, tiled=True)[:channels]
+    return (out_gate.astype(F32) * mixed).astype(BF16)
 
 
 def solution(mesh):

time: 36.4 us -> 34.9 us (0.959)
  waiting for transfers between devices: 6.47 us -> 3.69 us
  blocking collectives: 11.2 us -> 12.6 us
  other arithmetic: 0 us -> 0.68 us
  local copies, waits for them, and re-layouts: 0.66 us -> 0.01 us
    all_to_all x1, waiting for transfers between devices: 6.47 us -> 3.69 us  [on_device(): lax.all_to_all(parts, 'seq', split_axis=0, concat_axis=0, tiled=True)]
    all_to_all x1, blocking collectives: 11.2 us -> 12.6 us  [on_device(): lax.all_to_all(mixed, 'seq', split_axis=0, concat_axis=0, tiled=True)]
    convert_element_type x0 -> x1, other arithmetic: none -> 0.68 us  [on_device(): return (out_gate.astype(F32) * mixed).astype(BF16)]
    unnamed x1 -> x2, local copies, waits for them, and re-layouts: 0.66 us -> 0.01 us
  transfers between devices with their start and end apart: 1 -> 1, of which waited for: 1 -> 1; matrix products, arithmetic and copies ran while one was open for 0% -> 0% of each run, Pallas kernels for 17% -> 18%
where the time goes in v4:
time: 34.9 us; the launch traced here: 34.6 us
  blocking collectives  12.6 us (36%)
  Pallas kernels  9.34 us (27%)
  starting transfers between devices  8.32 us (24%)
  waiting for transfers between devices  3.69 us (11%)
  other arithmetic  0.68 us (2%)
    all_to_all x1, blocking collectives, on_device(): lax.all_to_all(mixed, 'seq', split_axis=0, concat_axis=0, tiled=True)  12.6 us
    all_to_all x1, starting transfers between devices, on_device(): lax.all_to_all(parts, 'seq', split_axis=0, concat_axis=0, tiled=True)  8.32 us
    pallas_call x1, Pallas kernels, make_filter(): pl.pallas_call(functools.partial(filter_kernel, own), out_shape=(pltpu.VM...  6.16 us
    all_to_all x1, waiting for transfers between devices, on_device(): lax.all_to_all(parts, 'seq', split_axis=0, concat_axis=0, tiled=True)  3.69 us
    pallas_call x1, Pallas kernels, pack(): pl.pallas_call(pack_kernel, out_shape=pltpu.VMEM((seq_devs, 2, own, local...  1.67 us
    pallas_call x1, Pallas kernels, mix(): pl.pallas_call(functools.partial(mix_kernel, own), out_shape=jax.ShapeDty...  1.51 us
  transfers between devices with their start and end apart: 1, of which 1 were waited for; matrix products, arithmetic and copies ran while one was open for 0% of the time, Pallas kernels for 18%

profile of v4, /device:TPU:0, one launch (start us, length us, event | category | flops | bytes accessed | tf_op | source)
XLA Modules:
  0.0 34.6 jit_solution(283389416054845974)
XLA Ops:
  0.0 1.7 %shard_map.172 = bf16[16,2,8,512]{3,2,1,0:T(8,128)(2,1)} custom-call(bf16[16,8,512]{2,1,0:T(8,128)(2,1)} %bitcast.13, bf16[16,8,512]{2,1,0:T(8,128)(2,1)} %bitcast.14), custom_call_target="tpu_custom_call" | custom-call | tf_op jit(solution)/shard_map/pallas_call | solution.py:384
  1.7 8.3 %all-to-all-start = ((bf16[16,2,8,512]{3,2,1,0:T(8,128)(2,1)}), bf16[16,2,8,512]{3,2,1,0:T(8,128)(2,1)S(1)}, u32[]{:S(2)}, u32[]{:S(2)}) async-start(bf16[16,2,8,512]{3,2,1,0:T(8,128)(2,1)} %shard_map.172), calls=%async_computation | async-start | bytes 524288 | tf_op jit(solution)/shard_map/all_to_all | solution.py:468
  10.0 6.2 %shard_map.173 = (f32[512,256]{1,0:T(8,128)S(1)}, bf16[8,256,256]{2,1,0:T(8,128)(2,1)S(1)}, f32[8,128]{1,0:T(8,128)S(1)}, bf16[128,192]{1,0:T(8,128)(2,1)S(1)}, ...) custom-call(bf16[128,8192]{1,0:T(8,128)(2,1)} %constant.12.clone.emb, ...), custom_call_target="tpu_custom_call" | custom-call | tf_op jit(solution)/shard_map/pallas_call | solution.py:401
  16.2 0.0 copy-start
  16.2 3.7 %all-to-all-done.parts_ref = bf16[16,2,8,512]{3,2,1,0:T(8,128)(2,1)S(1)} async-done(((bf16[16,2,8,512]{3,2,1,0:T(8,128)(2,1)}), bf16[16,2,8,512]{3,2,1,0:T(8,128)(2,1)S(1)}, u32[]{:S(2)}, u32[]{:S(2)}) %all-to-all-start) | async-done | bytes 262176 | tf_op jit(solution)/shard_map/all_to_all | solution.py:468
  19.9 1.5 %shard_map.174 = f32[128,512]{1,0:T(8,128)S(1)} custom-call(bf16[16,2,8,512]{3,2,1,0:T(8,128)(2,1)S(1)} %all-to-all-done.parts_ref, f32[512,256]{1,0:T(8,128)S(1)} %get-tuple-element.13.spectrum_ref, bf16[8,256,256]{2,1,0:T(8,128)(2,1)S(1)} %get-tuple-element.14.toeplitz_ref, f32[8,128]{1,0:T(8,128)S(1)} %get-tuple-element.15.skip_ref, ...), custom_call_target="tpu_custom_call" | custom-call | tf_op jit(solution)/shard_map/pallas_call | solution.py:431
  21.4 12.6 %all_to_all.17 = f32[16,8,512]{2,1,0:T(8,128)S(1)} all-to-all(f32[16,8,512]{2,1,0:T(8,128)S(1)} %bitcast.12), channel_id=1, replica_groups=mesh['seq'=16,'ch'=2] {'seq'}, dimensions={0} | all-to-all | bytes 524288 | tf_op jit(solution)/shard_map/all_to_all | solution.py:482
  34.0 0.0 copy-done
  34.0 0.7 %fusion = bf16[128,512]{1,0:T(8,128)(2,1)} fusion(f32[16,8,512]{2,1,0:T(8,128)S(1)} %all_to_all.17, bf16[128,512]{1,0:T(8,128)(2,1)S(1)} %copy-done), kind=kLoop, calls=%fused_computation.1 | loop fusion | flops 196608 | bytes 524288 | tf_op jit(solution)/shard_map/convert_element_type | solution.py:483
Async XLA Ops:
  1.7 18.2 %all-to-all-start = ((bf16[16,2,8,512]{3,2,1,0:T(8,128)(2,1)}), bf16[16,2,8,512]{3,2,1,0:T(8,128)(2,1)S(1)}, u32[]{:S(2)}, u32[]{:S(2)}) async-start(bf16[16,2,8,512]{3,2,1,0:T(8,128)(2,1)} %shard_map.172), calls=%async_computation | async-start | bytes 524288 | tf_op jit(solution)/shard_map/all_to_all | solution.py:468
  16.2 17.8 %copy-start = (bf16[128,512]{1,0:T(8,128)(2,1)S(1)}, bf16[128,512]{1,0:T(8,128)(2,1)}, u32[]{:S(2)}) copy-start(bf16[128,512]{1,0:T(8,128)(2,1)} %param.20) | copy-start | bytes 393220

commit v5 on v4

--- a/solution.py
+++ b/solution.py
@@ -12,6 +12,8 @@
 BANDS = 16
 LANES = 128
 TILES = 4
+LEVEL_BITS = 6
+LEVELS = 2**LEVEL_BITS
 F32 = jnp.float32
 BF16 = jnp.bfloat16
 in_space = pltpu.with_memory_space_constraint
@@ -143,6 +145,44 @@
             )
         )
     return matmul(outer_back_ref[...], stack_three(jnp.concatenate(columns, axis=1)))
+
+
+def step_of(high):
+    size = jnp.abs(high)
+    return jnp.maximum(lax.reduce_precision(size * (1.0 + 0.75 / 128), 8, 7) - size, 1e-30)
+
+
+def rest_level(vals, high):
+    level = jnp.floor(((vals - high) / step_of(high) + 0.5) * LEVELS)
+    return jnp.clip(level, 0.0, LEVELS - 1.0).astype(jnp.int32)
+
+
+def pair_code(one, two):
+    index = one * LEVELS + two
+    size = jnp.left_shift(128 + (index & 127), (index >> 7) & 15).astype(F32)
+    return jnp.where(index >= 2048, -size, size)
+
+
+def pair_levels(code):
+    size = jnp.abs(code).astype(jnp.int32)
+    index = jnp.where(code < 0, 2048, 0)
+    for shift in (8, 4, 2, 1):
+        more = size >= (128 << shift)
+        size = jnp.where(more, size >> shift, size)
+        index = jnp.where(more, index + shift * 128, index)
+    index = index + size - 128
+    return index >> LEVEL_BITS, index & (LEVELS - 1)
+
+
+def gate(coded, out_gate):
+    local_len = out_gate.shape[1]
+    half = local_len // 2
+    parts = []
+    for start, level in zip((0, half), pair_levels(coded[:, local_len:].astype(F32))):
+        high = coded[:, start : start + half].astype(F32)
+        vals = high + step_of(high) * ((level.astype(F32) + 0.5) * (1.0 / LEVELS) - 0.5)
+        parts.append((out_gate[:, start : start + half].astype(F32) * vals).astype(BF16))
+    return jnp.concatenate(parts, axis=1)
 
 
 def pack_kernel(signal_ref, in_gate_ref, parts_ref, sems):
@@ -360,6 +400,7 @@
         mixed_ref[pl.ds(c, blocks, stride=own), :] = (
             conv[:, c * LANES : (c + 1) * LANES] + skip_ref[c : c + 1, :] * gated[c]
         )
+    columns = []
     for q in range(local_blocks):
         if own % 8 == 0:
             column = jnp.concatenate(
@@ -369,13 +410,18 @@
                 ],
                 axis=0,
             )
-            out_ref[:, q * LANES : (q + 1) * LANES] = column
         else:
             for c in range(own):
                 signal_ref[pl.ds(c, seq_devs, stride=own), :] = mixed_ref[
                     pl.ds(q * own + c, seq_devs, stride=part_rows), :
                 ]
-            out_ref[:, q * LANES : (q + 1) * LANES] = signal_ref[: seq_devs * own, :]
+            column = signal_ref[: seq_devs * own, :]
+        high = column.astype(BF16)
+        out_ref[:, q * LANES : (q + 1) * LANES] = high
+        columns.append(rest_level(column, high.astype(F32)))
+    for q in range(local_blocks // 2):
+        code = pair_code(columns[q], columns[q + local_blocks // 2]).astype(BF16)
+        out_ref[:, local_len + q * LANES : local_len + (q + 1) * LANES] = code
 
 
 def pack(parts, seq_devs, own):
@@ -430,7 +476,7 @@
     vmem = pl.BlockSpec(memory_space=pltpu.VMEM)
     return pl.pallas_call(
         functools.partial(mix_kernel, own),
-        out_shape=jax.ShapeDtypeStruct((seq_devs * own, local_len), F32),
+        out_shape=jax.ShapeDtypeStruct((seq_devs * own, local_len * 3 // 2), BF16),
         in_specs=[vmem] * (1 + len(shared)),
         out_specs=vmem,
         scratch_shapes=[pltpu.VMEM((rows + own, LANES), F32)]
@@ -479,8 +525,8 @@
     )
     shared = make_filter(params, own, seq_devs * local_len)
     mixed = mix(parts, shared)
-    mixed = lax.all_to_all(mixed, "seq", split_axis=0, concat_axis=0, tiled=True)[:channels]
-    return (out_gate.astype(F32) * mixed).astype(BF16)
+    coded = lax.all_to_all(mixed, "seq", split_axis=0, concat_axis=0, tiled=True)[:channels]
+    return gate(coded, out_gate)
 
 
 def solution(mesh):

time: 34.9 us -> 34.3 us (0.983)
  blocking collectives: 12.6 us -> 11.4 us
    all_to_all x1, blocking collectives: 12.6 us -> 11.4 us  [on_device(): lax.all_to_all(mixed, 'seq', split_axis=0, concat_axis=0, tiled=True)]
    concatenate x0 -> x1, other arithmetic: none -> 0.67 us  [gate(): return jnp.concatenate(parts, axis=1)]
    convert_element_type x1, other arithmetic: 0.68 us -> 0.26 us  [gate(): (out_gate[:, start:start + half].astype(F32) * vals).astype(BF16)]
where the time goes in v5:
time: 34.3 us; the launch traced here: 34 us
  blocking collectives  11.4 us (33%)
  Pallas kernels  9.58 us (28%)
  starting transfers between devices  8.32 us (24%)
  waiting for transfers between devices  3.69 us (11%)
  other arithmetic  0.93 us (3%)
    all_to_all x1, blocking collectives, on_device(): lax.all_to_all(mixed, 'seq', split_axis=0, concat_axis=0, tiled=True)  11.4 us
    all_to_all x1, starting transfers between devices, on_device(): lax.all_to_all(parts, 'seq', split_axis=0, concat_axis=0, tiled=True)  8.32 us
    pallas_call x1, Pallas kernels, make_filter(): pl.pallas_call(functools.partial(filter_kernel, own), out_shape=(pltpu.VM...  6.16 us
    all_to_all x1, waiting for transfers between devices, on_device(): lax.all_to_all(parts, 'seq', split_axis=0, concat_axis=0, tiled=True)  3.69 us
    pallas_call x1, Pallas kernels, mix(): pl.pallas_call(functools.partial(mix_kernel, own), out_shape=jax.ShapeDty...  1.75 us
    pallas_call x1, Pallas kernels, pack(): pl.pallas_call(pack_kernel, out_shape=pltpu.VMEM((seq_devs, 2, own, local...  1.67 us
  transfers between devices with their start and end apart: 1, of which 1 were waited for; matrix products, arithmetic and copies ran while one was open for 0% of the time, Pallas kernels for 18%

profile of v5, /device:TPU:0, one launch (start us, length us, event | category | flops | bytes accessed | tf_op | source)
XLA Modules:
  0.0 34.0 jit_solution(12134424701913006410)
XLA Ops:
  0.0 1.7 %shard_map.172 = bf16[16,2,8,512]{3,2,1,0:T(8,128)(2,1)} custom-call(bf16[16,8,512]{2,1,0:T(8,128)(2,1)} %bitcast.11, bf16[16,8,512]{2,1,0:T(8,128)(2,1)} %bitcast.12), custom_call_target="tpu_custom_call" | custom-call | tf_op jit(solution)/shard_map/pallas_call | solution.py:430
  1.7 8.3 %all-to-all-start = ((bf16[16,2,8,512]{3,2,1,0:T(8,128)(2,1)}), bf16[16,2,8,512]{3,2,1,0:T(8,128)(2,1)S(1)}, u32[]{:S(2)}, u32[]{:S(2)}) async-start(bf16[16,2,8,512]{3,2,1,0:T(8,128)(2,1)} %shard_map.172), calls=%async_computation | async-start | bytes 524288 | tf_op jit(solution)/shard_map/all_to_all | solution.py:514
  10.0 6.2 %shard_map.173 = (f32[512,256]{1,0:T(8,128)S(1)}, bf16[8,256,256]{2,1,0:T(8,128)(2,1)S(1)}, f32[8,128]{1,0:T(8,128)S(1)}, bf16[128,192]{1,0:T(8,128)(2,1)S(1)}, ...) custom-call(bf16[128,8192]{1,0:T(8,128)(2,1)} %constant.54.clone.emb, ...), custom_call_target="tpu_custom_call" | custom-call | tf_op jit(solution)/shard_map/pallas_call | solution.py:447
  16.2 0.0 copy-start
  16.2 3.7 %all-to-all-done.parts_ref = bf16[16,2,8,512]{3,2,1,0:T(8,128)(2,1)S(1)} async-done(((bf16[16,2,8,512]{3,2,1,0:T(8,128)(2,1)}), bf16[16,2,8,512]{3,2,1,0:T(8,128)(2,1)S(1)}, u32[]{:S(2)}, u32[]{:S(2)}) %all-to-all-start) | async-done | bytes 262176 | tf_op jit(solution)/shard_map/all_to_all | solution.py:514
  19.9 1.7 %shard_map.174 = bf16[128,768]{1,0:T(8,128)(2,1)S(1)} custom-call(bf16[16,2,8,512]{3,2,1,0:T(8,128)(2,1)S(1)} %all-to-all-done.parts_ref, f32[512,256]{1,0:T(8,128)S(1)} %get-tuple-element.13.spectrum_ref, bf16[8,256,256]{2,1,0:T(8,128)(2,1)S(1)} %get-tuple-element.14.toeplitz_ref, f32[8,128]{1,0:T(8,128)S(1)} %get-tuple-element.15.skip_ref, ...), custom_call_target="tpu_custom_call" | custom-call | tf_op jit(solution)/shard_map/pallas_call | solution.py:477
  21.6 11.4 %all_to_all.17 = bf16[16,8,768]{2,1,0:T(8,128)(2,1)S(1)} all-to-all(bf16[16,8,768]{2,1,0:T(8,128)(2,1)S(1)} %bitcast.9), channel_id=1, replica_groups=mesh['seq'=16,'ch'=2] {'seq'}, dimensions={0} | all-to-all | bytes 393216 | tf_op jit(solution)/shard_map/all_to_all | solution.py:528
  33.1 0.0 copy-done
  33.1 0.3 fusion.11
  33.3 0.7 %pad_maximum_fusion = bf16[128,512]{1,0:T(8,128)(2,1)} fusion(bf16[128,256]{1,0:T(8,128)(2,1)S(1)} %get-tuple-element.22, bf16[128,256]{1,0:T(8,128)(2,1)S(1)} %get-tuple-element.21), kind=kLoop, calls=%fused_computation.30 | loop fusion | flops 262144 | bytes 262144 | tf_op jit(solution)/shard_map/concatenate | solution.py:185
Async XLA Ops:
  1.7 18.2 %all-to-all-start = ((bf16[16,2,8,512]{3,2,1,0:T(8,128)(2,1)}), bf16[16,2,8,512]{3,2,1,0:T(8,128)(2,1)S(1)}, u32[]{:S(2)}, u32[]{:S(2)}) async-start(bf16[16,2,8,512]{3,2,1,0:T(8,128)(2,1)} %shard_map.172), calls=%async_computation | async-start | bytes 524288 | tf_op jit(solution)/shard_map/all_to_all | solution.py:514
  16.2 16.9 %copy-start = (bf16[128,512]{1,0:T(8,128)(2,1)S(1)}, bf16[128,512]{1,0:T(8,128)(2,1)}, u32[]{:S(2)}) copy-start(bf16[128,512]{1,0:T(8,128)(2,1)} %param.20) | copy-start | bytes 393220

commit v6 on v5

--- a/solution.py
+++ b/solution.py
@@ -11,6 +11,7 @@
 
 BANDS = 16
 LANES = 128
+GROUPS = 4
 TILES = 4
 LEVEL_BITS = 6
 LEVELS = 2**LEVEL_BITS
@@ -115,7 +116,7 @@
     )
 
 
-def forward(columns, outer_ref, twiddle_ref, inner_ref):
+def outer_forward(columns, outer_ref, twiddle_ref):
     blocks = columns[0].shape[0]
     mixed = matmul(outer_ref[...], stack_three(jnp.concatenate(columns, axis=1)))
     cos_vals, sin_vals = twiddle_ref[0], twiddle_ref[1]
@@ -128,11 +129,10 @@
                 [real * cos_vals + imag * sin_vals, imag * cos_vals - real * sin_vals], axis=1
             )
         )
-    return inner_product(jnp.concatenate(rows, axis=0), inner_ref)
-
-
-def backward(spectrum, channels, inner_back_ref, twiddle_ref, outer_back_ref):
-    vals = inner_product(spectrum, inner_back_ref)
+    return rows
+
+
+def outer_backward(vals, channels, twiddle_ref, outer_back_ref):
     blocks = vals.shape[0] // channels
     cos_vals, sin_vals = twiddle_ref[0], twiddle_ref[1]
     columns = []
@@ -178,22 +178,12 @@
     local_len = out_gate.shape[1]
     half = local_len // 2
     parts = []
-    for start, level in zip((0, half), pair_levels(coded[:, local_len:].astype(F32))):
+    code = coded[:, local_len:].astype(F32)
+    for start, level in zip((0, half), pair_levels(code)):
         high = coded[:, start : start + half].astype(F32)
         vals = high + step_of(high) * ((level.astype(F32) + 0.5) * (1.0 / LEVELS) - 0.5)
         parts.append((out_gate[:, start : start + half].astype(F32) * vals).astype(BF16))
     return jnp.concatenate(parts, axis=1)
-
-
-def pack_kernel(signal_ref, in_gate_ref, parts_ref, sems):
-    copies = [
-        pltpu.make_async_copy(ref, parts_ref.at[:, i], sems.at[i])
-        for i, ref in enumerate((signal_ref, in_gate_ref))
-    ]
-    for copy in copies:
-        copy.start()
-    for copy in copies:
-        copy.wait()
 
 
 def filter_kernel(
@@ -332,7 +322,9 @@
         copy.wait()
     blocks = full_len // LANES
     columns = [filter_ref[pl.ds(c, blocks, stride=own), :] for c in range(own)]
-    spectrum_ref[...] = forward(columns, outer_ref, twiddle_ref, inner_ref)
+    spectrum_ref[...] = inner_product(
+        jnp.concatenate(outer_forward(columns, outer_ref, twiddle_ref), axis=0), inner_ref
+    )
     taps = taps_ref[own_rows, :]
     tap_count = taps.shape[1]
     square = (tap_count, tap_count)
@@ -389,13 +381,19 @@
         gated.append(
             in_gate_ref[pl.ds(c, blocks, stride=own), :] * (both[:, :LANES] + both[:, LANES:])
         )
-    vals = forward(gated, outer_ref, twiddle_ref, inner_ref)
-    real, imag = vals[:, :LANES], vals[:, LANES:]
-    filt_real, filt_imag = spectrum_ref[:, :LANES], spectrum_ref[:, LANES:]
-    product = jnp.concatenate(
-        [real * filt_real - imag * filt_imag, real * filt_imag + imag * filt_real], axis=1
-    )
-    conv = backward(product, own, inner_back_ref, twiddle_ref, outer_back_ref)
+    mid = outer_forward(gated, outer_ref, twiddle_ref)
+    step = max(1, own // GROUPS)
+    backs = []
+    for start in range(0, own, step):
+        rows = slice(start * blocks, (start + step) * blocks)
+        vals = inner_product(jnp.concatenate(mid[start : start + step], axis=0), inner_ref)
+        real, imag = vals[:, :LANES], vals[:, LANES:]
+        filt_real, filt_imag = spectrum_ref[rows, :LANES], spectrum_ref[rows, LANES:]
+        product = jnp.concatenate(
+            [real * filt_real - imag * filt_imag, real * filt_imag + imag * filt_real], axis=1
+        )
+        backs.append(inner_product(product, inner_back_ref))
+    conv = outer_backward(jnp.concatenate(backs, axis=0), own, twiddle_ref, outer_back_ref)
     for c in range(own):
         mixed_ref[pl.ds(c, blocks, stride=own), :] = (
             conv[:, c * LANES : (c + 1) * LANES] + skip_ref[c : c + 1, :] * gated[c]
@@ -422,18 +420,6 @@
     for q in range(local_blocks // 2):
         code = pair_code(columns[q], columns[q + local_blocks // 2]).astype(BF16)
         out_ref[:, local_len + q * LANES : local_len + (q + 1) * LANES] = code
-
-
-def pack(parts, seq_devs, own):
-    local_len = parts[0].shape[1]
-    hbm = pl.BlockSpec(memory_space=pltpu.HBM)
-    return pl.pallas_call(
-        pack_kernel,
-        out_shape=pltpu.VMEM((seq_devs, 2, own, local_len), BF16),
-        in_specs=[hbm] * 2,
-        out_specs=pl.BlockSpec(memory_space=pltpu.VMEM),
-        scratch_shapes=[pltpu.SemaphoreType.DMA((2,))],
-    )(*[in_space(part.reshape(seq_devs, own, local_len), pltpu.HBM) for part in parts])
 
 
 def make_filter(params, own, full_len):
@@ -510,7 +496,7 @@
         skip_gain = jnp.pad(skip_gain, (0, spare))
         decay_rate = jnp.pad(decay_rate, (0, spare), mode="edge")
         out_weight = jnp.pad(out_weight, ((0, 0), (0, spare)))
-    parts = pack(parts, seq_devs, own)
+    parts = jnp.stack([part.reshape(seq_devs, own, local_len) for part in parts], axis=1)
     parts = lax.all_to_all(parts, "seq", split_axis=0, concat_axis=0, tiled=True)
     params = (
         embed_weight,

time: 34.3 us -> 34.1 us (level)
  Pallas kernels: 9.58 us -> 7.73 us
  other arithmetic: 0.93 us -> 2.61 us
    another operation x0 -> x1, other arithmetic: none -> 1.68 us  [on_device(): jnp.stack([part.reshape(seq_devs, own, local_len) for part in parts], axi...]
    pallas_call x1 -> x0, Pallas kernels: 1.67 us -> none  [pack(): pl.pallas_call(pack_kernel, out_shape=pltpu.VMEM((seq_devs, 2, own, local...]
where the time goes in v6:
time: 34.1 us; the launch traced here: 33.8 us
  blocking collectives  11.4 us (33%)
  starting transfers between devices  8.31 us (24%)
  Pallas kernels  7.73 us (23%)
  waiting for transfers between devices  3.69 us (11%)
  other arithmetic  2.61 us (8%)
    all_to_all x1, blocking collectives, on_device(): lax.all_to_all(mixed, 'seq', split_axis=0, concat_axis=0, tiled=True)  11.4 us
    all_to_all x1, starting transfers between devices, on_device(): lax.all_to_all(parts, 'seq', split_axis=0, concat_axis=0, tiled=True)  8.31 us
    pallas_call x1, Pallas kernels, make_filter(): pl.pallas_call(functools.partial(filter_kernel, own), out_shape=(pltpu.VM...  6.16 us
    all_to_all x1, waiting for transfers between devices, on_device(): lax.all_to_all(parts, 'seq', split_axis=0, concat_axis=0, tiled=True)  3.69 us
    another operation x1, other arithmetic, on_device(): jnp.stack([part.reshape(seq_devs, own, local_len) for part in parts], axi...  1.68 us
    pallas_call x1, Pallas kernels, mix(): pl.pallas_call(functools.partial(mix_kernel, own), out_shape=jax.ShapeDty...  1.57 us
  transfers between devices with their start and end apart: 1, of which 1 were waited for; matrix products, arithmetic and copies ran while one was open for 0% of the time, Pallas kernels for 18%

profile of v6, /device:TPU:0, one launch (start us, length us, event | category | flops | bytes accessed | tf_op | source)
XLA Modules:
  0.0 33.8 jit_solution(7284349463407284133)
XLA Ops:
  0.0 1.7 %pad_maximum_fusion = bf16[16,2,8,512]{3,2,1,0:T(8,128)(2,1)} fusion(bf16[16,1,8,512]{3,2,1,0:T(8,128)(2,1)} %bitcast.11, bf16[16,1,8,512]{3,2,1,0:T(8,128)(2,1)} %bitcast.12), kind=kLoop, calls=%fused_computation | loop fusion | flops 131072 | bytes 524288 | tf_op jit(solution)/shard_map/stack | solution.py:499
  1.7 8.3 %all-to-all-start = ((bf16[16,2,8,512]{3,2,1,0:T(8,128)(2,1)}), bf16[16,2,8,512]{3,2,1,0:T(8,128)(2,1)S(1)}, u32[]{:S(2)}, u32[]{:S(2)}) async-start(bf16[16,2,8,512]{3,2,1,0:T(8,128)(2,1)} %pad_maximum_fusion), calls=%async_computation | async-start | bytes 524288 | tf_op jit(solution)/shard_map/all_to_all | solution.py:500
  10.0 6.2 %shard_map.172 = (f32[512,256]{1,0:T(8,128)S(1)}, bf16[8,256,256]{2,1,0:T(8,128)(2,1)S(1)}, f32[8,128]{1,0:T(8,128)S(1)}, bf16[128,192]{1,0:T(8,128)(2,1)S(1)}, ...) custom-call(bf16[128,8192]{1,0:T(8,128)(2,1)} %constant.54.clone.emb, ...), custom_call_target="tpu_custom_call" | custom-call | tf_op jit(solution)/shard_map/pallas_call | solution.py:433
  16.2 0.0 copy-start
  16.2 3.7 %all-to-all-done.parts_ref = bf16[16,2,8,512]{3,2,1,0:T(8,128)(2,1)S(1)} async-done(((bf16[16,2,8,512]{3,2,1,0:T(8,128)(2,1)}), bf16[16,2,8,512]{3,2,1,0:T(8,128)(2,1)S(1)}, u32[]{:S(2)}, u32[]{:S(2)}) %all-to-all-start) | async-done | bytes 262176 | tf_op jit(solution)/shard_map/all_to_all | solution.py:500
  19.9 1.6 %shard_map.173 = bf16[128,768]{1,0:T(8,128)(2,1)S(1)} custom-call(bf16[16,2,8,512]{3,2,1,0:T(8,128)(2,1)S(1)} %all-to-all-done.parts_ref, f32[512,256]{1,0:T(8,128)S(1)} %get-tuple-element.13.spectrum_ref, bf16[8,256,256]{2,1,0:T(8,128)(2,1)S(1)} %get-tuple-element.14.toeplitz_ref, f32[8,128]{1,0:T(8,128)S(1)} %get-tuple-element.15.skip_ref, ...), custom_call_target="tpu_custom_call" | custom-call | tf_op jit(solution)/shard_map/pallas_call | solution.py:463
  21.4 11.4 %all_to_all.17 = bf16[16,8,768]{2,1,0:T(8,128)(2,1)S(1)} all-to-all(bf16[16,8,768]{2,1,0:T(8,128)(2,1)S(1)} %bitcast.9), channel_id=1, replica_groups=mesh['seq'=16,'ch'=2] {'seq'}, dimensions={0} | all-to-all | bytes 393216 | tf_op jit(solution)/shard_map/all_to_all | solution.py:514
  32.9 0.0 copy-done
  32.9 0.3 fusion.11
  33.1 0.7 %pad_maximum_fusion.1 = bf16[128,512]{1,0:T(8,128)(2,1)} fusion(bf16[128,256]{1,0:T(8,128)(2,1)S(1)} %get-tuple-element.22, bf16[128,256]{1,0:T(8,128)(2,1)S(1)} %get-tuple-element.21), kind=kLoop, calls=%fused_computation.31 | loop fusion | flops 262144 | bytes 262144 | tf_op jit(solution)/shard_map/concatenate | solution.py:186
Async XLA Ops:
  1.7 18.2 %all-to-all-start = ((bf16[16,2,8,512]{3,2,1,0:T(8,128)(2,1)}), bf16[16,2,8,512]{3,2,1,0:T(8,128)(2,1)S(1)}, u32[]{:S(2)}, u32[]{:S(2)}) async-start(bf16[16,2,8,512]{3,2,1,0:T(8,128)(2,1)} %pad_maximum_fusion), calls=%async_computation | async-start | bytes 524288 | tf_op jit(solution)/shard_map/all_to_all | solution.py:500
  16.2 16.7 %copy-start = (bf16[128,512]{1,0:T(8,128)(2,1)S(1)}, bf16[128,512]{1,0:T(8,128)(2,1)}, u32[]{:S(2)}) copy-start(bf16[128,512]{1,0:T(8,128)(2,1)} %param.20) | copy-start | bytes 393220

commit v7 on v6

--- a/solution.py
+++ b/solution.py
@@ -13,8 +13,7 @@
 LANES = 128
 GROUPS = 4
 TILES = 4
-LEVEL_BITS = 6
-LEVELS = 2**LEVEL_BITS
+SPAN = 120.0
 F32 = jnp.float32
 BF16 = jnp.bfloat16
 in_space = pltpu.with_memory_space_constraint
@@ -147,43 +146,21 @@
     return matmul(outer_back_ref[...], stack_three(jnp.concatenate(columns, axis=1)))
 
 
-def step_of(high):
-    size = jnp.abs(high)
-    return jnp.maximum(lax.reduce_precision(size * (1.0 + 0.75 / 128), 8, 7) - size, 1e-30)
-
-
-def rest_level(vals, high):
-    level = jnp.floor(((vals - high) / step_of(high) + 0.5) * LEVELS)
-    return jnp.clip(level, 0.0, LEVELS - 1.0).astype(jnp.int32)
-
-
-def pair_code(one, two):
-    index = one * LEVELS + two
-    size = jnp.left_shift(128 + (index & 127), (index >> 7) & 15).astype(F32)
-    return jnp.where(index >= 2048, -size, size)
-
-
-def pair_levels(code):
-    size = jnp.abs(code).astype(jnp.int32)
-    index = jnp.where(code < 0, 2048, 0)
-    for shift in (8, 4, 2, 1):
-        more = size >= (128 << shift)
-        size = jnp.where(more, size >> shift, size)
-        index = jnp.where(more, index + shift * 128, index)
-    index = index + size - 128
-    return index >> LEVEL_BITS, index & (LEVELS - 1)
-
-
-def gate(coded, out_gate):
-    local_len = out_gate.shape[1]
-    half = local_len // 2
-    parts = []
-    code = coded[:, local_len:].astype(F32)
-    for start, level in zip((0, half), pair_levels(code)):
-        high = coded[:, start : start + half].astype(F32)
-        vals = high + step_of(high) * ((level.astype(F32) + 0.5) * (1.0 / LEVELS) - 0.5)
-        parts.append((out_gate[:, start : start + half].astype(F32) * vals).astype(BF16))
-    return jnp.concatenate(parts, axis=1)
+def code_group(columns):
+    top = functools.reduce(jnp.maximum, [jnp.abs(column) for column in columns])
+    scale = lax.reduce_precision(jnp.maximum(top, 1e-30) * (1.0 + 1.0 / 128), 8, 7)
+    factor = 2.0 * SPAN / scale
+    codes = []
+    for column in columns:
+        size = jnp.exp2(jnp.abs(column) * factor - SPAN)
+        codes.append(jnp.where(column < 0, -size, size).astype(BF16))
+    return codes, scale.astype(BF16)
+
+
+def decode_group(codes, scale):
+    codes = codes.astype(F32)
+    share = jnp.log(jnp.abs(codes)) * (0.5 / SPAN / math.log(2.0)) + 0.5
+    return jnp.where(codes < 0, -share, share) * scale.astype(F32)
 
 
 def filter_kernel(
@@ -414,12 +391,11 @@
                     pl.ds(q * own + c, seq_devs, stride=part_rows), :
                 ]
             column = signal_ref[: seq_devs * own, :]
-        high = column.astype(BF16)
-        out_ref[:, q * LANES : (q + 1) * LANES] = high
-        columns.append(rest_level(column, high.astype(F32)))
-    for q in range(local_blocks // 2):
-        code = pair_code(columns[q], columns[q + local_blocks // 2]).astype(BF16)
-        out_ref[:, local_len + q * LANES : local_len + (q + 1) * LANES] = code
+        columns.append(column)
+    codes, scale = code_group(columns)
+    for q in range(local_blocks):
+        out_ref[:, q * LANES : (q + 1) * LANES] = codes[q]
+    out_ref[:, local_len:] = scale
 
 
 def make_filter(params, own, full_len):
@@ -462,7 +438,7 @@
     vmem = pl.BlockSpec(memory_space=pltpu.VMEM)
     return pl.pallas_call(
         functools.partial(mix_kernel, own),
-        out_shape=jax.ShapeDtypeStruct((seq_devs * own, local_len * 3 // 2), BF16),
+        out_shape=jax.ShapeDtypeStruct((seq_devs * own, local_len + LANES), BF16),
         in_specs=[vmem] * (1 + len(shared)),
         out_specs=vmem,
         scratch_shapes=[pltpu.VMEM((rows + own, LANES), F32)]
@@ -512,7 +488,9 @@
     shared = make_filter(params, own, seq_devs * local_len)
     mixed = mix(parts, shared)
     coded = lax.all_to_all(mixed, "seq", split_axis=0, concat_axis=0, tiled=True)[:channels]
-    return gate(coded, out_gate)
+    scale = jnp.concatenate([coded[:, local_len:]] * (local_len // LANES), axis=1)
+    vals = decode_group(coded[:, :local_len], scale)
+    return (out_gate.astype(F32) * vals).astype(BF16)
 
 
 def solution(mesh):

time: 34.1 us -> 33.6 us (0.985)
    concatenate x1 -> x0, other arithmetic: 0.67 us -> none  [gate(): return jnp.concatenate(parts, axis=1)]
    convert_element_type x1, other arithmetic: 0.26 us -> 0.78 us  [on_device(): return (out_gate.astype(F32) * vals).astype(BF16)]
where the time goes in v7:
time: 33.6 us; the launch traced here: 33.4 us
  blocking collectives  11.3 us (34%)
  starting transfers between devices  8.31 us (25%)
  Pallas kernels  7.59 us (23%)
  waiting for transfers between devices  3.69 us (11%)
  other arithmetic  2.46 us (7%)
    all_to_all x1, blocking collectives, on_device(): lax.all_to_all(mixed, 'seq', split_axis=0, concat_axis=0, tiled=True)  11.3 us
    all_to_all x1, starting transfers between devices, on_device(): lax.all_to_all(parts, 'seq', split_axis=0, concat_axis=0, tiled=True)  8.31 us
    pallas_call x1, Pallas kernels, make_filter(): pl.pallas_call(functools.partial(filter_kernel, own), out_shape=(pltpu.VM...  6.16 us
    all_to_all x1, waiting for transfers between devices, on_device(): lax.all_to_all(parts, 'seq', split_axis=0, concat_axis=0, tiled=True)  3.69 us
    another operation x1, other arithmetic, on_device(): jnp.stack([part.reshape(seq_devs, own, local_len) for part in parts], axi...  1.68 us
    pallas_call x1, Pallas kernels, mix(): pl.pallas_call(functools.partial(mix_kernel, own), out_shape=jax.ShapeDty...  1.42 us
    convert_element_type x1, other arithmetic, on_device(): return (out_gate.astype(F32) * vals).astype(BF16)  0.78 us
  transfers between devices with their start and end apart: 1, of which 1 were waited for; matrix products, arithmetic and copies ran while one was open for 0% of the time, Pallas kernels for 18%

profile of v7, /device:TPU:0, one launch (start us, length us, event | category | flops | bytes accessed | tf_op | source)
XLA Modules:
  0.0 33.4 jit_solution(7733529384880821171)
XLA Ops:
  0.0 1.7 %pad_maximum_fusion = bf16[16,2,8,512]{3,2,1,0:T(8,128)(2,1)} fusion(bf16[16,1,8,512]{3,2,1,0:T(8,128)(2,1)} %bitcast.12, bf16[16,1,8,512]{3,2,1,0:T(8,128)(2,1)} %bitcast.13), kind=kLoop, calls=%fused_computation.9 | loop fusion | flops 131072 | bytes 524288 | tf_op jit(solution)/shard_map/stack | solution.py:475
  1.7 8.3 %all-to-all-start = ((bf16[16,2,8,512]{3,2,1,0:T(8,128)(2,1)}), bf16[16,2,8,512]{3,2,1,0:T(8,128)(2,1)S(1)}, u32[]{:S(2)}, u32[]{:S(2)}) async-start(bf16[16,2,8,512]{3,2,1,0:T(8,128)(2,1)} %pad_maximum_fusion), calls=%async_computation | async-start | bytes 524288 | tf_op jit(solution)/shard_map/all_to_all | solution.py:476
  10.0 6.2 %shard_map.172 = (f32[512,256]{1,0:T(8,128)S(1)}, bf16[8,256,256]{2,1,0:T(8,128)(2,1)S(1)}, f32[8,128]{1,0:T(8,128)S(1)}, bf16[128,192]{1,0:T(8,128)(2,1)S(1)}, ...) custom-call(bf16[128,8192]{1,0:T(8,128)(2,1)} %constant.18.clone.emb, ...), custom_call_target="tpu_custom_call" | custom-call | tf_op jit(solution)/shard_map/pallas_call | solution.py:409
  16.2 0.0 copy-start
  16.2 3.7 %all-to-all-done.parts_ref = bf16[16,2,8,512]{3,2,1,0:T(8,128)(2,1)S(1)} async-done(((bf16[16,2,8,512]{3,2,1,0:T(8,128)(2,1)}), bf16[16,2,8,512]{3,2,1,0:T(8,128)(2,1)S(1)}, u32[]{:S(2)}, u32[]{:S(2)}) %all-to-all-start) | async-done | bytes 262176 | tf_op jit(solution)/shard_map/all_to_all | solution.py:476
  19.9 1.4 %shard_map.173 = bf16[128,640]{1,0:T(8,128)(2,1)S(1)} custom-call(bf16[16,2,8,512]{3,2,1,0:T(8,128)(2,1)S(1)} %all-to-all-done.parts_ref, f32[512,256]{1,0:T(8,128)S(1)} %get-tuple-element.13.spectrum_ref, bf16[8,256,256]{2,1,0:T(8,128)(2,1)S(1)} %get-tuple-element.14.toeplitz_ref, f32[8,128]{1,0:T(8,128)S(1)} %get-tuple-element.15.skip_ref, ...), custom_call_target="tpu_custom_call" | custom-call | tf_op jit(solution)/shard_map/pallas_call | solution.py:439
  21.3 11.3 %all_to_all.17 = bf16[16,8,640]{2,1,0:T(8,128)(2,1)S(1)} all-to-all(bf16[16,8,640]{2,1,0:T(8,128)(2,1)S(1)} %bitcast.9), channel_id=1, replica_groups=mesh['seq'=16,'ch'=2] {'seq'}, dimensions={0} | all-to-all | bytes 327680 | tf_op jit(solution)/shard_map/all_to_all | solution.py:490
  32.6 0.0 copy-done
  32.6 0.8 %fusion.5 = bf16[128,512]{1,0:T(8,128)(2,1)} fusion(bf16[128,512]{1,0:T(8,128)(2,1)S(1)} %copy-done, bf16[128,640]{1,0:T(8,128)(2,1)S(1)} %bitcast.11, bf16[128,128]{1,0:T(8,128)(2,1)S(1)} %slice.9), kind=kLoop, calls=%fused_computation.8 | loop fusion | flops 1245184 | bytes 425984 | tf_op jit(solution)/shard_map/convert_element_type | solution.py:493
  (1 shorter events, 0.0 us)
Async XLA Ops:
  1.7 18.2 %all-to-all-start = ((bf16[16,2,8,512]{3,2,1,0:T(8,128)(2,1)}), bf16[16,2,8,512]{3,2,1,0:T(8,128)(2,1)S(1)}, u32[]{:S(2)}, u32[]{:S(2)}) async-start(bf16[16,2,8,512]{3,2,1,0:T(8,128)(2,1)} %pad_maximum_fusion), calls=%async_computation | async-start | bytes 524288 | tf_op jit(solution)/shard_map/all_to_all | solution.py:476
  16.2 16.4 %copy-start = (bf16[128,512]{1,0:T(8,128)(2,1)S(1)}, bf16[128,512]{1,0:T(8,128)(2,1)}, u32[]{:S(2)}) copy-start(bf16[128,512]{1,0:T(8,128)(2,1)} %param.20) | copy-start | bytes 393220

commit v8 on v7

--- a/solution.py
+++ b/solution.py
@@ -12,7 +12,7 @@
 BANDS = 16
 LANES = 128
 GROUPS = 4
-TILES = 4
+TILES = 2
 SPAN = 120.0
 F32 = jnp.float32
 BF16 = jnp.bfloat16
@@ -75,7 +75,7 @@
     return [float(v) for v in fit]
 
 
-SINE_FIT = sine_fit(7)
+SINE_FIT = sine_fit(6)
 
 
 def sine_of_turns(turns):
@@ -260,9 +260,7 @@
         axis=0,
     ).astype(BF16)
     one, two, _ = split_three(mid_weight_ref[...] * freq)
-    weight_two = jnp.concatenate(
-        [jnp.concatenate([one, one], axis=0).T, jnp.concatenate([two, two], axis=0).T], axis=0
-    ).astype(BF16)
+    weight_two = jnp.concatenate([one, one, two], axis=0).T.astype(BF16)
     vec_ref[0:1, :] = mid_bias_ref[...] * freq
     bias_two = vec_ref[...].T[:, 0:1]
     one, two, _ = split_three(out_weight_ref[...])
@@ -286,8 +284,7 @@
         first = sine_of_turns(
             turns[:hidden] + turns[hidden : 2 * hidden] + turns[2 * hidden :]
         )
-        turns = matmul(weight_two, jnp.concatenate(split_two(first), axis=0))
-        second = sine_of_turns(turns[:hidden] + turns[hidden:] + bias_two)
+        second = sine_of_turns(matmul(weight_two, stack_three(first)) + bias_two)
         raw = matmul(weight_three, jnp.concatenate(split_two(second), axis=0))
         positions = (start + lax.broadcasted_iota(jnp.int32, (own, tile_len), 1)).astype(F32)
         vals = (raw[:own] + raw[own:]) * (scale * jnp.exp(-decay * positions))
@@ -424,7 +421,7 @@
             pltpu.VMEM((8, channels), F32),
             pltpu.VMEM((channels, 8), F32),
             pltpu.VMEM((2, channels, 2 * hidden), F32),
-            pltpu.VMEM((blocks * own, LANES), F32),
+            pltpu.VMEM(((blocks + 1) * own, LANES), F32),
             pltpu.SemaphoreType.DMA((len(operands) - 1,)),
             pltpu.SemaphoreType.DMA((TILES,)),
         ],
@@ -441,8 +438,8 @@
         out_shape=jax.ShapeDtypeStruct((seq_devs * own, local_len + LANES), BF16),
         in_specs=[vmem] * (1 + len(shared)),
         out_specs=vmem,
-        scratch_shapes=[pltpu.VMEM((rows + own, LANES), F32)]
-        + [pltpu.VMEM((rows, LANES), F32)] * 2,
+        scratch_shapes=[pltpu.VMEM((rows + 2 * own, LANES), F32)]
+        + [pltpu.VMEM((rows + own, LANES), F32)] * 2,
         compiler_params=pltpu.CompilerParams(vmem_limit_bytes=48 * 2**20),
     )(parts, *[in_space(vals, pltpu.VMEM) for vals in shared])
 

time: 33.6 us -> 33.6 us (level)
  waiting for transfers between devices: 3.69 us -> 4.3 us
  Pallas kernels: 7.59 us -> 6.98 us
    all_to_all x1, waiting for transfers between devices: 3.69 us -> 4.3 us  [on_device(): lax.all_to_all(parts, 'seq', split_axis=0, concat_axis=0, tiled=True)]
    pallas_call x1, Pallas kernels: 6.16 us -> 5.55 us  [make_filter(): pl.pallas_call(functools.partial(filter_kernel, own), out_shape=(pltpu.VM...]
  transfers between devices with their start and end apart: 1 -> 1, of which waited for: 1 -> 1; matrix products, arithmetic and copies ran while one was open for 0% -> 0% of each run, Pallas kernels for 18% -> 17%
where the time goes in v8:
time: 33.6 us; the launch traced here: 33.4 us
  blocking collectives  11.3 us (34%)
  starting transfers between devices  8.31 us (25%)
  Pallas kernels  6.98 us (21%)
  waiting for transfers between devices  4.3 us (13%)
  other arithmetic  2.46 us (7%)
    all_to_all x1, blocking collectives, on_device(): lax.all_to_all(mixed, 'seq', split_axis=0, concat_axis=0, tiled=True)  11.3 us
    all_to_all x1, starting transfers between devices, on_device(): lax.all_to_all(parts, 'seq', split_axis=0, concat_axis=0, tiled=True)  8.31 us
    pallas_call x1, Pallas kernels, make_filter(): pl.pallas_call(functools.partial(filter_kernel, own), out_shape=(pltpu.VM...  5.55 us
    all_to_all x1, waiting for transfers between devices, on_device(): lax.all_to_all(parts, 'seq', split_axis=0, concat_axis=0, tiled=True)  4.3 us
    another operation x1, other arithmetic, on_device(): jnp.stack([part.reshape(seq_devs, own, local_len) for part in parts], axi...  1.68 us
    pallas_call x1, Pallas kernels, mix(): pl.pallas_call(functools.partial(mix_kernel, own), out_shape=jax.ShapeDty...  1.42 us
    convert_element_type x1, other arithmetic, on_device(): return (out_gate.astype(F32) * vals).astype(BF16)  0.78 us
  transfers between devices with their start and end apart: 1, of which 1 were waited for; matrix products, arithmetic and copies ran while one was open for 0% of the time, Pallas kernels for 17%

profile of v8, /device:TPU:0, one launch (start us, length us, event | category | flops | bytes accessed | tf_op | source)
XLA Modules:
  0.0 33.4 jit_solution(13963429628744074844)
XLA Ops:
  0.0 1.7 %pad_maximum_fusion = bf16[16,2,8,512]{3,2,1,0:T(8,128)(2,1)} fusion(bf16[16,1,8,512]{3,2,1,0:T(8,128)(2,1)} %bitcast.12, bf16[16,1,8,512]{3,2,1,0:T(8,128)(2,1)} %bitcast.13), kind=kLoop, calls=%fused_computation.9 | loop fusion | flops 131072 | bytes 524288 | tf_op jit(solution)/shard_map/stack | solution.py:472
  1.7 8.3 %all-to-all-start = ((bf16[16,2,8,512]{3,2,1,0:T(8,128)(2,1)}), bf16[16,2,8,512]{3,2,1,0:T(8,128)(2,1)S(1)}, u32[]{:S(2)}, u32[]{:S(2)}) async-start(bf16[16,2,8,512]{3,2,1,0:T(8,128)(2,1)} %pad_maximum_fusion), calls=%async_computation | async-start | bytes 524288 | tf_op jit(solution)/shard_map/all_to_all | solution.py:473
  10.0 5.6 %shard_map.172 = (f32[512,256]{1,0:T(8,128)S(1)}, bf16[8,256,256]{2,1,0:T(8,128)(2,1)S(1)}, f32[8,128]{1,0:T(8,128)S(1)}, bf16[128,192]{1,0:T(8,128)(2,1)S(1)}, ...) custom-call(bf16[128,8192]{1,0:T(8,128)(2,1)} %constant.18.clone.emb, ...), custom_call_target="tpu_custom_call" | custom-call | tf_op jit(solution)/shard_map/pallas_call | solution.py:406
  15.6 0.0 copy-start
  15.6 4.3 %all-to-all-done.parts_ref = bf16[16,2,8,512]{3,2,1,0:T(8,128)(2,1)S(1)} async-done(((bf16[16,2,8,512]{3,2,1,0:T(8,128)(2,1)}), bf16[16,2,8,512]{3,2,1,0:T(8,128)(2,1)S(1)}, u32[]{:S(2)}, u32[]{:S(2)}) %all-to-all-start) | async-done | bytes 262176 | tf_op jit(solution)/shard_map/all_to_all | solution.py:473
  19.9 1.4 %shard_map.173 = bf16[128,640]{1,0:T(8,128)(2,1)S(1)} custom-call(bf16[16,2,8,512]{3,2,1,0:T(8,128)(2,1)S(1)} %all-to-all-done.parts_ref, f32[512,256]{1,0:T(8,128)S(1)} %get-tuple-element.13.spectrum_ref, bf16[8,256,256]{2,1,0:T(8,128)(2,1)S(1)} %get-tuple-element.14.toeplitz_ref, f32[8,128]{1,0:T(8,128)S(1)} %get-tuple-element.15.skip_ref, ...), custom_call_target="tpu_custom_call" | custom-call | tf_op jit(solution)/shard_map/pallas_call | solution.py:436
  21.3 11.3 %all_to_all.17 = bf16[16,8,640]{2,1,0:T(8,128)(2,1)S(1)} all-to-all(bf16[16,8,640]{2,1,0:T(8,128)(2,1)S(1)} %bitcast.9), channel_id=1, replica_groups=mesh['seq'=16,'ch'=2] {'seq'}, dimensions={0} | all-to-all | bytes 327680 | tf_op jit(solution)/shard_map/all_to_all | solution.py:487
  32.6 0.0 copy-done
  32.6 0.8 %fusion.5 = bf16[128,512]{1,0:T(8,128)(2,1)} fusion(bf16[128,512]{1,0:T(8,128)(2,1)S(1)} %copy-done, bf16[128,640]{1,0:T(8,128)(2,1)S(1)} %bitcast.11, bf16[128,128]{1,0:T(8,128)(2,1)S(1)} %slice.9), kind=kLoop, calls=%fused_computation.8 | loop fusion | flops 1245184 | bytes 425984 | tf_op jit(solution)/shard_map/convert_element_type | solution.py:490
  (1 shorter events, 0.0 us)
Async XLA Ops:
  1.7 18.2 %all-to-all-start = ((bf16[16,2,8,512]{3,2,1,0:T(8,128)(2,1)}), bf16[16,2,8,512]{3,2,1,0:T(8,128)(2,1)S(1)}, u32[]{:S(2)}, u32[]{:S(2)}) async-start(bf16[16,2,8,512]{3,2,1,0:T(8,128)(2,1)} %pad_maximum_fusion), calls=%async_computation | async-start | bytes 524288 | tf_op jit(solution)/shard_map/all_to_all | solution.py:473
  15.6 17.0 %copy-start = (bf16[128,512]{1,0:T(8,128)(2,1)S(1)}, bf16[128,512]{1,0:T(8,128)(2,1)}, u32[]{:S(2)}) copy-start(bf16[128,512]{1,0:T(8,128)(2,1)} %param.20) | copy-start | bytes 393220

commit v9 on v8

--- a/solution.py
+++ b/solution.py
@@ -14,6 +14,7 @@
 GROUPS = 4
 TILES = 2
 SPAN = 120.0
+ORDER_SEED = 115
 F32 = jnp.float32
 BF16 = jnp.bfloat16
 in_space = pltpu.with_memory_space_constraint
@@ -161,6 +162,16 @@
     codes = codes.astype(F32)
     share = jnp.log(jnp.abs(codes)) * (0.5 / SPAN / math.log(2.0)) + 0.5
     return jnp.where(codes < 0, -share, share) * scale.astype(F32)
+
+
+def exchange_order(count):
+    return [int(place) for place in np.random.RandomState(ORDER_SEED).permutation(count)]
+
+
+def exchange(chunks, order):
+    return lax.all_to_all(
+        chunks, "seq", split_axis=0, concat_axis=0, tiled=True, axis_index_groups=[order]
+    )
 
 
 def filter_kernel(
@@ -237,7 +248,11 @@
         )
     for copy in copies[:8] + embed_copies + copies[8:]:
         copy.start()
-    first_channel = pl.multiple_of(lax.axis_index("seq") * own, own)
+    seq_index = lax.axis_index("seq")
+    first_channel = 0
+    for place, device in enumerate(exchange_order(lax.axis_size("seq"))):
+        first_channel = jnp.where(seq_index == device, place * own, first_channel)
+    first_channel = pl.multiple_of(first_channel, own)
     pad_ref[...] = jnp.zeros_like(pad_ref)
     vec_ref[...] = jnp.zeros_like(vec_ref)
     row_ref[...] = jnp.zeros_like(row_ref)
@@ -336,12 +351,13 @@
     part_rows = local_blocks * own
     blocks = seq_devs * local_blocks
     signal_ref[:own, :] = jnp.zeros((own, LANES), F32)
-    for p in range(seq_devs):
+    order = exchange_order(seq_devs)
+    for place, p in enumerate(order):
         for q in range(local_blocks):
             at = p * part_rows + q * own
             lanes = slice(q * LANES, (q + 1) * LANES)
-            signal_ref[own + at : 2 * own + at, :] = parts_ref[p, 0, :, lanes].astype(F32)
-            in_gate_ref[at : at + own, :] = parts_ref[p, 1, :, lanes].astype(F32)
+            signal_ref[own + at : 2 * own + at, :] = parts_ref[place, 0, :, lanes].astype(F32)
+            in_gate_ref[at : at + own, :] = parts_ref[place, 1, :, lanes].astype(F32)
     gated = []
     for c in range(own):
         window = jnp.concatenate(
@@ -378,15 +394,14 @@
             column = jnp.concatenate(
                 [
                     mixed_ref[p * part_rows + q * own : p * part_rows + (q + 1) * own, :]
-                    for p in range(seq_devs)
+                    for p in order
                 ],
                 axis=0,
             )
         else:
-            for c in range(own):
-                signal_ref[pl.ds(c, seq_devs, stride=own), :] = mixed_ref[
-                    pl.ds(q * own + c, seq_devs, stride=part_rows), :
-                ]
+            for place, p in enumerate(order):
+                at = p * part_rows + q * own
+                signal_ref[place * own : (place + 1) * own, :] = mixed_ref[at : at + own, :]
             column = signal_ref[: seq_devs * own, :]
         columns.append(column)
     codes, scale = code_group(columns)
@@ -470,7 +485,8 @@
         decay_rate = jnp.pad(decay_rate, (0, spare), mode="edge")
         out_weight = jnp.pad(out_weight, ((0, 0), (0, spare)))
     parts = jnp.stack([part.reshape(seq_devs, own, local_len) for part in parts], axis=1)
-    parts = lax.all_to_all(parts, "seq", split_axis=0, concat_axis=0, tiled=True)
+    order = exchange_order(seq_devs)
+    parts = exchange(parts, order)
     params = (
         embed_weight,
         embed_bias[None, :],
@@ -484,7 +500,9 @@
     )
     shared = make_filter(params, own, seq_devs * local_len)
     mixed = mix(parts, shared)
-    coded = lax.all_to_all(mixed, "seq", split_axis=0, concat_axis=0, tiled=True)[:channels]
+    coded = exchange(mixed.reshape(seq_devs, own, -1), order).reshape(
+        seq_devs * own, -1
+    )[:channels]
     scale = jnp.concatenate([coded[:, local_len:]] * (local_len // LANES), axis=1)
     vals = decode_group(coded[:, :local_len], scale)
     return (out_gate.astype(F32) * vals).astype(BF16)

time: 33.6 us -> 30.3 us (0.902)
  waiting for transfers between devices: 4.3 us -> 0.98 us
  starting transfers between devices: 8.31 us -> 9.33 us
  blocking collectives: 11.3 us -> 10.3 us
    all_to_all x1, waiting for transfers between devices: 4.3 us -> 0.98 us  [exchange(): lax.all_to_all(chunks, 'seq', split_axis=0, concat_axis=0, tiled=True, ax...]
    all_to_all x1, starting transfers between devices: 8.31 us -> 9.33 us  [exchange(): lax.all_to_all(chunks, 'seq', split_axis=0, concat_axis=0, tiled=True, ax...]
    all_to_all x1, blocking collectives: 11.3 us -> 10.3 us  [exchange(): lax.all_to_all(chunks, 'seq', split_axis=0, concat_axis=0, tiled=True, ax...]
  transfers between devices with their start and end apart: 1 -> 1, of which waited for: 1 -> 1; matrix products, arithmetic and copies ran while one was open for 0% -> 0% of each run, Pallas kernels for 17% -> 18%
where the time goes in v9:
time: 30.3 us; the launch traced here: 30.1 us
  blocking collectives  10.3 us (34%)
  starting transfers between devices  9.33 us (31%)
  Pallas kernels  6.96 us (23%)
  other arithmetic  2.46 us (8%)
  waiting for transfers between devices  0.98 us (3%)
    all_to_all x1, blocking collectives, exchange(): lax.all_to_all(chunks, 'seq', split_axis=0, concat_axis=0, tiled=True, ax...  10.3 us
    all_to_all x1, starting transfers between devices, exchange(): lax.all_to_all(chunks, 'seq', split_axis=0, concat_axis=0, tiled=True, ax...  9.33 us
    pallas_call x1, Pallas kernels, make_filter(): pl.pallas_call(functools.partial(filter_kernel, own), out_shape=(pltpu.VM...  5.54 us
    another operation x1, other arithmetic, on_device(): jnp.stack([part.reshape(seq_devs, own, local_len) for part in parts], axi...  1.68 us
    pallas_call x1, Pallas kernels, mix(): pl.pallas_call(functools.partial(mix_kernel, own), out_shape=jax.ShapeDty...  1.42 us
    all_to_all x1, waiting for transfers between devices, exchange(): lax.all_to_all(chunks, 'seq', split_axis=0, concat_axis=0, tiled=True, ax...  0.98 us
    convert_element_type x1, other arithmetic, on_device(): return (out_gate.astype(F32) * vals).astype(BF16)  0.78 us
  transfers between devices with their start and end apart: 1, of which 1 were waited for; matrix products, arithmetic and copies ran while one was open for 0% of the time, Pallas kernels for 18%

profile of v9, /device:TPU:0, one launch (start us, length us, event | category | flops | bytes accessed | tf_op | source)
XLA Modules:
  0.0 30.1 jit_solution(17037219595700121280)
XLA Ops:
  0.0 1.7 %pad_maximum_fusion = bf16[16,2,8,512]{3,2,1,0:T(8,128)(2,1)} fusion(bf16[16,1,8,512]{3,2,1,0:T(8,128)(2,1)} %bitcast.12, bf16[16,1,8,512]{3,2,1,0:T(8,128)(2,1)} %bitcast.13), kind=kLoop, calls=%fused_computation.9 | loop fusion | flops 131072 | bytes 524288 | tf_op jit(solution)/shard_map/stack | solution.py:487
  1.7 9.3 %all-to-all-start = ((bf16[16,2,8,512]{3,2,1,0:T(8,128)(2,1)}), bf16[16,2,8,512]{3,2,1,0:T(8,128)(2,1)S(1)}, u32[]{:S(2)}, u32[]{:S(2)}) async-start(bf16[16,2,8,512]{3,2,1,0:T(8,128)(2,1)} %pad_maximum_fusion), calls=%async_computation | async-start | bytes 524288 | tf_op jit(solution)/shard_map/all_to_all | solution.py:172
  11.0 5.5 %shard_map.172 = (f32[512,256]{1,0:T(8,128)S(1)}, bf16[8,256,256]{2,1,0:T(8,128)(2,1)S(1)}, f32[8,128]{1,0:T(8,128)S(1)}, bf16[128,192]{1,0:T(8,128)(2,1)S(1)}, ...) custom-call(bf16[128,8192]{1,0:T(8,128)(2,1)} %constant.18.clone.emb, ...), custom_call_target="tpu_custom_call" | custom-call | tf_op jit(solution)/shard_map/pallas_call | solution.py:421
  16.6 0.0 copy-start
  16.6 1.0 %all-to-all-done.parts_ref = bf16[16,2,8,512]{3,2,1,0:T(8,128)(2,1)S(1)} async-done(((bf16[16,2,8,512]{3,2,1,0:T(8,128)(2,1)}), bf16[16,2,8,512]{3,2,1,0:T(8,128)(2,1)S(1)}, u32[]{:S(2)}, u32[]{:S(2)}) %all-to-all-start) | async-done | bytes 262176 | tf_op jit(solution)/shard_map/all_to_all | solution.py:172
  17.5 1.4 %shard_map.173 = bf16[128,640]{1,0:T(8,128)(2,1)S(1)} custom-call(bf16[16,2,8,512]{3,2,1,0:T(8,128)(2,1)S(1)} %all-to-all-done.parts_ref, f32[512,256]{1,0:T(8,128)S(1)} %get-tuple-element.13.spectrum_ref, bf16[8,256,256]{2,1,0:T(8,128)(2,1)S(1)} %get-tuple-element.14.toeplitz_ref, f32[8,128]{1,0:T(8,128)S(1)} %get-tuple-element.15.skip_ref, ...), custom_call_target="tpu_custom_call" | custom-call | tf_op jit(solution)/shard_map/pallas_call | solution.py:451
  19.0 10.3 %all_to_all.10 = bf16[16,8,640]{2,1,0:T(8,128)(2,1)S(1)} all-to-all(bf16[16,8,640]{2,1,0:T(8,128)(2,1)S(1)} %bitcast.9), channel_id=1, replica_groups={{22,26,14,20,8,16,24,6,18,2,10,28,12,30,0,4},{23,27,15,21,9,17,25,7,19,..., dimensions={0} | all-to-all | bytes 327680 | tf_op jit(solution)/shard_map/all_to_all | solution.py:172
  29.3 0.0 copy-done
  29.3 0.8 %fusion.5 = bf16[128,512]{1,0:T(8,128)(2,1)} fusion(bf16[128,512]{1,0:T(8,128)(2,1)S(1)} %copy-done, bf16[128,640]{1,0:T(8,128)(2,1)S(1)} %bitcast.11, bf16[128,128]{1,0:T(8,128)(2,1)S(1)} %slice.9), kind=kLoop, calls=%fused_computation.8 | loop fusion | flops 1245184 | bytes 425984 | tf_op jit(solution)/shard_map/convert_element_type | solution.py:508
  (1 shorter events, 0.0 us)
Async XLA Ops:
  1.7 15.9 %all-to-all-start = ((bf16[16,2,8,512]{3,2,1,0:T(8,128)(2,1)}), bf16[16,2,8,512]{3,2,1,0:T(8,128)(2,1)S(1)}, u32[]{:S(2)}, u32[]{:S(2)}) async-start(bf16[16,2,8,512]{3,2,1,0:T(8,128)(2,1)} %pad_maximum_fusion), calls=%async_computation | async-start | bytes 524288 | tf_op jit(solution)/shard_map/all_to_all | solution.py:172
  16.6 12.7 %copy-start = (bf16[128,512]{1,0:T(8,128)(2,1)S(1)}, bf16[128,512]{1,0:T(8,128)(2,1)}, u32[]{:S(2)}) copy-start(bf16[128,512]{1,0:T(8,128)(2,1)} %param.20) | copy-start | bytes 393220

commit v10 on v9

--- a/solution.py
+++ b/solution.py
@@ -14,7 +14,6 @@
 GROUPS = 4
 TILES = 2
 SPAN = 120.0
-ORDER_SEED = 115
 F32 = jnp.float32
 BF16 = jnp.bfloat16
 in_space = pltpu.with_memory_space_constraint
@@ -165,7 +164,8 @@
 
 
 def exchange_order(count):
-    return [int(place) for place in np.random.RandomState(ORDER_SEED).permutation(count)]
+    first = count // 2 + count // 8
+    return [(first + place) % count for place in range(count)]
 
 
 def exchange(chunks, order):

time: 30.3 us -> 30.2 us (level)
  starting transfers between devices: 9.33 us -> 8.79 us
  waiting for transfers between devices: 0.98 us -> 1.32 us
    all_to_all x1, starting transfers between devices: 9.33 us -> 8.79 us  [exchange(): lax.all_to_all(chunks, 'seq', split_axis=0, concat_axis=0, tiled=True, ax...]
    all_to_all x1, waiting for transfers between devices: 0.98 us -> 1.32 us  [exchange(): lax.all_to_all(chunks, 'seq', split_axis=0, concat_axis=0, tiled=True, ax...]
  transfers between devices with their start and end apart: 1 -> 1, of which waited for: 1 -> 1; matrix products, arithmetic and copies ran while one was open for 0% -> 0% of each run, Pallas kernels for 18% -> 19%
where the time goes in v10:
time: 30.2 us; the launch traced here: 29.9 us
  blocking collectives  10.3 us (34%)
  starting transfers between devices  8.79 us (29%)
  Pallas kernels  6.96 us (23%)
  other arithmetic  2.46 us (8%)
  waiting for transfers between devices  1.32 us (4%)
    all_to_all x1, blocking collectives, exchange(): lax.all_to_all(chunks, 'seq', split_axis=0, concat_axis=0, tiled=True, ax...  10.3 us
    all_to_all x1, starting transfers between devices, exchange(): lax.all_to_all(chunks, 'seq', split_axis=0, concat_axis=0, tiled=True, ax...  8.79 us
    pallas_call x1, Pallas kernels, make_filter(): pl.pallas_call(functools.partial(filter_kernel, own), out_shape=(pltpu.VM...  5.54 us
    another operation x1, other arithmetic, on_device(): jnp.stack([part.reshape(seq_devs, own, local_len) for part in parts], axi...  1.68 us
    pallas_call x1, Pallas kernels, mix(): pl.pallas_call(functools.partial(mix_kernel, own), out_shape=jax.ShapeDty...  1.42 us
    all_to_all x1, waiting for transfers between devices, exchange(): lax.all_to_all(chunks, 'seq', split_axis=0, concat_axis=0, tiled=True, ax...  1.32 us
    convert_element_type x1, other arithmetic, on_device(): return (out_gate.astype(F32) * vals).astype(BF16)  0.78 us
  transfers between devices with their start and end apart: 1, of which 1 were waited for; matrix products, arithmetic and copies ran while one was open for 0% of the time, Pallas kernels for 19%

profile of v10, /device:TPU:0, one launch (start us, length us, event | category | flops | bytes accessed | tf_op | source)
XLA Modules:
  0.0 29.9 jit_solution(5591031807201778133)
XLA Ops:
  0.0 1.7 %pad_maximum_fusion = bf16[16,2,8,512]{3,2,1,0:T(8,128)(2,1)} fusion(bf16[16,1,8,512]{3,2,1,0:T(8,128)(2,1)} %bitcast.12, bf16[16,1,8,512]{3,2,1,0:T(8,128)(2,1)} %bitcast.13), kind=kLoop, calls=%fused_computation.9 | loop fusion | flops 131072 | bytes 524288 | tf_op jit(solution)/shard_map/stack | solution.py:487
  1.7 8.8 %all-to-all-start = ((bf16[16,2,8,512]{3,2,1,0:T(8,128)(2,1)}), bf16[16,2,8,512]{3,2,1,0:T(8,128)(2,1)S(1)}, u32[]{:S(2)}, u32[]{:S(2)}) async-start(bf16[16,2,8,512]{3,2,1,0:T(8,128)(2,1)} %pad_maximum_fusion), calls=%async_computation | async-start | bytes 524288 | tf_op jit(solution)/shard_map/all_to_all | solution.py:172
  10.5 5.5 %shard_map.172 = (f32[512,256]{1,0:T(8,128)S(1)}, bf16[8,256,256]{2,1,0:T(8,128)(2,1)S(1)}, f32[8,128]{1,0:T(8,128)S(1)}, bf16[128,192]{1,0:T(8,128)(2,1)S(1)}, ...) custom-call(bf16[128,8192]{1,0:T(8,128)(2,1)} %constant.18.clone.emb, ...), custom_call_target="tpu_custom_call" | custom-call | tf_op jit(solution)/shard_map/pallas_call | solution.py:421
  16.0 0.0 copy-start
  16.0 1.3 %all-to-all-done.parts_ref = bf16[16,2,8,512]{3,2,1,0:T(8,128)(2,1)S(1)} async-done(((bf16[16,2,8,512]{3,2,1,0:T(8,128)(2,1)}), bf16[16,2,8,512]{3,2,1,0:T(8,128)(2,1)S(1)}, u32[]{:S(2)}, u32[]{:S(2)}) %all-to-all-start) | async-done | bytes 262176 | tf_op jit(solution)/shard_map/all_to_all | solution.py:172
  17.4 1.4 %shard_map.173 = bf16[128,640]{1,0:T(8,128)(2,1)S(1)} custom-call(bf16[16,2,8,512]{3,2,1,0:T(8,128)(2,1)S(1)} %all-to-all-done.parts_ref, f32[512,256]{1,0:T(8,128)S(1)} %get-tuple-element.13.spectrum_ref, bf16[8,256,256]{2,1,0:T(8,128)(2,1)S(1)} %get-tuple-element.14.toeplitz_ref, f32[8,128]{1,0:T(8,128)S(1)} %get-tuple-element.15.skip_ref, ...), custom_call_target="tpu_custom_call" | custom-call | tf_op jit(solution)/shard_map/pallas_call | solution.py:451
  18.8 10.3 %all_to_all.10 = bf16[16,8,640]{2,1,0:T(8,128)(2,1)S(1)} all-to-all(bf16[16,8,640]{2,1,0:T(8,128)(2,1)S(1)} %bitcast.9), channel_id=1, replica_groups={{20,22,24,26,28,30,0,2,4,6,8,10,12,14,16,18},{21,23,25,27,29,31,1,3,5,7..., dimensions={0} | all-to-all | bytes 327680 | tf_op jit(solution)/shard_map/all_to_all | solution.py:172
  29.1 0.0 copy-done
  29.1 0.8 %fusion.5 = bf16[128,512]{1,0:T(8,128)(2,1)} fusion(bf16[128,512]{1,0:T(8,128)(2,1)S(1)} %copy-done, bf16[128,640]{1,0:T(8,128)(2,1)S(1)} %bitcast.11, bf16[128,128]{1,0:T(8,128)(2,1)S(1)} %slice.9), kind=kLoop, calls=%fused_computation.8 | loop fusion | flops 1245184 | bytes 425984 | tf_op jit(solution)/shard_map/convert_element_type | solution.py:508
  (1 shorter events, 0.0 us)
Async XLA Ops:
  1.7 15.7 %all-to-all-start = ((bf16[16,2,8,512]{3,2,1,0:T(8,128)(2,1)}), bf16[16,2,8,512]{3,2,1,0:T(8,128)(2,1)S(1)}, u32[]{:S(2)}, u32[]{:S(2)}) async-start(bf16[16,2,8,512]{3,2,1,0:T(8,128)(2,1)} %pad_maximum_fusion), calls=%async_computation | async-start | bytes 524288 | tf_op jit(solution)/shard_map/all_to_all | solution.py:172
  16.0 13.1 %copy-start = (bf16[128,512]{1,0:T(8,128)(2,1)S(1)}, bf16[128,512]{1,0:T(8,128)(2,1)}, u32[]{:S(2)}) copy-start(bf16[128,512]{1,0:T(8,128)(2,1)} %param.20) | copy-start | bytes 393220

commit v11 on v10

--- a/solution.py
+++ b/solution.py
@@ -13,7 +13,6 @@
 LANES = 128
 GROUPS = 4
 TILES = 2
-SPAN = 120.0
 F32 = jnp.float32
 BF16 = jnp.bfloat16
 in_space = pltpu.with_memory_space_constraint
@@ -144,23 +143,6 @@
             )
         )
     return matmul(outer_back_ref[...], stack_three(jnp.concatenate(columns, axis=1)))
-
-
-def code_group(columns):
-    top = functools.reduce(jnp.maximum, [jnp.abs(column) for column in columns])
-    scale = lax.reduce_precision(jnp.maximum(top, 1e-30) * (1.0 + 1.0 / 128), 8, 7)
-    factor = 2.0 * SPAN / scale
-    codes = []
-    for column in columns:
-        size = jnp.exp2(jnp.abs(column) * factor - SPAN)
-        codes.append(jnp.where(column < 0, -size, size).astype(BF16))
-    return codes, scale.astype(BF16)
-
-
-def decode_group(codes, scale):
-    codes = codes.astype(F32)
-    share = jnp.log(jnp.abs(codes)) * (0.5 / SPAN / math.log(2.0)) + 0.5
-    return jnp.where(codes < 0, -share, share) * scale.astype(F32)
 
 
 def exchange_order(count):
@@ -388,7 +370,6 @@
         mixed_ref[pl.ds(c, blocks, stride=own), :] = (
             conv[:, c * LANES : (c + 1) * LANES] + skip_ref[c : c + 1, :] * gated[c]
         )
-    columns = []
     for q in range(local_blocks):
         if own % 8 == 0:
             column = jnp.concatenate(
@@ -403,11 +384,7 @@
                 at = p * part_rows + q * own
                 signal_ref[place * own : (place + 1) * own, :] = mixed_ref[at : at + own, :]
             column = signal_ref[: seq_devs * own, :]
-        columns.append(column)
-    codes, scale = code_group(columns)
-    for q in range(local_blocks):
-        out_ref[:, q * LANES : (q + 1) * LANES] = codes[q]
-    out_ref[:, local_len:] = scale
+        out_ref[:, q * LANES : (q + 1) * LANES] = column
 
 
 def make_filter(params, own, full_len):
@@ -450,7 +427,7 @@
     vmem = pl.BlockSpec(memory_space=pltpu.VMEM)
     return pl.pallas_call(
         functools.partial(mix_kernel, own),
-        out_shape=jax.ShapeDtypeStruct((seq_devs * own, local_len + LANES), BF16),
+        out_shape=jax.ShapeDtypeStruct((seq_devs * own, local_len), F32),
         in_specs=[vmem] * (1 + len(shared)),
         out_specs=vmem,
         scratch_shapes=[pltpu.VMEM((rows + 2 * own, LANES), F32)]
@@ -500,11 +477,8 @@
     )
     shared = make_filter(params, own, seq_devs * local_len)
     mixed = mix(parts, shared)
-    coded = exchange(mixed.reshape(seq_devs, own, -1), order).reshape(
-        seq_devs * own, -1
-    )[:channels]
-    scale = jnp.concatenate([coded[:, local_len:]] * (local_len // LANES), axis=1)
-    vals = decode_group(coded[:, :local_len], scale)
+    vals = exchange(mixed.reshape(seq_devs, own, local_len), order)
+    vals = vals.reshape(seq_devs * own, local_len)[:channels]
     return (out_gate.astype(F32) * vals).astype(BF16)
 
 

time: 30.2 us -> 30.4 us (level)
  blocking collectives: 10.3 us -> 10.8 us
    all_to_all x1, blocking collectives: 10.3 us -> 10.8 us  [exchange(): lax.all_to_all(chunks, 'seq', split_axis=0, concat_axis=0, tiled=True, ax...]
  transfers between devices with their start and end apart: 1 -> 1, of which waited for: 1 -> 1; matrix products, arithmetic and copies ran while one was open for 0% -> 0% of each run, Pallas kernels for 19% -> 18%
where the time goes in v11:
time: 30.4 us; the launch traced here: 30.1 us
  blocking collectives  10.8 us (36%)
  starting transfers between devices  8.79 us (29%)
  Pallas kernels  6.86 us (23%)
  other arithmetic  2.36 us (8%)
  waiting for transfers between devices  1.32 us (4%)
    all_to_all x1, blocking collectives, exchange(): lax.all_to_all(chunks, 'seq', split_axis=0, concat_axis=0, tiled=True, ax...  10.8 us
    all_to_all x1, starting transfers between devices, exchange(): lax.all_to_all(chunks, 'seq', split_axis=0, concat_axis=0, tiled=True, ax...  8.79 us
    pallas_call x1, Pallas kernels, make_filter(): pl.pallas_call(functools.partial(filter_kernel, own), out_shape=(pltpu.VM...  5.54 us
    another operation x1, other arithmetic, on_device(): jnp.stack([part.reshape(seq_devs, own, local_len) for part in parts], axi...  1.68 us
    pallas_call x1, Pallas kernels, mix(): pl.pallas_call(functools.partial(mix_kernel, own), out_shape=jax.ShapeDty...  1.32 us
    all_to_all x1, waiting for transfers between devices, exchange(): lax.all_to_all(chunks, 'seq', split_axis=0, concat_axis=0, tiled=True, ax...  1.32 us
    convert_element_type x1, other arithmetic, on_device(): return (out_gate.astype(F32) * vals).astype(BF16)  0.68 us
  transfers between devices with their start and end apart: 1, of which 1 were waited for; matrix products, arithmetic and copies ran while one was open for 0% of the time, Pallas kernels for 18%

profile of v11, /device:TPU:0, one launch (start us, length us, event | category | flops | bytes accessed | tf_op | source)
XLA Modules:
  0.0 30.1 jit_solution(10116150933178218752)
XLA Ops:
  0.0 1.7 %pad_maximum_fusion = bf16[16,2,8,512]{3,2,1,0:T(8,128)(2,1)} fusion(bf16[16,1,8,512]{3,2,1,0:T(8,128)(2,1)} %bitcast.13, bf16[16,1,8,512]{3,2,1,0:T(8,128)(2,1)} %bitcast.14), kind=kLoop, calls=%fused_computation | loop fusion | flops 131072 | bytes 524288 | tf_op jit(solution)/shard_map/stack | solution.py:464
  1.7 8.8 %all-to-all-start = ((bf16[16,2,8,512]{3,2,1,0:T(8,128)(2,1)}), bf16[16,2,8,512]{3,2,1,0:T(8,128)(2,1)S(1)}, u32[]{:S(2)}, u32[]{:S(2)}) async-start(bf16[16,2,8,512]{3,2,1,0:T(8,128)(2,1)} %pad_maximum_fusion), calls=%async_computation | async-start | bytes 524288 | tf_op jit(solution)/shard_map/all_to_all | solution.py:154
  10.5 5.5 %shard_map.172 = (f32[512,256]{1,0:T(8,128)S(1)}, bf16[8,256,256]{2,1,0:T(8,128)(2,1)S(1)}, f32[8,128]{1,0:T(8,128)S(1)}, bf16[128,192]{1,0:T(8,128)(2,1)S(1)}, ...) custom-call(bf16[128,8192]{1,0:T(8,128)(2,1)} %constant.12.clone.emb, ...), custom_call_target="tpu_custom_call" | custom-call | tf_op jit(solution)/shard_map/pallas_call | solution.py:398
  16.0 0.0 copy-start
  16.0 1.3 %all-to-all-done.parts_ref = bf16[16,2,8,512]{3,2,1,0:T(8,128)(2,1)S(1)} async-done(((bf16[16,2,8,512]{3,2,1,0:T(8,128)(2,1)}), bf16[16,2,8,512]{3,2,1,0:T(8,128)(2,1)S(1)}, u32[]{:S(2)}, u32[]{:S(2)}) %all-to-all-start) | async-done | bytes 262176 | tf_op jit(solution)/shard_map/all_to_all | solution.py:154
  17.4 1.3 %shard_map.173 = f32[128,512]{1,0:T(8,128)S(1)} custom-call(bf16[16,2,8,512]{3,2,1,0:T(8,128)(2,1)S(1)} %all-to-all-done.parts_ref, f32[512,256]{1,0:T(8,128)S(1)} %get-tuple-element.13.spectrum_ref, bf16[8,256,256]{2,1,0:T(8,128)(2,1)S(1)} %get-tuple-element.14.toeplitz_ref, f32[8,128]{1,0:T(8,128)S(1)} %get-tuple-element.15.skip_ref, ...), custom_call_target="tpu_custom_call" | custom-call | tf_op jit(solution)/shard_map/pallas_call | solution.py:428
  18.7 10.8 %all_to_all.10 = f32[16,8,512]{2,1,0:T(8,128)S(1)} all-to-all(f32[16,8,512]{2,1,0:T(8,128)S(1)} %bitcast.12), channel_id=1, replica_groups={{20,22,24,26,28,30,0,2,4,6,8,10,12,14,16,18},{21,23,25,27,29,31,1,3,5,7..., dimensions={0} | all-to-all | bytes 524288 | tf_op jit(solution)/shard_map/all_to_all | solution.py:154
  29.4 0.0 copy-done
  29.5 0.7 %fusion = bf16[128,512]{1,0:T(8,128)(2,1)} fusion(f32[16,8,512]{2,1,0:T(8,128)S(1)} %all_to_all.10, bf16[128,512]{1,0:T(8,128)(2,1)S(1)} %copy-done), kind=kLoop, calls=%fused_computation.2 | loop fusion | flops 196608 | bytes 524288 | tf_op jit(solution)/shard_map/convert_element_type | solution.py:482
Async XLA Ops:
  1.7 15.7 %all-to-all-start = ((bf16[16,2,8,512]{3,2,1,0:T(8,128)(2,1)}), bf16[16,2,8,512]{3,2,1,0:T(8,128)(2,1)S(1)}, u32[]{:S(2)}, u32[]{:S(2)}) async-start(bf16[16,2,8,512]{3,2,1,0:T(8,128)(2,1)} %pad_maximum_fusion), calls=%async_computation | async-start | bytes 524288 | tf_op jit(solution)/shard_map/all_to_all | solution.py:154
  16.0 13.4 %copy-start = (bf16[128,512]{1,0:T(8,128)(2,1)S(1)}, bf16[128,512]{1,0:T(8,128)(2,1)}, u32[]{:S(2)}) copy-start(bf16[128,512]{1,0:T(8,128)(2,1)} %param.20) | copy-start | bytes 393220

commit v12 on v10

--- a/solution.py
+++ b/solution.py
@@ -246,7 +246,7 @@
                 embed_hbm.at[:, lanes], embed_ref.at[:, lanes], embed_sems.at[i]
             )
         )
-    for copy in copies[:8] + embed_copies + copies[8:]:
+    for copy in copies[:9] + embed_copies + copies[9:]:
         copy.start()
     seq_index = lax.axis_index("seq")
     first_channel = 0
@@ -256,7 +256,7 @@
     pad_ref[...] = jnp.zeros_like(pad_ref)
     vec_ref[...] = jnp.zeros_like(vec_ref)
     row_ref[...] = jnp.zeros_like(row_ref)
-    for copy in copies[:8]:
+    for copy in copies[:9]:
         copy.wait()
 
     freq = sine_freq_ref[...] * (0.5 / math.pi)
@@ -292,6 +292,21 @@
     skip_ref[...] = jnp.broadcast_to(column_ref[own_rows, 1:2], skip_ref.shape)
     scale = jnp.sqrt(2.0 * decay)
 
+    taps = taps_ref[own_rows, :]
+    tap_count = taps.shape[1]
+    square = (tap_count, tap_count)
+    upper = lax.broadcasted_iota(jnp.int32, square, 1) >= lax.broadcasted_iota(
+        jnp.int32, square, 0
+    )
+    for c in range(own):
+        lags = pltpu.roll(
+            jnp.broadcast_to(taps[c : c + 1], square), 0, 1, stride=1, stride_axis=0
+        )
+        high, low = split_two(
+            jnp.concatenate([jnp.where(upper, 0.0, lags), jnp.where(upper, lags, 0.0)], axis=0)
+        )
+        toeplitz_ref[c] = jnp.concatenate([high, low], axis=1)
+
     for i in range(TILES):
         start = i * tile_len
         embed_copies[i].wait()
@@ -307,27 +322,13 @@
             row = (start // LANES + j) * own
             filter_ref[row : row + own, :] = vals[:, j * LANES : (j + 1) * LANES]
 
-    for copy in copies[8:]:
+    for copy in copies[9:]:
         copy.wait()
     blocks = full_len // LANES
     columns = [filter_ref[pl.ds(c, blocks, stride=own), :] for c in range(own)]
     spectrum_ref[...] = inner_product(
         jnp.concatenate(outer_forward(columns, outer_ref, twiddle_ref), axis=0), inner_ref
     )
-    taps = taps_ref[own_rows, :]
-    tap_count = taps.shape[1]
-    square = (tap_count, tap_count)
-    upper = lax.broadcasted_iota(jnp.int32, square, 1) >= lax.broadcasted_iota(
-        jnp.int32, square, 0
-    )
-    for c in range(own):
-        lags = pltpu.roll(
-            jnp.broadcast_to(taps[c : c + 1], square), 0, 1, stride=1, stride_axis=0
-        )
-        high, low = split_two(
-            jnp.concatenate([jnp.where(upper, 0.0, lags), jnp.where(upper, lags, 0.0)], axis=0)
-        )
-        toeplitz_ref[c] = jnp.concatenate([high, low], axis=1)
 
 
 def mix_kernel(

time: 30.2 us -> 30.2 us (level)
  no operation moved by 1% of the time
where the time goes in v12:
time: 30.2 us; the launch traced here: 29.9 us
  blocking collectives  10.3 us (34%)
  starting transfers between devices  8.79 us (29%)
  Pallas kernels  6.97 us (23%)
  other arithmetic  2.46 us (8%)
  waiting for transfers between devices  1.32 us (4%)
    all_to_all x1, blocking collectives, exchange(): lax.all_to_all(chunks, 'seq', split_axis=0, concat_axis=0, tiled=True, ax...  10.3 us
    all_to_all x1, starting transfers between devices, exchange(): lax.all_to_all(chunks, 'seq', split_axis=0, concat_axis=0, tiled=True, ax...  8.79 us
    pallas_call x1, Pallas kernels, make_filter(): pl.pallas_call(functools.partial(filter_kernel, own), out_shape=(pltpu.VM...  5.54 us
    another operation x1, other arithmetic, on_device(): jnp.stack([part.reshape(seq_devs, own, local_len) for part in parts], axi...  1.68 us
    pallas_call x1, Pallas kernels, mix(): pl.pallas_call(functools.partial(mix_kernel, own), out_shape=jax.ShapeDty...  1.42 us
    all_to_all x1, waiting for transfers between devices, exchange(): lax.all_to_all(chunks, 'seq', split_axis=0, concat_axis=0, tiled=True, ax...  1.32 us
    convert_element_type x1, other arithmetic, on_device(): return (out_gate.astype(F32) * vals).astype(BF16)  0.78 us
  transfers between devices with their start and end apart: 1, of which 1 were waited for; matrix products, arithmetic and copies ran while one was open for 0% of the time, Pallas kernels for 19%

profile of v12, /device:TPU:0, one launch (start us, length us, event | category | flops | bytes accessed | tf_op | source)
XLA Modules:
  0.0 29.9 jit_solution(4289640606517968796)
XLA Ops:
  0.0 1.7 %pad_maximum_fusion = bf16[16,2,8,512]{3,2,1,0:T(8,128)(2,1)} fusion(bf16[16,1,8,512]{3,2,1,0:T(8,128)(2,1)} %bitcast.12, bf16[16,1,8,512]{3,2,1,0:T(8,128)(2,1)} %bitcast.13), kind=kLoop, calls=%fused_computation.9 | loop fusion | flops 131072 | bytes 524288 | tf_op jit(solution)/shard_map/stack | solution.py:488
  1.7 8.8 %all-to-all-start = ((bf16[16,2,8,512]{3,2,1,0:T(8,128)(2,1)}), bf16[16,2,8,512]{3,2,1,0:T(8,128)(2,1)S(1)}, u32[]{:S(2)}, u32[]{:S(2)}) async-start(bf16[16,2,8,512]{3,2,1,0:T(8,128)(2,1)} %pad_maximum_fusion), calls=%async_computation | async-start | bytes 524288 | tf_op jit(solution)/shard_map/all_to_all | solution.py:172
  10.5 5.5 %shard_map.172 = (f32[512,256]{1,0:T(8,128)S(1)}, bf16[8,256,256]{2,1,0:T(8,128)(2,1)S(1)}, f32[8,128]{1,0:T(8,128)S(1)}, bf16[128,192]{1,0:T(8,128)(2,1)S(1)}, ...) custom-call(bf16[128,8192]{1,0:T(8,128)(2,1)} %constant.18.clone.emb, ...), custom_call_target="tpu_custom_call" | custom-call | tf_op jit(solution)/shard_map/pallas_call | solution.py:422
  16.0 0.0 copy-start
  16.0 1.3 %all-to-all-done.parts_ref = bf16[16,2,8,512]{3,2,1,0:T(8,128)(2,1)S(1)} async-done(((bf16[16,2,8,512]{3,2,1,0:T(8,128)(2,1)}), bf16[16,2,8,512]{3,2,1,0:T(8,128)(2,1)S(1)}, u32[]{:S(2)}, u32[]{:S(2)}) %all-to-all-start) | async-done | bytes 262176 | tf_op jit(solution)/shard_map/all_to_all | solution.py:172
  17.4 1.4 %shard_map.173 = bf16[128,640]{1,0:T(8,128)(2,1)S(1)} custom-call(bf16[16,2,8,512]{3,2,1,0:T(8,128)(2,1)S(1)} %all-to-all-done.parts_ref, f32[512,256]{1,0:T(8,128)S(1)} %get-tuple-element.13.spectrum_ref, bf16[8,256,256]{2,1,0:T(8,128)(2,1)S(1)} %get-tuple-element.14.toeplitz_ref, f32[8,128]{1,0:T(8,128)S(1)} %get-tuple-element.15.skip_ref, ...), custom_call_target="tpu_custom_call" | custom-call | tf_op jit(solution)/shard_map/pallas_call | solution.py:452
  18.8 10.3 %all_to_all.10 = bf16[16,8,640]{2,1,0:T(8,128)(2,1)S(1)} all-to-all(bf16[16,8,640]{2,1,0:T(8,128)(2,1)S(1)} %bitcast.9), channel_id=1, replica_groups={{20,22,24,26,28,30,0,2,4,6,8,10,12,14,16,18},{21,23,25,27,29,31,1,3,5,7..., dimensions={0} | all-to-all | bytes 327680 | tf_op jit(solution)/shard_map/all_to_all | solution.py:172
  29.1 0.0 copy-done
  29.1 0.8 %fusion.5 = bf16[128,512]{1,0:T(8,128)(2,1)} fusion(bf16[128,512]{1,0:T(8,128)(2,1)S(1)} %copy-done, bf16[128,640]{1,0:T(8,128)(2,1)S(1)} %bitcast.11, bf16[128,128]{1,0:T(8,128)(2,1)S(1)} %slice.9), kind=kLoop, calls=%fused_computation.8 | loop fusion | flops 1245184 | bytes 425984 | tf_op jit(solution)/shard_map/convert_element_type | solution.py:509
  (1 shorter events, 0.0 us)
Async XLA Ops:
  1.7 15.7 %all-to-all-start = ((bf16[16,2,8,512]{3,2,1,0:T(8,128)(2,1)}), bf16[16,2,8,512]{3,2,1,0:T(8,128)(2,1)S(1)}, u32[]{:S(2)}, u32[]{:S(2)}) async-start(bf16[16,2,8,512]{3,2,1,0:T(8,128)(2,1)} %pad_maximum_fusion), calls=%async_computation | async-start | bytes 524288 | tf_op jit(solution)/shard_map/all_to_all | solution.py:172
  16.0 13.1 %copy-start = (bf16[128,512]{1,0:T(8,128)(2,1)S(1)}, bf16[128,512]{1,0:T(8,128)(2,1)}, u32[]{:S(2)}) copy-start(bf16[128,512]{1,0:T(8,128)(2,1)} %param.20) | copy-start | bytes 393220

commit v13 on v10

--- a/solution.py
+++ b/solution.py
@@ -165,7 +165,8 @@
 
 def exchange_order(count):
     first = count // 2 + count // 8
-    return [(first + place) % count for place in range(count)]
+    mixed = np.random.RandomState(147).permutation(count)
+    return [first] + [int(place) for place in mixed if place != first]
 
 
 def exchange(chunks, order):

time: 30.2 us -> 30.1 us (level)
  waiting for transfers between devices: 1.32 us -> 0.65 us
  blocking collectives: 10.3 us -> 10.9 us
    all_to_all x1, waiting for transfers between devices: 1.32 us -> 0.65 us  [exchange(): lax.all_to_all(chunks, 'seq', split_axis=0, concat_axis=0, tiled=True, ax...]
    all_to_all x1, blocking collectives: 10.3 us -> 10.9 us  [exchange(): lax.all_to_all(chunks, 'seq', split_axis=0, concat_axis=0, tiled=True, ax...]
where the time goes in v13:
time: 30.1 us; the launch traced here: 29.8 us
  blocking collectives  10.9 us (36%)
  starting transfers between devices  8.78 us (29%)
  Pallas kernels  6.98 us (23%)
  other arithmetic  2.46 us (8%)
  waiting for transfers between devices  0.65 us (2%)
    all_to_all x1, blocking collectives, exchange(): lax.all_to_all(chunks, 'seq', split_axis=0, concat_axis=0, tiled=True, ax...  10.9 us
    all_to_all x1, starting transfers between devices, exchange(): lax.all_to_all(chunks, 'seq', split_axis=0, concat_axis=0, tiled=True, ax...  8.78 us
    pallas_call x1, Pallas kernels, make_filter(): pl.pallas_call(functools.partial(filter_kernel, own), out_shape=(pltpu.VM...  5.56 us
    another operation x1, other arithmetic, on_device(): jnp.stack([part.reshape(seq_devs, own, local_len) for part in parts], axi...  1.68 us
    pallas_call x1, Pallas kernels, mix(): pl.pallas_call(functools.partial(mix_kernel, own), out_shape=jax.ShapeDty...  1.42 us
    convert_element_type x1, other arithmetic, on_device(): return (out_gate.astype(F32) * vals).astype(BF16)  0.78 us
    all_to_all x1, waiting for transfers between devices, exchange(): lax.all_to_all(chunks, 'seq', split_axis=0, concat_axis=0, tiled=True, ax...  0.65 us
  transfers between devices with their start and end apart: 1, of which 1 were waited for; matrix products, arithmetic and copies ran while one was open for 0% of the time, Pallas kernels for 19%

profile of v13, /device:TPU:0, one launch (start us, length us, event | category | flops | bytes accessed | tf_op | source)
XLA Modules:
  0.0 29.8 jit_solution(3950481829627312168)
XLA Ops:
  0.0 1.7 %pad_maximum_fusion = bf16[16,2,8,512]{3,2,1,0:T(8,128)(2,1)} fusion(bf16[16,1,8,512]{3,2,1,0:T(8,128)(2,1)} %bitcast.12, bf16[16,1,8,512]{3,2,1,0:T(8,128)(2,1)} %bitcast.13), kind=kLoop, calls=%fused_computation.9 | loop fusion | flops 131072 | bytes 524288 | tf_op jit(solution)/shard_map/stack | solution.py:488
  1.7 8.8 %all-to-all-start = ((bf16[16,2,8,512]{3,2,1,0:T(8,128)(2,1)}), bf16[16,2,8,512]{3,2,1,0:T(8,128)(2,1)S(1)}, u32[]{:S(2)}, u32[]{:S(2)}) async-start(bf16[16,2,8,512]{3,2,1,0:T(8,128)(2,1)} %pad_maximum_fusion), calls=%async_computation | async-start | bytes 524288 | tf_op jit(solution)/shard_map/all_to_all | solution.py:173
  10.5 5.6 %shard_map.172 = (f32[512,256]{1,0:T(8,128)S(1)}, bf16[8,256,256]{2,1,0:T(8,128)(2,1)S(1)}, f32[8,128]{1,0:T(8,128)S(1)}, bf16[128,192]{1,0:T(8,128)(2,1)S(1)}, ...) custom-call(bf16[128,8192]{1,0:T(8,128)(2,1)} %constant.18.clone.emb, ...), custom_call_target="tpu_custom_call" | custom-call | tf_op jit(solution)/shard_map/pallas_call | solution.py:422
  16.0 0.0 copy-start
  16.0 0.7 %all-to-all-done.parts_ref = bf16[16,2,8,512]{3,2,1,0:T(8,128)(2,1)S(1)} async-done(((bf16[16,2,8,512]{3,2,1,0:T(8,128)(2,1)}), bf16[16,2,8,512]{3,2,1,0:T(8,128)(2,1)S(1)}, u32[]{:S(2)}, u32[]{:S(2)}) %all-to-all-start) | async-done | bytes 262176 | tf_op jit(solution)/shard_map/all_to_all | solution.py:173
  16.7 1.4 %shard_map.173 = bf16[128,640]{1,0:T(8,128)(2,1)S(1)} custom-call(bf16[16,2,8,512]{3,2,1,0:T(8,128)(2,1)S(1)} %all-to-all-done.parts_ref, f32[512,256]{1,0:T(8,128)S(1)} %get-tuple-element.13.spectrum_ref, bf16[8,256,256]{2,1,0:T(8,128)(2,1)S(1)} %get-tuple-element.14.toeplitz_ref, f32[8,128]{1,0:T(8,128)S(1)} %get-tuple-element.15.skip_ref, ...), custom_call_target="tpu_custom_call" | custom-call | tf_op jit(solution)/shard_map/pallas_call | solution.py:452
  18.1 10.9 %all_to_all.10 = bf16[16,8,640]{2,1,0:T(8,128)(2,1)S(1)} all-to-all(bf16[16,8,640]{2,1,0:T(8,128)(2,1)S(1)} %bitcast.9), channel_id=1, replica_groups={{20,6,0,10,26,8,30,28,4,2,22,24,18,14,16,12},{21,7,1,11,27,9,31,29,5,3,..., dimensions={0} | all-to-all | bytes 327680 | tf_op jit(solution)/shard_map/all_to_all | solution.py:173
  29.0 0.0 copy-done
  29.0 0.8 %fusion.5 = bf16[128,512]{1,0:T(8,128)(2,1)} fusion(bf16[128,512]{1,0:T(8,128)(2,1)S(1)} %copy-done, bf16[128,640]{1,0:T(8,128)(2,1)S(1)} %bitcast.11, bf16[128,128]{1,0:T(8,128)(2,1)S(1)} %slice.9), kind=kLoop, calls=%fused_computation.8 | loop fusion | flops 1245184 | bytes 425984 | tf_op jit(solution)/shard_map/convert_element_type | solution.py:509
  (1 shorter events, 0.0 us)
Async XLA Ops:
  1.7 15.0 %all-to-all-start = ((bf16[16,2,8,512]{3,2,1,0:T(8,128)(2,1)}), bf16[16,2,8,512]{3,2,1,0:T(8,128)(2,1)S(1)}, u32[]{:S(2)}, u32[]{:S(2)}) async-start(bf16[16,2,8,512]{3,2,1,0:T(8,128)(2,1)} %pad_maximum_fusion), calls=%async_computation | async-start | bytes 524288 | tf_op jit(solution)/shard_map/all_to_all | solution.py:173
  16.0 13.0 %copy-start = (bf16[128,512]{1,0:T(8,128)(2,1)S(1)}, bf16[128,512]{1,0:T(8,128)(2,1)}, u32[]{:S(2)}) copy-start(bf16[128,512]{1,0:T(8,128)(2,1)} %param.20) | copy-start | bytes 393220
